TPU v7x, 256 devices: a whole 4x4x8 slice. The times are simulated.
256 devices in a mesh: shard: 32 (over z_hi, x, y), rep: 8 (over z_lo, core).
Axes of the slice: x: 4, y: 4, z: 8 (z_hi: 2, z_lo: 4; z = z_hi * 4 + z_lo), core: 2. Of those that a mesh axis runs over, the one named last changes fastest.
Arguments:
- tokens: bfloat16 [8, 4096, 2048], P('rep', 'shard'), may hold values from -8 to 8, as said below
- qkv_weight: bfloat16 [2048, 1536], P('shard'), may hold values from -0.125 to 0.125
- out_weight: bfloat16 [1024, 2048], P('shard'), may hold values from -0.1875 to 0.1875
- cotangent: bfloat16 [8, 4096, 2048], P('rep', 'shard'), may hold values from -6 to 6
Outputs:
- block_output: bfloat16 [8, 4096, 2048], P('rep', 'shard')
- tokens_grad: bfloat16 [8, 4096, 2048], P('rep', 'shard')
- qkv_grad: float32 [2048, 1536], P('shard')
- out_grad: float32 [1024, 2048], P('shard')
Inputs may be any that keep to these rules, and one draw needn't show every extreme that they name: `tokens`: each token's activations carry a scale of their own.
All inputs are finite; a program needn't handle non-finite values.
Results may differ from a plain program's by a relative error of at most 0.034.
Values may be sent and summed in bfloat16 or wider, within the bound.
A program may use at most 128 MiB of HBM per device.

v0:
```python
import math

import jax
import jax.numpy as jnp
from jax import lax
from jax.sharding import PartitionSpec as P

HEADS = 16
KV_HEADS = 4
HEAD_DIM = 64


ROPE_BASE = 500000.0
NEG_FILL = -1e30


def tables(positions, head_size):
    halves = head_size // 2
    frequency = ROPE_BASE ** (-(jnp.arange(halves, dtype=jnp.float32) * 2.0) / head_size)
    angles = positions.astype(jnp.float32)[:, None] * frequency[None, :]
    return (jnp.cos(angles), jnp.sin(angles))


def rotate(matrix, cos_rows, sin_rows, head_count):
    row_count = matrix.shape[0]
    head_size = matrix.shape[1] // head_count
    halves = head_size // 2
    pieces = matrix.reshape(row_count, head_count, 2, halves)
    lower_half = pieces[:, :, 0]
    upper_half = pieces[:, :, 1]
    cos_part = cos_rows[:, None, :]
    sin_part = sin_rows[:, None, :]
    turned = jnp.stack(
        [
            lower_half * cos_part - upper_half * sin_part,
            upper_half * cos_part + lower_half * sin_part,
        ],
        axis=2,
    )
    return turned.reshape(row_count, head_count * head_size)


def body(tokens, qkv_weight, out_weight, cotangent):
    inner_width = HEADS * HEAD_DIM
    kv_width = KV_HEADS * HEAD_DIM
    groups = HEADS // KV_HEADS
    logit_scale = HEAD_DIM ** (-0.5)
    inputs = tokens[0]
    grad_output = cotangent[0]
    tok_count = inputs.shape[0]
    shard_index = lax.axis_index("shard")
    qkv_full, out_full = (
        lax.all_gather(qkv_weight, "shard", axis=0, tiled=True),
        lax.all_gather(out_weight, "shard", axis=0, tiled=True),
    )
    positions = shard_index * tok_count + jnp.arange(tok_count, dtype=jnp.int32)
    cosine, sine = tables(positions, HEAD_DIM)
    projected = jnp.dot(inputs, qkv_full, preferred_element_type=jnp.float32)
    queries = rotate(projected[:, :inner_width], cosine, sine, HEADS).astype(jnp.bfloat16)
    key_rows = rotate(
        projected[:, inner_width : inner_width + kv_width], cosine, sine, KV_HEADS
    ).astype(jnp.bfloat16)
    value_rows = projected[:, inner_width + kv_width :].astype(jnp.bfloat16)
    stacked = jnp.concatenate([key_rows, value_rows], axis=1)
    gathered = lax.all_gather(stacked, "shard", axis=0, tiled=True)
    seq_len = gathered.shape[0]
    block_len = min(512, seq_len)
    visible_blocks = (shard_index * tok_count + tok_count - 1) // block_len + 1
    grouped_heads = queries.reshape(tok_count, KV_HEADS, groups, HEAD_DIM)

    def key_block(current_block_index):
        block_rows = lax.dynamic_slice_in_dim(
            gathered, current_block_index * block_len, block_len, 0
        )
        key_portion = block_rows[:, :kv_width].reshape(block_len, KV_HEADS, HEAD_DIM)
        value_portion = block_rows[:, kv_width:].reshape(block_len, KV_HEADS, HEAD_DIM)
        return (key_portion, value_portion)

    def block_scores(current_block_index, key_portion):
        attention_logits = (
            jnp.einsum(
                "nifc,zic->ifnz", grouped_heads, key_portion, preferred_element_type=jnp.float32
            )
            * logit_scale
        )
        key_pos = current_block_index * block_len + jnp.arange(block_len, dtype=jnp.int32)
        visible = key_pos[None, :] <= positions[:, None]
        return (attention_logits, visible)

    def first_pass(current_block_index, carried):
        running, summed = carried
        key_portion, value_portion = key_block(current_block_index)
        attention_logits, visible = block_scores(current_block_index, key_portion)
        row_peak = jnp.maximum(
            running, jnp.max(jnp.where(visible, attention_logits, NEG_FILL), axis=-1, keepdims=True)
        )
        fresh = jnp.sum(
            jnp.where(visible, jnp.exp(attention_logits - row_peak), 0.0), axis=-1, keepdims=True
        )
        return (row_peak, summed * jnp.exp(running - row_peak) + fresh)

    start_peak = jnp.full((KV_HEADS, groups, tok_count, 1), NEG_FILL, jnp.float32)
    start_sum = jnp.zeros((KV_HEADS, groups, tok_count, 1), jnp.float32)
    row_peak, summed = lax.fori_loop(0, visible_blocks, first_pass, (start_peak, start_sum))
    log_total = row_peak + jnp.log(summed)

    def second_pass(current_block_index, carried):
        key_portion, value_portion = key_block(current_block_index)
        attention_logits, visible = block_scores(current_block_index, key_portion)
        attention_probabilities = jnp.where(
            visible, jnp.exp(attention_logits - log_total), 0.0
        ).astype(jnp.bfloat16)
        update = jnp.einsum(
            "ezhm,meo->hezo",
            attention_probabilities,
            value_portion,
            preferred_element_type=jnp.float32,
        )
        return carried + update

    empty_out = jnp.zeros((tok_count, KV_HEADS, groups, HEAD_DIM), jnp.float32)
    attended_sum = lax.fori_loop(0, visible_blocks, second_pass, empty_out)
    attended_values = attended_sum.reshape(tok_count, inner_width).astype(jnp.bfloat16)
    block_output = jnp.dot(attended_values, out_full, preferred_element_type=jnp.float32).astype(
        jnp.bfloat16
    )
    grad_attended = lax.dot_general(
        grad_output, out_full, (((1,), (1,)), ((), ())), preferred_element_type=jnp.float32
    ).astype(jnp.bfloat16)
    out_share = lax.psum_scatter(
        lax.dot_general(
            attended_values,
            grad_output,
            (((0,), (0,)), ((), ())),
            preferred_element_type=jnp.float32,
        ).astype(jnp.bfloat16),
        "shard",
        scatter_dimension=0,
        tiled=True,
    ).astype(jnp.float32)
    gradient_grouped_heads = grad_attended.reshape(tok_count, KV_HEADS, groups, HEAD_DIM)
    attn_grouped = attended_values.reshape(tok_count, KV_HEADS, groups, HEAD_DIM)
    row_dots = jnp.einsum(
        "tkgd,tkgd->kgt", gradient_grouped_heads, attn_grouped, preferred_element_type=jnp.float32
    )[..., None]

    def backward_pass(current_block_index, carried):
        query_sum, term_rows = carried
        key_portion, value_portion = key_block(current_block_index)
        attention_logits, visible = block_scores(current_block_index, key_portion)
        probability = jnp.where(visible, jnp.exp(attention_logits - log_total), 0.0)
        gradient_probabilities = jnp.einsum(
            "nifc,zic->ifnz",
            gradient_grouped_heads,
            value_portion,
            preferred_element_type=jnp.float32,
        )
        score_gradient = (probability * (gradient_probabilities - row_dots)).astype(jnp.bfloat16)
        attention_probabilities = probability.astype(jnp.bfloat16)
        query_sum = query_sum + jnp.einsum(
            "ezhm,meo->hezo", score_gradient, key_portion, preferred_element_type=jnp.float32
        )
        key_contribution = (
            jnp.einsum(
                "jmua,ujmf->ajf", score_gradient, grouped_heads, preferred_element_type=jnp.float32
            )
            * logit_scale
        )
        value_contribution = jnp.einsum(
            "jmua,ujmf->ajf",
            attention_probabilities,
            gradient_grouped_heads,
            preferred_element_type=jnp.float32,
        )
        block_term = jnp.concatenate(
            [
                key_contribution.reshape(block_len, kv_width),
                value_contribution.reshape(block_len, kv_width),
            ],
            axis=1,
        )
        term_rows = lax.dynamic_update_slice_in_dim(
            term_rows, block_term, current_block_index * block_len, 0
        )
        return (query_sum, term_rows)

    empty_terms = jnp.zeros((seq_len, 2 * kv_width), jnp.float32)
    grad_query_sum, key_terms = lax.fori_loop(
        0, visible_blocks, backward_pass, (empty_out, empty_terms)
    )
    kv_grad = lax.psum_scatter(
        key_terms.astype(jnp.bfloat16), "shard", scatter_dimension=0, tiled=True
    ).astype(jnp.float32)
    query_gradient = rotate(
        grad_query_sum.reshape(tok_count, inner_width) * logit_scale, cosine, -sine, HEADS
    ).astype(jnp.bfloat16)
    grad_keys = rotate(kv_grad[:, :kv_width], cosine, -sine, KV_HEADS).astype(jnp.bfloat16)
    grad_values = kv_grad[:, kv_width:].astype(jnp.bfloat16)
    grad_proj = jnp.concatenate([query_gradient, grad_keys, grad_values], axis=1)
    tokens_grad = lax.dot_general(
        grad_proj, qkv_full, (((1,), (1,)), ((), ())), preferred_element_type=jnp.float32
    ).astype(jnp.bfloat16)
    qkv_share = lax.psum_scatter(
        lax.dot_general(
            inputs, grad_proj, (((0,), (0,)), ((), ())), preferred_element_type=jnp.float32
        ).astype(jnp.bfloat16),
        "shard",
        scatter_dimension=0,
        tiled=True,
    ).astype(jnp.float32)
    qkv_total, out_total = lax.psum((qkv_share, out_share), "rep")
    norm_factor = 1.0 / math.sqrt(lax.axis_size("rep") * seq_len)
    return (block_output[None], tokens_grad[None], qkv_total * norm_factor, out_total * norm_factor)


def solution(mesh):
    return jax.shard_map(
        body,
        mesh=mesh,
        in_specs=(
            P("rep", "shard", None),
            P("shard", None),
            P("shard", None),
            P("rep", "shard", None),
        ),
        out_specs=(
            P("rep", "shard", None),
            P("rep", "shard", None),
            P("shard", None),
            P("shard", None),
        ),
        check_vma=False,
    )
```

profile of v0, /device:TPU:1, one launch (start us, length us, event | category | flops | bytes accessed | tf_op | source)
XLA Modules:
  0.0 1274.9 jit_solution(13649723822725968365)
XLA Ops:
  7.2 0.0 copy-start
  7.2 0.0 all-gather.4.cloned.1.call-start
  7.2 0.7 all-gather.4.cloned.1.call-update
  7.9 0.0 all-gather.8.cloned.1.call-start
  8.0 0.7 all-gather.8.cloned.1.call-update
  8.7 0.0 all-gather.6.cloned.1.call-start
  8.7 0.1 fusion.39
  8.9 137.7 %all-gather.4.cloned.1.call-done = bf16[2048,1536]{1,0:T(8,128)(2,1)} async-done(((bf16[64,1536]{1,0:T(8,128)(2,1)}), bf16[2048,1536]{1,0:T(8,128)(2,1)}) %all-gather.4.cloned.1.call-update) | async-done | bytes 6291472 | tf_op jit(solution)/shard_map/all_gather | solution.py:53
  146.6 3.8 fusion.37
  150.4 0.1 copy.39
  150.6 0.1 copy.40
  150.7 0.7 pad_maximum_fusion.5
  151.3 0.0 all-gather.6.cloned.1.call-update
  151.4 0.0 reduce-scatter.10.cloned.1.call-start
  151.4 101.2 %all-gather.8.cloned.1.call-done = bf16[1024,2048]{1,0:T(8,128)(2,1)} async-done(((bf16[32,2048]{1,0:T(8,128)(2,1)}), bf16[1024,2048]{1,0:T(8,128)(2,1)}) %all-gather.8.cloned.1.call-update) | async-done | bytes 4194320 | tf_op jit(solution)/shard_map/all_gather | solution.py:54
  252.7 3.7 convolution_convert_fusion.4
  256.4 0.2 copy.44
  256.6 0.2 copy.41
  256.8 0.1 subtract_convert_fusion.1
  256.9 105.6 %all-gather.6.cloned.1.call-done = bf16[4096,512]{1,0:T(8,128)(2,1)} async-done(((bf16[128,512]{1,0:T(8,128)(2,1)}), bf16[4096,512]{1,0:T(8,128)(2,1)}) %all-gather.6.cloned.1.call-update) | async-done | bytes 4194320 | tf_op jit(solution)/shard_map/all_gather | solution.py:65
  362.5 6.5 copy.43
  369.0 2.8 while.37
  369.0 0.1 broadcast_compare_fusion.6
  369.2 1.0 constant_dynamic-slice_fusion.5
  370.2 0.8 fusion.91
  371.0 0.9 fusion.92
  371.9 2.5 while.38
  372.0 0.1 broadcast_compare_fusion.7
  372.1 1.1 constant_dynamic-slice_fusion.6
  373.2 1.2 fusion.96
  374.4 0.1 fusion.33
  374.6 2.6 broadcast_in_dim.71
  377.2 6.5 while.39
  377.2 0.1 broadcast_compare_fusion.8
  377.3 1.1 fusion.107
  378.4 0.8 fusion.108
  379.1 0.9 fusion.111
  380.0 1.4 fusion.109
  381.4 0.8 fusion.112
  382.2 0.5 fusion.110
  382.8 0.9 maximum_dynamic-update-slice_fusion.2
  383.7 6.6 copy.66
  390.2 0.0 reduce-scatter.10.cloned.1.call-update
  390.2 0.0 reduce-scatter.8.cloned.1.call-start
  390.3 3.3 convolution_convert_fusion.1
  393.6 0.0 reduce-scatter.8.cloned.1.call-update
  393.6 0.2 reduce-scatter.12.cloned.1.call-start
  393.9 0.1 subtract_convert_fusion
  394.0 289.6 %reduce-scatter.10.cloned.1.call-done = bf16[128,512]{1,0:T(8,128)(2,1)} async-done(((bf16[4096,512]{1,0:T(8,128)(2,1)}), bf16[128,512]{1,0:T(8,128)(2,1)}) %reduce-scatter.10.cloned.1.call-update) | async-done | bytes 131088
  683.6 0.9 fusion.43
  684.5 0.1 copy.71
  684.6 0.1 copy.72
  684.8 4.4 fusion.30
  689.2 8.7 copy.68
  697.9 0.0 reduce-scatter.12.cloned.1.call-update
  697.9 3.7 fusion.31
  701.6 216.0 %reduce-scatter.8.cloned.1.call-done = bf16[32,2048]{1,0:T(8,128)(2,1)} async-done(((bf16[1024,2048]{1,0:T(8,128)(2,1)}), bf16[32,2048]{1,0:T(8,128)(2,1)}) %reduce-scatter.8.cloned.1.call-update) | async-done | bytes 131088 | tf_op jit(solution)/shard_map/reduce_scatter | solution.py:130
  917.6 5.8 fusion.32
  923.4 284.2 %reduce-scatter.12.cloned.1.call-done = bf16[64,1536]{1,0:T(8,128)(2,1)} async-done(((bf16[2048,1536]{1,0:T(8,128)(2,1)}), bf16[64,1536]{1,0:T(8,128)(2,1)}) %reduce-scatter.12.cloned.1.call-update) | async-done | bytes 196624
  1207.6 1.1 copy.69
  1208.8 57.5 %all-reduce.2 = (f32[64,1536]{0,1:T(8,128)S(1)}, f32[32,2048]{1,0:T(8,128)S(1)}) all-reduce(bf16[64,1536]{0,1:T(8,128)(2,1)S(1)} %copy.69, bf16[32,2048]{1,0:T(8,128)(2,1)S(1)} %copy-done.2), channel_id=1, replica_groups=mesh['shard'=32,'rep'=8] {'rep'}, use_global_device_ids=true, to_apply=%region_10.11 | all-reduce | flops 163840 | bytes 983040 | tf_op jit(solution)/shard_map/psum | solution.py:211
  1266.3 0.1 broadcast_multiply_fusion
  1266.3 1.0 copy.46
  1267.3 0.7 broadcast_multiply_fusion.2
  (32 shorter events, 0.4 us)
Async XLA Ops:
  7.2 139.4 %copy-start = (bf16[1,128,2048]{2,1,0:T(8,128)(2,1)S(1)}, bf16[1,128,2048]{2,1,0:T(8,128)(2,1)}, u32[]{:S(2)}) copy-start(bf16[1,128,2048]{2,1,0:T(8,128)(2,1)} %param.10) | copy-start | bytes 1572868
  7.2 139.4 %all-gather.4.cloned.1.call-start = ((), (), s32[]{:S(2)}) async-start(), calls=%async_computation.3 | async-start | bytes 6488064 | tf_op jit(solution)/shard_map/all_gather | solution.py:53
  7.9 244.8 %all-gather.8.cloned.1.call-start = ((), (), s32[]{:S(2)}) async-start(), calls=%async_computation.5 | async-start | bytes 4325376 | tf_op jit(solution)/shard_map/all_gather | solution.py:54
  8.7 353.9 %all-gather.6.cloned.1.call-start = ((), (), s32[]{:S(2)}) async-start(), calls=%async_computation.4 | async-start | bytes 4325376 | tf_op jit(solution)/shard_map/all_gather | solution.py:65
  8.9 243.8 %copy-start.1 = (bf16[1,128,2048]{2,1,0:T(8,128)(2,1)S(1)}, bf16[1,128,2048]{2,1,0:T(8,128)(2,1)}, u32[]{:S(2)}) copy-start(bf16[1,128,2048]{2,1,0:T(8,128)(2,1)} %param.13) | copy-start | bytes 1572868
  151.4 532.3 %reduce-scatter.10.cloned.1.call-start = ((), (), s32[]{:S(2)}) async-start(), calls=%async_computation.7 | async-start | bytes 4325376
  390.2 527.4 %reduce-scatter.8.cloned.1.call-start = ((), (), s32[]{:S(2)}) async-start(), calls=%async_computation.6 | async-start | bytes 4325376 | tf_op jit(solution)/shard_map/reduce_scatter | solution.py:130
  393.6 814.0 %reduce-scatter.12.cloned.1.call-start = ((), (), s32[]{:S(2)}) async-start(), calls=%async_computation.8 | async-start | bytes 6488064
  917.6 291.2 %copy-start.2 = (bf16[32,2048]{1,0:T(8,128)(2,1)S(1)}, bf16[32,2048]{1,0:T(8,128)(2,1)}, u32[]{:S(2)}) copy-start(bf16[32,2048]{1,0:T(8,128)(2,1)} %reduce-scatter.8.cloned.1.call-done) | copy-start | bytes 393220
Sparse Core Ops, SparseCore 0:
  11.4 135.1 all-gather.3
  150.1 102.5 all-gather.7
  256.8 105.7 all-gather.5
  390.4 293.2 reduce-scatter.9
  686.0 231.5 reduce-scatter.7
  923.0 284.5 reduce-scatter.11
where the time goes:
time: 1280 us; the launch traced here: 1270 us
  waiting for transfers between devices  1140 us (89%)
  blocking collectives  57.5 us (4%)
  local copies, waits for them, and re-layouts  31.4 us (2%)
  matrix products  31 us (2%)
  between operations  14.4 us (1%)
    unnamed x8, waiting for transfers between devices  575 us
    reduce_scatter x1, waiting for transfers between devices, body(): lax.psum_scatter(lax.dot_general(attended_values, grad_output, (((0,), (0...  216 us
    all_gather x1, waiting for transfers between devices, body(): lax.all_gather(qkv_weight, 'shard', axis=0, tiled=True)  138 us
    all_gather x1, waiting for transfers between devices, body(): gathered = lax.all_gather(stacked, 'shard', axis=0, tiled=True)  106 us
    all_gather x1, waiting for transfers between devices, body(): lax.all_gather(out_weight, 'shard', axis=0, tiled=True)  101 us
    psum x1, blocking collectives, body(): qkv_total, out_total = lax.psum((qkv_share, out_share), 'rep')  57.5 us
  transfers between devices with their start and end apart: 6, of which 6 were waited for; matrix products, arithmetic and copies ran while one was open for 3% of the time, Pallas kernels for 0%

commit v1 on v0

--- a/solution.py
+++ b/solution.py
@@ -1,17 +1,700 @@
+import functools
 import math
 
 import jax
 import jax.numpy as jnp
 from jax import lax
+from jax.experimental import pallas as pl
+from jax.experimental.pallas import tpu as pltpu
 from jax.sharding import PartitionSpec as P
 
 HEADS = 16
 KV_HEADS = 4
 HEAD_DIM = 64
 
-
 ROPE_BASE = 500000.0
 NEG_FILL = -1e30
+MESH = pl.DeviceIdType.MESH
+BF16 = jnp.bfloat16
+F32 = jnp.float32
+VMEM_BYTES = 60 * 1024 * 1024
+
+
+class Net:
+    def __init__(self):
+        self.s = lax.axis_index("shard")
+        self.r = lax.axis_index("rep")
+        self.zh = self.s // 16
+        self.x = lax.rem(self.s // 4, 4)
+        self.y = lax.rem(self.s, 4)
+        self.zl = self.r // 2
+        self.core = lax.rem(self.r, 2)
+        self.z = self.zh * 4 + self.zl
+
+    def at(self, h, da, db):
+        dx, dy = (da, db) if h == 0 else (db, da)
+        return lax.rem(self.x + (dx + 4), 4), lax.rem(self.y + (dy + 4), 4)
+
+    def dev(self, h, da, db):
+        gx, gy = self.at(h, da, db)
+        return (self.zh * 16 + gx * 4 + gy, self.r)
+
+    def sibling(self):
+        return (self.s, self.zl * 2 + 1 - self.core)
+
+    def partner(self):
+        return (lax.rem(self.s + 16, 32), self.r)
+
+    def up(self, k):
+        z = lax.rem(self.z + k, 8)
+        return ((z // 4) * 16 + self.x * 4 + self.y, lax.rem(z, 4) * 2 + self.core)
+
+    def xy_neighbours(self):
+        return [self.dev(0, 1, 0), self.dev(0, -1, 0), self.dev(0, 0, 1), self.dev(0, 0, -1)]
+
+
+def greet(devices):
+    barrier = pltpu.get_barrier_semaphore()
+    for device in devices:
+        pl.semaphore_signal(barrier, inc=1, device_id=device, device_id_type=MESH)
+    pl.semaphore_wait(barrier, len(devices))
+
+
+class Wire:
+    def __init__(self, send_sems, recv_sems):
+        self.send_sems, self.recv_sems = send_sems, recv_sems
+        self.used = 0
+        self.sent = []
+
+    def new(self, count=1):
+        first = self.used
+        self.used += count
+        return first
+
+    def copy(self, src, dst, key, device):
+        return pltpu.make_async_remote_copy(
+            src_ref=src,
+            dst_ref=dst,
+            send_sem=self.send_sems.at[key],
+            recv_sem=self.recv_sems.at[key],
+            device_id=device,
+            device_id_type=MESH,
+        )
+
+    def send(self, src, dst, key, device):
+        made = self.copy(src, dst, key, device)
+        made.start()
+        self.sent.append(made)
+
+    def recv(self, ref, key, device):
+        self.copy(ref, ref, key, device).wait_recv()
+
+    def drain(self):
+        for made in self.sent:
+            made.wait_send()
+        self.sent = []
+
+
+SIDES = (1, -1)
+RING = (0, 1, -1, 2)
+AG_KEYS = 40
+
+
+def side(d):
+    return 0 if d == 1 else 1
+
+
+def gather_stages(net, wire, own, piece):
+    base = wire.new(AG_KEYS)
+
+    def s1(h, d):
+        return base + h * 2 + side(d)
+
+    def s2(h, d):
+        return base + 4 + h * 2 + side(d)
+
+    def t1(h, da, d):
+        return base + 8 + (h * 4 + RING.index(da)) * 2 + side(d)
+
+    def t2(h, da, d):
+        return base + 24 + (h * 4 + RING.index(da)) * 2 + side(d)
+
+    def at(h, da, db, part=None):
+        return piece(*net.at(h, da, db), h, part)
+
+    def spread(h, da, src):
+        for d in SIDES:
+            wire.send(src, at(h, da, 0), t1(h, da, d), net.dev(h, 0, d))
+
+    def pass_on(h, da):
+        for d in SIDES:
+            wire.recv(at(h, da, -d), t1(h, da, d), net.dev(h, 0, -d))
+            part = side(d)
+            wire.send(at(h, da, -d, part), at(h, da, -d, part), t2(h, da, d), net.dev(h, 0, d))
+
+    def stage_a():
+        for h in (0, 1):
+            for d in SIDES:
+                wire.send(own(h), at(h, 0, 0), s1(h, d), net.dev(h, d, 0))
+        for h in (0, 1):
+            spread(h, 0, own(h))
+
+    def stage_b():
+        for d in SIDES:
+            for h in (0, 1):
+                wire.recv(at(h, -d, 0), s1(h, d), net.dev(h, -d, 0))
+                part = side(d)
+                wire.send(at(h, -d, 0, part), at(h, -d, 0, part), s2(h, d), net.dev(h, d, 0))
+        for d in SIDES:
+            for h in (0, 1):
+                spread(h, -d, at(h, -d, 0))
+
+    def stage_c():
+        for h in (0, 1):
+            pass_on(h, 0)
+
+    def stage_d():
+        for h in (0, 1):
+            for d in SIDES:
+                wire.recv(at(h, 2, 0, side(d)), s2(h, d), net.dev(h, -d, 0))
+            spread(h, 2, at(h, 2, 0))
+
+    def stage_e():
+        for da in (-1, 1):
+            for h in (0, 1):
+                pass_on(h, da)
+
+    def stage_f():
+        for h in (0, 1):
+            pass_on(h, 2)
+
+    def stage_g():
+        for da in (0, -1, 1, 2):
+            for h in (0, 1):
+                for d in SIDES:
+                    wire.recv(at(h, da, 2, side(d)), t2(h, da, d), net.dev(h, 0, -d))
+
+    return [stage_a, stage_b, stage_c, stage_d, stage_e, stage_f, stage_g]
+
+
+def scatter_scratch(rows, cols):
+    return [
+        pltpu.VMEM((2, 4, 2, rows // 2, cols), BF16),
+        pltpu.VMEM((2, 4, 2, rows, cols), BF16),
+        pltpu.VMEM((2, 4, 2, rows, cols), BF16),
+        pltpu.VMEM((2, 3, rows, cols), F32),
+        pltpu.VMEM((2, rows, cols), BF16),
+        pltpu.VMEM((2, 2, rows // 2, cols), BF16),
+        pltpu.VMEM((2, 2, rows, cols), BF16),
+        pltpu.VMEM((2, 2, rows, cols), BF16),
+    ]
+
+
+def scatter_stages(net, wire, own, bufs, emit):
+    t2b, t1s, t1b, row_sum, s2s, s2b, s1s, s1b = bufs
+    rows = row_sum.shape[2]
+    half = rows // 2
+    base = wire.new(AG_KEYS)
+
+    def s1(h, d):
+        return base + h * 2 + side(d)
+
+    def s2(h, d):
+        return base + 4 + h * 2 + side(d)
+
+    def t1(h, i, d):
+        return base + 8 + (h * 4 + i) * 2 + side(d)
+
+    def t2(h, i, d):
+        return base + 24 + (h * 4 + i) * 2 + side(d)
+
+    def load(h, da, db, part=None):
+        return own(*net.at(h, da, db), h, part)[...].astype(F32)
+
+    order = (2, 1, -1, 0)
+
+    def stage_a():
+        for da in order:
+            i = RING.index(da)
+            for h in (0, 1):
+                for d in SIDES:
+                    p = side(d)
+                    wire.send(own(*net.at(h, da, 2), h, p), t2b.at[h, i, p], t2(h, i, d), net.dev(h, 0, d))
+
+    def stage_b():
+        for da in order:
+            i = RING.index(da)
+            for h in (0, 1):
+                for d in SIDES:
+                    p = side(d)
+                    wire.recv(t2b.at[h, i, p], t2(h, i, d), net.dev(h, 0, -d))
+                    t1s[h, i, p, pl.ds(p * half, half)] = (
+                        load(h, da, d, p) + t2b[h, i, p].astype(F32)
+                    ).astype(BF16)
+                    t1s[h, i, p, pl.ds((1 - p) * half, half)] = load(h, da, d, 1 - p).astype(BF16)
+                    wire.send(t1s.at[h, i, p], t1b.at[h, i, p], t1(h, i, d), net.dev(h, 0, d))
+
+    def stage_c():
+        for da in order:
+            i = RING.index(da)
+            for h in (0, 1):
+                for d in SIDES:
+                    wire.recv(t1b.at[h, i, side(d)], t1(h, i, d), net.dev(h, 0, -d))
+                total = load(h, da, 0) + t1b[h, i, 0].astype(F32) + t1b[h, i, 1].astype(F32)
+                if da == 2:
+                    s2s[h] = total.astype(BF16)
+                    for d in SIDES:
+                        p = side(d)
+                        wire.send(s2s.at[h, pl.ds(p * half, half)], s2b.at[h, p], s2(h, d), net.dev(h, d, 0))
+                else:
+                    row_sum[h, i] = total
+
+    def stage_d():
+        for h in (0, 1):
+            for d in SIDES:
+                p = side(d)
+                i = RING.index(d)
+                wire.recv(s2b.at[h, p], s2(h, d), net.dev(h, -d, 0))
+                s1s[h, p, pl.ds(p * half, half)] = (
+                    row_sum[h, i, pl.ds(p * half, half)] + s2b[h, p].astype(F32)
+                ).astype(BF16)
+                s1s[h, p, pl.ds((1 - p) * half, half)] = row_sum[h, i, pl.ds((1 - p) * half, half)].astype(BF16)
+                wire.send(s1s.at[h, p], s1b.at[h, p], s1(h, d), net.dev(h, d, 0))
+
+    def stage_e():
+        for h in (0, 1):
+            for d in SIDES:
+                wire.recv(s1b.at[h, side(d)], s1(h, d), net.dev(h, -d, 0))
+            emit(h, row_sum[h, 0] + s1b[h, 0].astype(F32) + s1b[h, 1].astype(F32))
+
+    return [stage_a, stage_b, stage_c, stage_d, stage_e]
+
+
+def weight_gather_kernel(qkv_in, out_in, qkv_full, out_full, send_sems, recv_sems, local_sems):
+    net = Net()
+    wire = Wire(send_sems, recv_sems)
+    core, s = net.core, net.s
+    other = 1 - net.zh
+    qcols = pl.ds(pl.multiple_of(core * 768, 128), 768)
+
+    def ocols(h):
+        return pl.ds(pl.multiple_of(core * 1024 + h * 512, 128), 512)
+
+    def qkv_piece(group):
+        def piece(gx, gy, h, part):
+            row = (group * 16 + gx * 4 + gy) * 64 + h * 32
+            if part is None:
+                return qkv_full.at[pl.ds(pl.multiple_of(row, 16), 32), qcols]
+            return qkv_full.at[pl.ds(pl.multiple_of(row + part * 16, 16), 16), qcols]
+
+        return piece
+
+    def out_piece(group):
+        def piece(gx, gy, h, part):
+            row = (group * 16 + gx * 4 + gy) * 32
+            if part is None:
+                return out_full.at[pl.ds(pl.multiple_of(row, 16), 32), ocols(h)]
+            return out_full.at[pl.ds(pl.multiple_of(row + part * 16, 16), 16), ocols(h)]
+
+        return piece
+
+    greet(net.xy_neighbours() + [net.sibling(), net.partner()])
+
+    ohalf = pl.ds(pl.multiple_of(core * 1024, 128), 1024)
+    qrow = pl.ds(pl.multiple_of(s * 64, 64), 64)
+    orow = pl.ds(pl.multiple_of(s * 32, 32), 32)
+    zkey = wire.new(2)
+    wire.send(qkv_in.at[:, qcols], qkv_full.at[qrow, qcols], zkey, net.partner())
+    wire.send(out_in.at[:, ohalf], out_full.at[orow, ohalf], zkey + 1, net.partner())
+    own_q = gather_stages(net, wire, lambda h: qkv_in.at[pl.ds(h * 32, 32), qcols], qkv_piece(net.zh))
+    own_o = gather_stages(net, wire, lambda h: out_in.at[:, ocols(h)], out_piece(net.zh))
+    for a, b in zip(own_q[:1], own_o[:1]):
+        a()
+        b()
+    keep_q = pltpu.make_async_copy(qkv_in.at[:, qcols], qkv_full.at[qrow, qcols], local_sems.at[0])
+    keep_o = pltpu.make_async_copy(out_in.at[:, ohalf], out_full.at[orow, ohalf], local_sems.at[1])
+    keep_q.start()
+    keep_o.start()
+    for a, b in zip(own_q[1:6], own_o[1:6]):
+        a()
+        b()
+    far = lax.rem(s + 16, 32)
+    far_q = qkv_full.at[pl.ds(pl.multiple_of(far * 64, 64), 64), qcols]
+    far_o = out_full.at[pl.ds(pl.multiple_of(far * 32, 32), 32), ohalf]
+    wire.recv(far_q, zkey, net.partner())
+    wire.recv(far_o, zkey + 1, net.partner())
+    far_qp, far_op = qkv_piece(other), out_piece(other)
+    two_q = gather_stages(net, wire, lambda h: far_qp(net.x, net.y, h, None), far_qp)
+    two_o = gather_stages(net, wire, lambda h: far_op(net.x, net.y, h, None), far_op)
+    two_q[0]()
+    two_o[0]()
+    own_q[6]()
+    own_o[6]()
+    keep_q.wait()
+    keep_o.wait()
+
+    dkey = wire.new(4)
+
+    def sides_of(group, which):
+        cols = pl.ds(pl.multiple_of(which * 768, 128), 768)
+        cols_o = pl.ds(pl.multiple_of(which * 1024, 128), 1024)
+        return (
+            qkv_full.at[pl.ds(pl.multiple_of(group * 1024, 64), 1024), cols],
+            out_full.at[pl.ds(pl.multiple_of(group * 512, 32), 512), cols_o],
+        )
+
+    def share(group, key):
+        for i, ref in enumerate(sides_of(group, core)):
+            wire.send(ref, ref, key + i, net.sibling())
+
+    share(net.zh, dkey)
+    for a, b in zip(two_q[1:], two_o[1:]):
+        a()
+        b()
+    share(other, dkey + 2)
+    for group, key in ((net.zh, dkey), (other, dkey + 2)):
+        for i, ref in enumerate(sides_of(group, 1 - core)):
+            wire.recv(ref, key + i, net.sibling())
+    wire.drain()
+
+
+def gather_weights(qkv_weight, out_weight):
+    keys = 4 * AG_KEYS + 6
+    return pl.pallas_call(
+        weight_gather_kernel,
+        out_shape=(
+            jax.ShapeDtypeStruct((2048, 1536), BF16),
+            jax.ShapeDtypeStruct((1024, 2048), BF16),
+        ),
+        in_specs=[pl.BlockSpec(memory_space=pl.ANY)] * 2,
+        out_specs=[pl.BlockSpec(memory_space=pl.ANY)] * 2,
+        scratch_shapes=[
+            pltpu.SemaphoreType.DMA((keys,)),
+            pltpu.SemaphoreType.DMA((keys,)),
+            pltpu.SemaphoreType.DMA((2,)),
+        ],
+        compiler_params=pltpu.CompilerParams(collective_id=0, has_side_effects=True),
+        name="gather_weights",
+    )(qkv_weight, out_weight)
+
+
+def kv_gather_kernel(kv_in, kv_full, send_sems, recv_sems, local_sems):
+    net = Net()
+    wire = Wire(send_sems, recv_sems)
+    other = 1 - net.zh
+
+    def kv_piece(group):
+        def piece(gx, gy, h, part):
+            row = (group * 16 + gx * 4 + gy) * 128 + h * 64
+            if part is None:
+                return kv_full.at[pl.ds(pl.multiple_of(row, 32), 64)]
+            return kv_full.at[pl.ds(pl.multiple_of(row + part * 32, 32), 32)]
+
+        return piece
+
+    greet(net.xy_neighbours() + [net.partner()])
+    mine = kv_full.at[pl.ds(pl.multiple_of(net.s * 128, 128), 128)]
+    zkey = wire.new(1)
+    wire.send(kv_in, mine, zkey, net.partner())
+    near = gather_stages(net, wire, lambda h: kv_in.at[pl.ds(h * 64, 64)], kv_piece(net.zh))
+    near[0]()
+    keep = pltpu.make_async_copy(kv_in, mine, local_sems.at[0])
+    keep.start()
+    for stage in near[1:6]:
+        stage()
+    far = lax.rem(net.s + 16, 32)
+    wire.recv(kv_full.at[pl.ds(pl.multiple_of(far * 128, 128), 128)], zkey, net.partner())
+    far_piece = kv_piece(other)
+    rest = gather_stages(net, wire, lambda h: far_piece(net.x, net.y, h, None), far_piece)
+    rest[0]()
+    near[6]()
+    for stage in rest[1:]:
+        stage()
+    keep.wait()
+    wire.drain()
+
+
+def gather_kv(stacked):
+    keys = 2 * AG_KEYS + 1
+    return pl.pallas_call(
+        kv_gather_kernel,
+        out_shape=jax.ShapeDtypeStruct((4096, 512), BF16),
+        in_specs=[pl.BlockSpec(memory_space=pl.ANY)],
+        out_specs=pl.BlockSpec(memory_space=pl.ANY),
+        scratch_shapes=[
+            pltpu.SemaphoreType.DMA((keys,)),
+            pltpu.SemaphoreType.DMA((keys,)),
+            pltpu.SemaphoreType.DMA((1,)),
+        ],
+        compiler_params=pltpu.CompilerParams(collective_id=1, has_side_effects=True),
+        name="gather_kv",
+    )(stacked)
+
+
+def kv_scatter_kernel(terms, result, far_out, far_in, send_sems, recv_sems, *bufs):
+    net = Net()
+    wire = Wire(send_sems, recv_sems)
+    far_bufs, near_bufs = bufs[:8], bufs[8:]
+
+    def own(group):
+        def piece(gx, gy, h, part):
+            row = (group * 16 + gx * 4 + gy) * 128 + h * 64
+            if part is None:
+                return terms.at[pl.ds(pl.multiple_of(row, 32), 64)]
+            return terms.at[pl.ds(pl.multiple_of(row + part * 32, 32), 32)]
+
+        return piece
+
+    greet(net.xy_neighbours() + [net.partner()])
+    zkey = wire.new(2)
+
+    def emit_far(h, total):
+        far_out[h] = total.astype(BF16)
+        wire.send(far_out.at[h], far_in.at[h], zkey + h, net.partner())
+
+    def emit_near(h, total):
+        result[pl.ds(h * 64, 64)] = total
+
+    far = scatter_stages(net, wire, own(1 - net.zh), far_bufs, emit_far)
+    near = scatter_stages(net, wire, own(net.zh), near_bufs, emit_near)
+    far[0]()
+    far[1]()
+    near[0]()
+    far[2]()
+    near[1]()
+    far[3]()
+    near[2]()
+    far[4]()
+    near[3]()
+    near[4]()
+    for h in (0, 1):
+        wire.recv(far_in.at[h], zkey + h, net.partner())
+        result[pl.ds(h * 64, 64)] += far_in[h].astype(F32)
+    wire.drain()
+
+
+def scatter_kv(terms):
+    keys = 2 * AG_KEYS + 2
+    return pl.pallas_call(
+        kv_scatter_kernel,
+        out_shape=jax.ShapeDtypeStruct((128, 512), F32),
+        in_specs=[pl.BlockSpec(memory_space=pltpu.VMEM)],
+        out_specs=pl.BlockSpec(memory_space=pltpu.VMEM),
+        scratch_shapes=[
+            pltpu.VMEM((2, 64, 512), BF16),
+            pltpu.VMEM((2, 64, 512), BF16),
+            pltpu.SemaphoreType.DMA((keys,)),
+            pltpu.SemaphoreType.DMA((keys,)),
+            *scatter_scratch(64, 512),
+            *scatter_scratch(64, 512),
+        ],
+        compiler_params=pltpu.CompilerParams(
+            collective_id=2, has_side_effects=True, vmem_limit_bytes=VMEM_BYTES
+        ),
+        name="scatter_kv",
+    )(terms)
+
+
+def weight_scatter_kernel(
+    scale,
+    dq,
+    do,
+    out_q,
+    out_o,
+    sib_q,
+    sib_o,
+    sum_q,
+    sum_o,
+    zs_q,
+    zs_o,
+    zr_q,
+    zr_o,
+    keep_q,
+    keep_o,
+    fin_q,
+    fin_o,
+    send_sems,
+    recv_sems,
+    local_sems,
+    *bufs,
+):
+    net = Net()
+    wire = Wire(send_sems, recv_sems)
+    core = net.core
+    cols_q = [pl.ds(pl.multiple_of(c * 768, 128), 768) for c in (core, 1 - core)]
+    cols_o = [pl.ds(pl.multiple_of(c * 1024, 128), 1024) for c in (core, 1 - core)]
+    greet(net.xy_neighbours() + [net.sibling()] + [net.up(k) for k in range(1, 8)])
+
+    ckey = wire.new(4)
+    for g in (0, 1):
+        rq, ro = pl.ds(g * 1024, 1024), pl.ds(g * 512, 512)
+        wire.send(dq.at[rq, cols_q[1]], sib_q.at[rq], ckey + 2 * g, net.sibling())
+        wire.send(do.at[ro, cols_o[1]], sib_o.at[ro], ckey + 2 * g + 1, net.sibling())
+
+    def add_cores(g):
+        rq, ro = pl.ds(g * 1024, 1024), pl.ds(g * 512, 512)
+        wire.recv(sib_q.at[rq], ckey + 2 * g, net.sibling())
+        wire.recv(sib_o.at[ro], ckey + 2 * g + 1, net.sibling())
+
+        def step(i, carry):
+            rows = pl.ds(pl.multiple_of(g * 1024 + i * 64, 64), 64)
+            sum_q[rows] = (dq[rows, cols_q[0]].astype(F32) + sib_q[rows].astype(F32)).astype(BF16)
+            rows = pl.ds(pl.multiple_of(g * 512 + i * 32, 32), 32)
+            sum_o[rows] = (do[rows, cols_o[0]].astype(F32) + sib_o[rows].astype(F32)).astype(BF16)
+            return carry
+
+        lax.fori_loop(0, 16, step, 0)
+
+    def own_q(g):
+        def piece(gx, gy, h, part):
+            row = (g * 16 + gx * 4 + gy) * 64 + h * 32
+            if part is None:
+                return sum_q.at[pl.ds(pl.multiple_of(row, 16), 32)]
+            return sum_q.at[pl.ds(pl.multiple_of(row + part * 16, 16), 16)]
+
+        return piece
+
+    def own_o(g):
+        def piece(gx, gy, h, part):
+            row = (g * 16 + gx * 4 + gy) * 32
+            if part is None:
+                return sum_o.at[pl.ds(pl.multiple_of(row, 16), 32), pl.ds(h * 512, 512)]
+            return sum_o.at[pl.ds(pl.multiple_of(row + part * 16, 16), 16), pl.ds(h * 512, 512)]
+
+        return piece
+
+    def emit_q(g):
+        def emit(h, total):
+            for part in (0, 1):
+                rows = total[part * 16 : part * 16 + 16]
+                keep_q[g, 2 * h + part] = rows
+                zs_q[g, 2 * h + part] = rows.astype(BF16)
+
+        return emit
+
+    def emit_o(g):
+        def emit(h, total):
+            for part in (0, 1):
+                columns = total[:, part * 256 : part * 256 + 256]
+                keep_o[g, 2 * h + part] = columns
+                zs_o[g, 2 * h + part] = columns.astype(BF16)
+
+        return emit
+
+    runs = []
+    for g in (0, 1):
+        runs.append(
+            (
+                scatter_stages(net, wire, own_q(g), bufs[16 * g : 16 * g + 8], emit_q(g)),
+                scatter_stages(net, wire, own_o(g), bufs[16 * g + 8 : 16 * g + 16], emit_o(g)),
+            )
+        )
+
+    def run(g, stage):
+        for stages in runs[g]:
+            stages[stage]()
+
+    add_cores(0)
+    run(0, 0)
+    add_cores(1)
+    run(1, 0)
+    run(0, 1)
+    run(1, 1)
+    run(0, 2)
+    run(1, 2)
+    run(0, 3)
+    run(1, 3)
+    run(0, 4)
+    run(1, 4)
+
+    z1 = wire.new(14)
+    for k in range(1, 8):
+        target = lax.rem(net.z + k, 8)
+        g, l = target // 4, lax.rem(target, 4)
+        wire.send(zs_q.at[g, l], zr_q.at[k - 1], z1 + 2 * (k - 1), net.up(k))
+        wire.send(zs_o.at[g, l], zr_o.at[k - 1], z1 + 2 * (k - 1) + 1, net.up(k))
+    total_q, total_o = keep_q[net.zh, net.zl], keep_o[net.zh, net.zl]
+    for k in range(1, 8):
+        wire.recv(zr_q.at[k - 1], z1 + 2 * (k - 1), net.up(8 - k))
+        wire.recv(zr_o.at[k - 1], z1 + 2 * (k - 1) + 1, net.up(8 - k))
+        total_q = total_q + zr_q[k - 1].astype(F32)
+        total_o = total_o + zr_o[k - 1].astype(F32)
+    fin_q[...] = total_q * scale
+    fin_o[...] = total_o * scale
+
+    def place(l):
+        return (
+            out_q.at[pl.ds(pl.multiple_of(l * 16, 16), 16), cols_q[0]],
+            out_o.at[:, pl.ds(pl.multiple_of(core * 1024 + l * 256, 128), 256)],
+        )
+
+    def level(k):
+        l = lax.rem(net.zl + k, 4)
+        return l, (net.s, l * 2 + core)
+
+    z2 = wire.new(6)
+    mine = place(net.zl)
+    for k in (1, 2, 3):
+        device = level(k)[1]
+        wire.send(fin_q, mine[0], z2 + 2 * (k - 1), device)
+        wire.send(fin_o, mine[1], z2 + 2 * (k - 1) + 1, device)
+    own_copies = [
+        pltpu.make_async_copy(fin_q, mine[0], local_sems.at[0]),
+        pltpu.make_async_copy(fin_o, mine[1], local_sems.at[1]),
+    ]
+    for made in own_copies:
+        made.start()
+    for k in (1, 2, 3):
+        l, device = level(4 - k)
+        there = place(l)
+        wire.recv(there[0], z2 + 2 * (k - 1), device)
+        wire.recv(there[1], z2 + 2 * (k - 1) + 1, device)
+    for made in own_copies:
+        made.wait()
+    last = wire.new(2)
+    wire.send(out_q.at[:, cols_q[0]], out_q.at[:, cols_q[0]], last, net.sibling())
+    wire.send(out_o.at[:, cols_o[0]], out_o.at[:, cols_o[0]], last + 1, net.sibling())
+    wire.recv(out_q.at[:, cols_q[1]], last, net.sibling())
+    wire.recv(out_o.at[:, cols_o[1]], last + 1, net.sibling())
+    wire.drain()
+
+
+def scatter_weights(dq, do, scale):
+    keys = 4 * AG_KEYS + 4 + 14 + 6 + 2
+    return pl.pallas_call(
+        functools.partial(weight_scatter_kernel, scale),
+        out_shape=(
+            jax.ShapeDtypeStruct((64, 1536), F32),
+            jax.ShapeDtypeStruct((32, 2048), F32),
+        ),
+        in_specs=[pl.BlockSpec(memory_space=pltpu.VMEM)] * 2,
+        out_specs=[pl.BlockSpec(memory_space=pltpu.VMEM)] * 2,
+        scratch_shapes=[
+            pltpu.VMEM((2048, 768), BF16),
+            pltpu.VMEM((1024, 1024), BF16),
+            pltpu.VMEM((2048, 768), BF16),
+            pltpu.VMEM((1024, 1024), BF16),
+            pltpu.VMEM((2, 4, 16, 768), BF16),
+            pltpu.VMEM((2, 4, 32, 256), BF16),
+            pltpu.VMEM((7, 16, 768), BF16),
+            pltpu.VMEM((7, 32, 256), BF16),
+            pltpu.VMEM((2, 4, 16, 768), F32),
+            pltpu.VMEM((2, 4, 32, 256), F32),
+            pltpu.VMEM((16, 768), F32),
+            pltpu.VMEM((32, 256), F32),
+            pltpu.SemaphoreType.DMA((keys,)),
+            pltpu.SemaphoreType.DMA((keys,)),
+            pltpu.SemaphoreType.DMA((2,)),
+            *scatter_scratch(32, 768),
+            *scatter_scratch(32, 512),
+            *scatter_scratch(32, 768),
+            *scatter_scratch(32, 512),
+        ],
+        compiler_params=pltpu.CompilerParams(
+            collective_id=3, has_side_effects=True, vmem_limit_bytes=VMEM_BYTES
+        ),
+        name="scatter_weights",
+    )(dq, do)
 
 
 def tables(positions, head_size):
@@ -49,10 +732,7 @@
     grad_output = cotangent[0]
     tok_count = inputs.shape[0]
     shard_index = lax.axis_index("shard")
-    qkv_full, out_full = (
-        lax.all_gather(qkv_weight, "shard", axis=0, tiled=True),
-        lax.all_gather(out_weight, "shard", axis=0, tiled=True),
-    )
+    qkv_full, out_full = gather_weights(qkv_weight, out_weight)
     positions = shard_index * tok_count + jnp.arange(tok_count, dtype=jnp.int32)
     cosine, sine = tables(positions, HEAD_DIM)
     projected = jnp.dot(inputs, qkv_full, preferred_element_type=jnp.float32)
@@ -62,7 +742,7 @@
     ).astype(jnp.bfloat16)
     value_rows = projected[:, inner_width + kv_width :].astype(jnp.bfloat16)
     stacked = jnp.concatenate([key_rows, value_rows], axis=1)
-    gathered = lax.all_gather(stacked, "shard", axis=0, tiled=True)
+    gathered = gather_kv(stacked)
     seq_len = gathered.shape[0]
     block_len = min(512, seq_len)
     visible_blocks = (shard_index * tok_count + tok_count - 1) // block_len + 1
@@ -127,17 +807,9 @@
     grad_attended = lax.dot_general(
         grad_output, out_full, (((1,), (1,)), ((), ())), preferred_element_type=jnp.float32
     ).astype(jnp.bfloat16)
-    out_share = lax.psum_scatter(
-        lax.dot_general(
-            attended_values,
-            grad_output,
-            (((0,), (0,)), ((), ())),
-            preferred_element_type=jnp.float32,
-        ).astype(jnp.bfloat16),
-        "shard",
-        scatter_dimension=0,
-        tiled=True,
-    ).astype(jnp.float32)
+    out_term = lax.dot_general(
+        attended_values, grad_output, (((0,), (0,)), ((), ())), preferred_element_type=jnp.float32
+    ).astype(jnp.bfloat16)
     gradient_grouped_heads = grad_attended.reshape(tok_count, KV_HEADS, groups, HEAD_DIM)
     attn_grouped = attended_values.reshape(tok_count, KV_HEADS, groups, HEAD_DIM)
     row_dots = jnp.einsum(
@@ -188,9 +860,7 @@
     grad_query_sum, key_terms = lax.fori_loop(
         0, visible_blocks, backward_pass, (empty_out, empty_terms)
     )
-    kv_grad = lax.psum_scatter(
-        key_terms.astype(jnp.bfloat16), "shard", scatter_dimension=0, tiled=True
-    ).astype(jnp.float32)
+    kv_grad = scatter_kv(key_terms.astype(jnp.bfloat16))
     query_gradient = rotate(
         grad_query_sum.reshape(tok_count, inner_width) * logit_scale, cosine, -sine, HEADS
     ).astype(jnp.bfloat16)
@@ -200,17 +870,12 @@
     tokens_grad = lax.dot_general(
         grad_proj, qkv_full, (((1,), (1,)), ((), ())), preferred_element_type=jnp.float32
     ).astype(jnp.bfloat16)
-    qkv_share = lax.psum_scatter(
-        lax.dot_general(
-            inputs, grad_proj, (((0,), (0,)), ((), ())), preferred_element_type=jnp.float32
-        ).astype(jnp.bfloat16),
-        "shard",
-        scatter_dimension=0,
-        tiled=True,
-    ).astype(jnp.float32)
-    qkv_total, out_total = lax.psum((qkv_share, out_share), "rep")
+    qkv_term = lax.dot_general(
+        inputs, grad_proj, (((0,), (0,)), ((), ())), preferred_element_type=jnp.float32
+    ).astype(jnp.bfloat16)
     norm_factor = 1.0 / math.sqrt(lax.axis_size("rep") * seq_len)
-    return (block_output[None], tokens_grad[None], qkv_total * norm_factor, out_total * norm_factor)
+    qkv_grad, out_grad = scatter_weights(qkv_term, out_term, norm_factor)
+    return (block_output[None], tokens_grad[None], qkv_grad, out_grad)
 
 
 def solution(mesh):

time: 1280 us -> 323 us (0.25)
  waiting for transfers between devices: 1140 us -> 0 us
  Pallas kernels: 0 us -> 270 us
  blocking collectives: 57.5 us -> 0 us
  between operations: 14.4 us -> 0.94 us
    unnamed x8 -> x0, waiting for transfers between devices: 575 us -> none
    all_gather x3 -> x0, waiting for transfers between devices: 345 us -> none  [the longest x1 138 us: body(): lax.all_gather(qkv_weight, 'shard', axis=0, tiled=True)]
    pallas_call x0 -> x4, Pallas kernels: none -> 270 us  [the longest x1 118 us: scatter_kv(): pl.pallas_call(kv_scatter_kernel, out_shape=jax.ShapeDtypeStruct((128, 51...]
    reduce_scatter x1 -> x0, waiting for transfers between devices: 216 us -> none  [body(): lax.psum_scatter(lax.dot_general(attended_values, grad_output, (((0,), (0...]
    psum x1 -> x0, blocking collectives: 57.5 us -> none  [body(): qkv_total, out_total = lax.psum((qkv_share, out_share), 'rep')]
    unnamed x13 -> x10, local copies, waits for them, and re-layouts: 24.1 us -> 10.3 us
  transfers between devices with their start and end apart: 6 -> 0, of which waited for: 6 -> 0; matrix products, arithmetic and copies ran while one was open for 3% -> 0% of each run, Pallas kernels for 0% -> 0%
where the time goes in v1:
time: 323 us; the launch traced here: 322 us
  Pallas kernels  270 us (84%)
  matrix products  29 us (9%)
  local copies, waits for them, and re-layouts  19.5 us (6%)
    pallas_call x1, Pallas kernels, scatter_kv(): pl.pallas_call(kv_scatter_kernel, out_shape=jax.ShapeDtypeStruct((128, 51...  118 us
    pallas_call x1, Pallas kernels, scatter_weights(): pl.pallas_call(functools.partial(weight_scatter_kernel, scale), out_shape...  70.4 us
    pallas_call x1, Pallas kernels, gather_weights(): pl.pallas_call(weight_gather_kernel, out_shape=(jax.ShapeDtypeStruct((204...  52.3 us
    pallas_call x1, Pallas kernels, gather_kv(): pl.pallas_call(kv_gather_kernel, out_shape=jax.ShapeDtypeStruct((4096, 51...  29.7 us
    unnamed x10, local copies, waits for them, and re-layouts  10.3 us

profile of v1, /device:TPU:1, one launch (start us, length us, event | category | flops | bytes accessed | tf_op | source)
XLA Modules:
  0.0 322.2 jit_solution(8673474676430141456)
XLA Ops:
  0.6 0.0 copy-start
  0.7 52.3 %gather_weights.1 = (bf16[2048,1536]{1,0:T(8,128)(2,1)}, bf16[1024,2048]{1,0:T(8,128)(2,1)}) custom-call(bf16[64,1536]{1,0:T(8,128)(2,1)} %qkv_in.1, bf16[32,2048]{1,0:T(8,128)(2,1)} %out_in.1), custom_call_target="tpu_custom_call" | custom-call | tf_op jit(solution)/shard_map/gather_weights/pallas_call | solution.py:363
  53.0 0.0 copy-done
  53.0 3.8 %convolution_bitcast_fusion.2 = f32[128,1536]{1,0:T(8,128)S(1)} fusion(bf16[2048,1536]{1,0:T(8,128)(2,1)} %get-tuple-element.139, bf16[1,128,2048]{2,1,0:T(8,128)(2,1)S(1)} %copy-done), kind=kOutput, calls=%fused_computation.53 | convolution fusion | flops 805306368 | bytes 7602176 | tf_op jit(solution)/shard_map/dot_general | solution.py:738
  56.8 0.1 copy.25
  56.9 0.1 fusion.40
  57.1 0.1 copy.26
  57.3 0.7 pad_maximum_fusion.6.kv_in
  57.9 29.7 %gather_kv.1 = bf16[4096,512]{1,0:T(8,128)(2,1)} custom-call(bf16[128,512]{1,0:T(8,128)(2,1)} %pad_maximum_fusion.6.kv_in), custom_call_target="tpu_custom_call" | custom-call | tf_op jit(solution)/shard_map/gather_kv/pallas_call | solution.py:419
  87.7 6.4 %copy.29 = bf16[4096,512]{0,1:T(8,128)(2,1)} copy(bf16[4096,512]{1,0:T(8,128)(2,1)} %gather_kv.1) | data formatting | bytes 8388608
  94.1 0.2 copy.27
  94.3 0.1 subtract_convert_fusion.1
  94.5 0.4 copy.30
  94.9 2.9 while.37
  95.0 0.1 broadcast_compare_fusion.6
  95.1 1.0 constant_dynamic-slice_fusion.5
  96.1 0.8 fusion.90
  96.9 0.9 fusion.91
  97.9 0.0 copy-start.2
  97.9 2.7 while.38
  97.9 1.1 constant_dynamic-slice_fusion.6
  99.0 0.1 broadcast_compare_fusion.7
  99.2 1.4 fusion.95
  100.6 0.0 copy-start.1
  100.6 0.0 copy-done.2
  100.6 3.6 %fusion.35 = (f32[4,4,128]{2,1,0:T(4,128)S(1)}, bf16[128,4,4,64]{0,3,2,1:T(8,128)(2,1)S(1)}, bf16[1024,128]{1,0:T(8,128)(2,1)S(1)}) fusion(f32[128,4,4,64]{0,3,2,1:T(8,128)S(1)} %get-tuple-element.142, bf16[1024,2048]{1,0:T(8,128)(2,1)} %get-tuple-element.143, bf16[1,128,2048]{2,1,0:T(8,128)(2,1)S(1)} %copy-done.2), kind=kOutput, calls=%fused_computation.60 | convolution fusion | flops 537655296 | bytes 5775360 | tf_op jit(solution)/shard_map/dot_general | solution.py:807
  104.2 0.0 copy-done.1
  104.3 1.5 fusion.33
  105.8 2.3 broadcast_in_dim.71.clone
  108.2 6.7 %while.39 = (s32[]{:T(128)}, f32[128,4,4,64]{0,3,2,1:T(8,128)S(1)}, bf16[4096,512]{1,0:T(8,128)(2,1)}, s32[]{:T(128)}, bf16[4096,512]{0,1:T(8,128)(2,1)}, /*inde...) while((s32[]{:T(128)}, f32[128,4,4,64]{0,3,2,1:T(8,128)S(1)}, ...), condition=%wide.region_7.8_spmd.clone, body=%wide.region_6.7_spmd.clone.sunk | while | flops 683082368 | bytes 26703076 | solution.py:860
  108.2 1.1 fusion.106
  109.2 0.8 fusion.107
  110.0 0.1 broadcast_compare_fusion.8
  110.2 1.4 fusion.108
  111.6 0.5 fusion.109
  112.1 0.9 fusion.110
  113.0 0.8 fusion.111
  113.8 0.2 copy.64
  114.0 0.9 constant_dynamic-update-slice_fusion.2
  114.9 117.6 %scatter_kv.1 = f32[128,512]{1,0:T(8,128)} custom-call(bf16[4096,512]{1,0:T(8,128)(2,1)} %get-tuple-element.145.terms), custom_call_target="tpu_custom_call" | custom-call | tf_op jit(solution)/shard_map/scatter_kv/pallas_call | solution.py:478
  232.5 0.9 slice.104
  233.4 0.1 copy.34
  233.5 0.9 slice.65
  234.4 0.1 copy.33
  234.6 0.1 subtract_convert_fusion
  234.7 5.8 %fusion.34 = bf16[1,128,2048]{2,1,0:T(8,128)(2,1)} fusion(bf16[2048,1536]{1,0:T(8,128)(2,1)} %get-tuple-element.139, bf16[128,256]{0,1:T(8,128)(2,1)S(1)} %copy.34, bf16[128,256]{0,1:T(8,128)(2,1)S(1)} %bitcast.245, bf16[128,1024]{0,1:T(8,128)(2,1)S(1)} %bitcast.240), kind=kOutput, calls=%fused_computation.57 | convolution fusion | flops 806748160 | bytes 7208960 | tf_op jit(solution)/shard_map/dot_general | solution.py:870
  240.5 4.5 %fusion.32.dq = bf16[2048,1536]{1,0:T(8,128)(2,1)} fusion(bf16[1,128,2048]{2,1,0:T(8,128)(2,1)S(1)} %copy-done, bf16[128,256]{0,1:T(8,128)(2,1)S(1)} %copy.34, bf16[128,256]{0,1:T(8,128)(2,1)S(1)} %bitcast.246, bf16[128,1024]{0,1:T(8,128)(2,1)S(1)} %bitcast.241), kind=kOutput, calls=%fused_computation.51 | convolution fusion | flops 809631744 | bytes 7208960 | tf_op jit(solution)/shard_map/dot_general | solution.py:873
  245.0 3.3 %convolution_convert_fusion.1.do = bf16[1024,2048]{1,0:T(8,128)(2,1)} fusion(bf16[128,1024]{0,1:T(8,128)(2,1)S(1)} %bitcast.238, bf16[1,128,2048]{2,1,0:T(8,128)(2,1)S(1)} %copy-done.2), kind=kOutput, calls=%fused_computation.52 | convolution fusion | flops 538968064 | bytes 4980736 | tf_op jit(solution)/shard_map/dot_general | solution.py:810
  248.3 70.4 %scatter_weights.1 = (f32[64,1536]{1,0:T(8,128)}, f32[32,2048]{1,0:T(8,128)}) custom-call(bf16[2048,1536]{1,0:T(8,128)(2,1)} %fusion.32.dq, bf16[1024,2048]{1,0:T(8,128)(2,1)} %convolution_convert_fusion.1.do), custom_call_target="tpu_custom_call" | custom-call | tf_op jit(solution)/shard_map/scatter_weights/pallas_call | solution.py:664
  318.8 1.8 copy.92
  320.5 1.7 copy.93
  (27 shorter events, 0.4 us)
Async XLA Ops:
  0.6 52.4 %copy-start = (bf16[1,128,2048]{2,1,0:T(8,128)(2,1)S(1)}, bf16[1,128,2048]{2,1,0:T(8,128)(2,1)}, u32[]{:S(2)}) copy-start(bf16[1,128,2048]{2,1,0:T(8,128)(2,1)} %param.10) | copy-start | bytes 1572868
  97.9 2.8 copy-start.2
  100.6 3.6 %copy-start.1 = (bf16[1024,2048]{1,0:T(8,128)(2,1)S(1)}, bf16[1024,2048]{1,0:T(8,128)(2,1)}, u32[]{:S(2)}) copy-start(bf16[1024,2048]{1,0:T(8,128)(2,1)} %get-tuple-element.143) | copy-start | bytes 12582916

commit v2 on v1

--- a/solution.py
+++ b/solution.py
@@ -697,6 +697,152 @@
     )(dq, do)
 
 
+BLOCK = 512
+
+
+def spread_heads(rows_t, padded, natural):
+    padded[...] = jnp.zeros_like(padded)
+    for g in range(4):
+        for k in range(4):
+            head = 4 * g + k
+            padded[g, g * 64 : g * 64 + 64, k * 128 : k * 128 + 128] = rows_t[head * 64 : head * 64 + 64]
+        natural[g * 512 : g * 512 + 512] = padded[g].T
+
+
+def attention_kernel(
+    shard_of,
+    q_ref,
+    do_ref,
+    kv_ref,
+    att_ref,
+    dq_ref,
+    terms_ref,
+    qt,
+    qn,
+    dot_,
+    don,
+    probs,
+    peaks,
+    peak,
+    total,
+    acc,
+    dqt,
+    dots,
+    pcat,
+    dcat,
+):
+    s = shard_of()
+    blocks = s // 4 + 1
+    spread_heads(q_ref[...].T, qt, qn)
+    spread_heads(do_ref[...].T, dot_, don)
+    peak[...] = jnp.full_like(peak, NEG_FILL)
+    total[...] = jnp.zeros_like(total)
+    acc[...] = jnp.zeros_like(acc)
+    dqt[...] = jnp.zeros_like(dqt)
+
+    def rows_of(j):
+        return pl.ds(pl.multiple_of(j * BLOCK, BLOCK), BLOCK)
+
+    def forward(j, masked):
+        keys = kv_ref[rows_of(j), 0:256]
+        values_t = kv_ref[rows_of(j), 256:512].T
+        if masked:
+            key_at = lax.broadcasted_iota(jnp.int32, (BLOCK, 512), 0) + j * BLOCK
+            query_at = lax.rem(lax.broadcasted_iota(jnp.int32, (BLOCK, 512), 1), 128) + s * 128
+            visible = key_at <= query_at
+        for g in range(4):
+            scores = jnp.dot(keys, qt[g], preferred_element_type=F32)
+            if masked:
+                scores = jnp.where(visible, scores, NEG_FILL)
+            before = peak[g]
+            now = jnp.maximum(before, jnp.max(scores, axis=0, keepdims=True))
+            fade = jnp.exp(before - now)
+            e = jnp.exp(scores - now)
+            total[g] = total[g] * fade + jnp.sum(e, axis=0, keepdims=True)
+            e = e.astype(BF16)
+            probs[g, j] = e
+            peaks[g, j] = now
+            peak[g] = now
+            acc[g] = acc[g] * fade + jnp.dot(values_t[g * 64 : g * 64 + 64], e, preferred_element_type=F32)
+
+    def forward_step(j, carry):
+        forward(j, False)
+        return carry
+
+    lax.fori_loop(0, blocks - 1, forward_step, 0)
+    forward(blocks - 1, True)
+
+    pieces = []
+    for g in range(4):
+        attended = (acc[g] / total[g]).astype(BF16)
+        grads = dot_[g, g * 64 : g * 64 + 64].astype(F32)
+        dots[g] = jnp.sum(attended.astype(F32) * grads, axis=0, keepdims=True)
+        peak[g] = peak[g] + jnp.log(total[g])
+        for k in range(4):
+            pieces.append(attended[:, k * 128 : k * 128 + 128])
+    att_ref[...] = jnp.concatenate(pieces, axis=0).T
+
+    def backward_step(j, carry):
+        keys_t = kv_ref[rows_of(j), 0:256].T
+        values = kv_ref[rows_of(j), 256:512]
+        for g in range(4):
+            p = probs[g, j].astype(F32) * jnp.exp(peaks[g, j] - peak[g])
+            grads = jnp.dot(values, dot_[g], preferred_element_type=F32)
+            ds = (p * (grads - dots[g])).astype(BF16)
+            pcat[:, g * 512 : g * 512 + 512] = p.astype(BF16)
+            dcat[:, g * 512 : g * 512 + 512] = ds
+            dqt[g] += jnp.dot(keys_t[g * 64 : g * 64 + 64], ds, preferred_element_type=F32)
+        terms_ref[rows_of(j), 0:256] = jnp.dot(dcat[...], qn[...], preferred_element_type=F32).astype(BF16)
+        terms_ref[rows_of(j), 256:512] = jnp.dot(pcat[...], don[...], preferred_element_type=F32).astype(BF16)
+        return carry
+
+    lax.fori_loop(0, blocks, backward_step, 0)
+
+    def blank_step(j, carry):
+        terms_ref[rows_of(j)] = jnp.zeros((BLOCK, 512), BF16)
+        return carry
+
+    lax.fori_loop(blocks, 8, blank_step, 0)
+    pieces = []
+    for g in range(4):
+        for k in range(4):
+            pieces.append(dqt[g, :, k * 128 : k * 128 + 128])
+    dq_ref[...] = jnp.concatenate(pieces, axis=0).T
+
+
+ATTENTION_SCRATCH = [
+    pltpu.VMEM((4, 256, 512), BF16),
+    pltpu.VMEM((2048, 256), BF16),
+    pltpu.VMEM((4, 256, 512), BF16),
+    pltpu.VMEM((2048, 256), BF16),
+    pltpu.VMEM((4, 8, BLOCK, 512), BF16),
+    pltpu.VMEM((4, 8, 1, 512), F32),
+    pltpu.VMEM((4, 1, 512), F32),
+    pltpu.VMEM((4, 1, 512), F32),
+    pltpu.VMEM((4, 64, 512), F32),
+    pltpu.VMEM((4, 64, 512), F32),
+    pltpu.VMEM((4, 1, 512), F32),
+    pltpu.VMEM((BLOCK, 2048), BF16),
+    pltpu.VMEM((BLOCK, 2048), BF16),
+]
+
+
+def attention(queries, grads, kv, shard_of=lambda: lax.axis_index("shard")):
+    return pl.pallas_call(
+        functools.partial(attention_kernel, shard_of),
+        out_shape=(
+            jax.ShapeDtypeStruct((128, 1024), BF16),
+            jax.ShapeDtypeStruct((128, 1024), F32),
+            jax.ShapeDtypeStruct((4096, 512), BF16),
+        ),
+        in_specs=[pl.BlockSpec(memory_space=pltpu.VMEM)] * 3,
+        out_specs=[pl.BlockSpec(memory_space=pltpu.VMEM)] * 3,
+        scratch_shapes=ATTENTION_SCRATCH,
+        compiler_params=pltpu.CompilerParams(vmem_limit_bytes=VMEM_BYTES),
+        name="attention",
+    )(queries, grads, kv)
+
+
 def tables(positions, head_size):
     halves = head_size // 2
     frequency = ROPE_BASE ** (-(jnp.arange(halves, dtype=jnp.float32) * 2.0) / head_size)
@@ -726,154 +872,38 @@
 def body(tokens, qkv_weight, out_weight, cotangent):
     inner_width = HEADS * HEAD_DIM
     kv_width = KV_HEADS * HEAD_DIM
-    groups = HEADS // KV_HEADS
     logit_scale = HEAD_DIM ** (-0.5)
     inputs = tokens[0]
     grad_output = cotangent[0]
     tok_count = inputs.shape[0]
-    shard_index = lax.axis_index("shard")
     qkv_full, out_full = gather_weights(qkv_weight, out_weight)
-    positions = shard_index * tok_count + jnp.arange(tok_count, dtype=jnp.int32)
+    positions = lax.axis_index("shard") * tok_count + jnp.arange(tok_count, dtype=jnp.int32)
     cosine, sine = tables(positions, HEAD_DIM)
-    projected = jnp.dot(inputs, qkv_full, preferred_element_type=jnp.float32)
-    queries = rotate(projected[:, :inner_width], cosine, sine, HEADS).astype(jnp.bfloat16)
-    key_rows = rotate(
-        projected[:, inner_width : inner_width + kv_width], cosine, sine, KV_HEADS
-    ).astype(jnp.bfloat16)
-    value_rows = projected[:, inner_width + kv_width :].astype(jnp.bfloat16)
-    stacked = jnp.concatenate([key_rows, value_rows], axis=1)
-    gathered = gather_kv(stacked)
-    seq_len = gathered.shape[0]
-    block_len = min(512, seq_len)
-    visible_blocks = (shard_index * tok_count + tok_count - 1) // block_len + 1
-    grouped_heads = queries.reshape(tok_count, KV_HEADS, groups, HEAD_DIM)
-
-    def key_block(current_block_index):
-        block_rows = lax.dynamic_slice_in_dim(
-            gathered, current_block_index * block_len, block_len, 0
-        )
-        key_portion = block_rows[:, :kv_width].reshape(block_len, KV_HEADS, HEAD_DIM)
-        value_portion = block_rows[:, kv_width:].reshape(block_len, KV_HEADS, HEAD_DIM)
-        return (key_portion, value_portion)
-
-    def block_scores(current_block_index, key_portion):
-        attention_logits = (
-            jnp.einsum(
-                "nifc,zic->ifnz", grouped_heads, key_portion, preferred_element_type=jnp.float32
-            )
-            * logit_scale
-        )
-        key_pos = current_block_index * block_len + jnp.arange(block_len, dtype=jnp.int32)
-        visible = key_pos[None, :] <= positions[:, None]
-        return (attention_logits, visible)
-
-    def first_pass(current_block_index, carried):
-        running, summed = carried
-        key_portion, value_portion = key_block(current_block_index)
-        attention_logits, visible = block_scores(current_block_index, key_portion)
-        row_peak = jnp.maximum(
-            running, jnp.max(jnp.where(visible, attention_logits, NEG_FILL), axis=-1, keepdims=True)
-        )
-        fresh = jnp.sum(
-            jnp.where(visible, jnp.exp(attention_logits - row_peak), 0.0), axis=-1, keepdims=True
-        )
-        return (row_peak, summed * jnp.exp(running - row_peak) + fresh)
-
-    start_peak = jnp.full((KV_HEADS, groups, tok_count, 1), NEG_FILL, jnp.float32)
-    start_sum = jnp.zeros((KV_HEADS, groups, tok_count, 1), jnp.float32)
-    row_peak, summed = lax.fori_loop(0, visible_blocks, first_pass, (start_peak, start_sum))
-    log_total = row_peak + jnp.log(summed)
-
-    def second_pass(current_block_index, carried):
-        key_portion, value_portion = key_block(current_block_index)
-        attention_logits, visible = block_scores(current_block_index, key_portion)
-        attention_probabilities = jnp.where(
-            visible, jnp.exp(attention_logits - log_total), 0.0
-        ).astype(jnp.bfloat16)
-        update = jnp.einsum(
-            "ezhm,meo->hezo",
-            attention_probabilities,
-            value_portion,
-            preferred_element_type=jnp.float32,
-        )
-        return carried + update
-
-    empty_out = jnp.zeros((tok_count, KV_HEADS, groups, HEAD_DIM), jnp.float32)
-    attended_sum = lax.fori_loop(0, visible_blocks, second_pass, empty_out)
-    attended_values = attended_sum.reshape(tok_count, inner_width).astype(jnp.bfloat16)
-    block_output = jnp.dot(attended_values, out_full, preferred_element_type=jnp.float32).astype(
-        jnp.bfloat16
-    )
+    projected = jnp.dot(inputs, qkv_full, preferred_element_type=F32)
+    queries = rotate(projected[:, :inner_width], cosine, sine, HEADS).astype(BF16)
+    key_rows = rotate(projected[:, inner_width : inner_width + kv_width], cosine, sine, KV_HEADS).astype(BF16)
+    value_rows = projected[:, inner_width + kv_width :].astype(BF16)
+    kv = gather_kv(jnp.concatenate([key_rows, value_rows], axis=1))
     grad_attended = lax.dot_general(
-        grad_output, out_full, (((1,), (1,)), ((), ())), preferred_element_type=jnp.float32
-    ).astype(jnp.bfloat16)
+        grad_output, out_full, (((1,), (1,)), ((), ())), preferred_element_type=F32
+    ).astype(BF16)
+    attended, query_sum, kv_terms = attention(queries * BF16(logit_scale), grad_attended, kv)
+    block_output = jnp.dot(attended, out_full, preferred_element_type=F32).astype(BF16)
     out_term = lax.dot_general(
-        attended_values, grad_output, (((0,), (0,)), ((), ())), preferred_element_type=jnp.float32
-    ).astype(jnp.bfloat16)
-    gradient_grouped_heads = grad_attended.reshape(tok_count, KV_HEADS, groups, HEAD_DIM)
-    attn_grouped = attended_values.reshape(tok_count, KV_HEADS, groups, HEAD_DIM)
-    row_dots = jnp.einsum(
-        "tkgd,tkgd->kgt", gradient_grouped_heads, attn_grouped, preferred_element_type=jnp.float32
-    )[..., None]
-
-    def backward_pass(current_block_index, carried):
-        query_sum, term_rows = carried
-        key_portion, value_portion = key_block(current_block_index)
-        attention_logits, visible = block_scores(current_block_index, key_portion)
-        probability = jnp.where(visible, jnp.exp(attention_logits - log_total), 0.0)
-        gradient_probabilities = jnp.einsum(
-            "nifc,zic->ifnz",
-            gradient_grouped_heads,
-            value_portion,
-            preferred_element_type=jnp.float32,
-        )
-        score_gradient = (probability * (gradient_probabilities - row_dots)).astype(jnp.bfloat16)
-        attention_probabilities = probability.astype(jnp.bfloat16)
-        query_sum = query_sum + jnp.einsum(
-            "ezhm,meo->hezo", score_gradient, key_portion, preferred_element_type=jnp.float32
-        )
-        key_contribution = (
-            jnp.einsum(
-                "jmua,ujmf->ajf", score_gradient, grouped_heads, preferred_element_type=jnp.float32
-            )
-            * logit_scale
-        )
-        value_contribution = jnp.einsum(
-            "jmua,ujmf->ajf",
-            attention_probabilities,
-            gradient_grouped_heads,
-            preferred_element_type=jnp.float32,
-        )
-        block_term = jnp.concatenate(
-            [
-                key_contribution.reshape(block_len, kv_width),
-                value_contribution.reshape(block_len, kv_width),
-            ],
-            axis=1,
-        )
-        term_rows = lax.dynamic_update_slice_in_dim(
-            term_rows, block_term, current_block_index * block_len, 0
-        )
-        return (query_sum, term_rows)
-
-    empty_terms = jnp.zeros((seq_len, 2 * kv_width), jnp.float32)
-    grad_query_sum, key_terms = lax.fori_loop(
-        0, visible_blocks, backward_pass, (empty_out, empty_terms)
-    )
-    kv_grad = scatter_kv(key_terms.astype(jnp.bfloat16))
-    query_gradient = rotate(
-        grad_query_sum.reshape(tok_count, inner_width) * logit_scale, cosine, -sine, HEADS
-    ).astype(jnp.bfloat16)
-    grad_keys = rotate(kv_grad[:, :kv_width], cosine, -sine, KV_HEADS).astype(jnp.bfloat16)
-    grad_values = kv_grad[:, kv_width:].astype(jnp.bfloat16)
+        attended, grad_output, (((0,), (0,)), ((), ())), preferred_element_type=F32
+    ).astype(BF16)
+    kv_grad = scatter_kv(kv_terms)
+    query_gradient = rotate(query_sum * logit_scale, cosine, -sine, HEADS).astype(BF16)
+    grad_keys = rotate(kv_grad[:, :kv_width], cosine, -sine, KV_HEADS).astype(BF16)
+    grad_values = kv_grad[:, kv_width:].astype(BF16)
     grad_proj = jnp.concatenate([query_gradient, grad_keys, grad_values], axis=1)
     tokens_grad = lax.dot_general(
-        grad_proj, qkv_full, (((1,), (1,)), ((), ())), preferred_element_type=jnp.float32
-    ).astype(jnp.bfloat16)
+        grad_proj, qkv_full, (((1,), (1,)), ((), ())), preferred_element_type=F32
+    ).astype(BF16)
     qkv_term = lax.dot_general(
-        inputs, grad_proj, (((0,), (0,)), ((), ())), preferred_element_type=jnp.float32
-    ).astype(jnp.bfloat16)
-    norm_factor = 1.0 / math.sqrt(lax.axis_size("rep") * seq_len)
+        inputs, grad_proj, (((0,), (0,)), ((), ())), preferred_element_type=F32
+    ).astype(BF16)
+    norm_factor = 1.0 / math.sqrt(lax.axis_size("rep") * lax.axis_size("shard") * tok_count)
     qkv_grad, out_grad = scatter_weights(qkv_term, out_term, norm_factor)
     return (block_output[None], tokens_grad[None], qkv_grad, out_grad)
 

time: 323 us -> 264 us (0.82)
  Pallas kernels: 270 us -> 231 us
  local copies, waits for them, and re-layouts: 19.5 us -> 6.97 us
  matrix products: 29 us -> 23.1 us
    pallas_call x1, Pallas kernels: 118 us -> 67 us  [scatter_kv(): pl.pallas_call(kv_scatter_kernel, out_shape=jax.ShapeDtypeStruct((128, 51...]
    pallas_call x0 -> x1, Pallas kernels: none -> 11.3 us  [attention(): pl.pallas_call(functools.partial(attention_kernel, shard_of), out_shape=(...]
    dot_general x10 -> x3, matrix products: 15.1 us -> 8.15 us  [the longest x1 3.79 us: body(): jnp.dot(attended, out_full, preferred_element_type=F32).astype(BF16)]
    unnamed x10, local copies, waits for them, and re-layouts: 10.3 us -> 3.46 us
where the time goes in v2:
time: 264 us
  Pallas kernels  231 us (88%)
  matrix products  23.1 us (9%)
  local copies, waits for them, and re-layouts  6.97 us (3%)
    pallas_call x1, Pallas kernels, scatter_weights(): pl.pallas_call(functools.partial(weight_scatter_kernel, scale), out_shape...  70.3 us
    pallas_call x1, Pallas kernels, scatter_kv(): pl.pallas_call(kv_scatter_kernel, out_shape=jax.ShapeDtypeStruct((128, 51...  67 us
    pallas_call x1, Pallas kernels, gather_weights(): pl.pallas_call(weight_gather_kernel, out_shape=(jax.ShapeDtypeStruct((204...  52.3 us
    pallas_call x1, Pallas kernels, gather_kv(): pl.pallas_call(kv_gather_kernel, out_shape=jax.ShapeDtypeStruct((4096, 51...  29.7 us
    pallas_call x1, Pallas kernels, attention(): pl.pallas_call(functools.partial(attention_kernel, shard_of), out_shape=(...  11.3 us
    dot_general x1, matrix products, body(): lax.dot_general(grad_proj, qkv_full, (((1,), (1,)), ((), ())), preferred_...  5.78 us

profile of v2, /device:TPU:1, one launch (start us, length us, event | category | flops | bytes accessed | tf_op | source)
XLA Modules:
  0.0 263.9 jit_solution(3537353273821963705)
XLA Ops:
  0.6 0.0 copy-start
  0.7 0.1 fusion.8
  0.8 52.3 %gather_weights.1 = (bf16[2048,1536]{1,0:T(8,128)(2,1)}, bf16[1024,2048]{1,0:T(8,128)(2,1)}) custom-call(bf16[64,1536]{1,0:T(8,128)(2,1)} %qkv_in.1, bf16[32,2048]{1,0:T(8,128)(2,1)} %out_in.1), custom_call_target="tpu_custom_call" | custom-call | tf_op jit(solution)/shard_map/gather_weights/pallas_call | solution.py:363
  53.2 0.0 copy-start.1
  53.2 4.7 %fusion.3.do_ref = bf16[128,1024]{1,0:T(8,128)(2,1)} fusion(bf16[1024,2048]{1,0:T(8,128)(2,1)} %get-tuple-element.12, bf16[1,128,2048]{2,1,0:T(8,128)(2,1)} %param.7), kind=kOutput, calls=%fused_computation.9 | convolution fusion | flops 537001984 | bytes 4980736 | tf_op jit(solution)/shard_map/dot_general | solution.py:887
  57.9 0.0 copy-done
  57.9 0.0 copy-done.1
  57.9 1.0 convolution_bitcast_fusion
  59.0 0.2 copy.12
  59.2 0.1 subtract_convert_fusion.1
  59.3 0.9 copy.16.q_ref
  60.2 0.1 copy.14
  60.3 0.1 copy.15
  60.4 0.7 pad_maximum_fusion.4.kv_in
  61.1 29.7 %gather_kv.1.kv_ref = bf16[4096,512]{1,0:T(8,128)(2,1)} custom-call(bf16[128,512]{1,0:T(8,128)(2,1)} %pad_maximum_fusion.4.kv_in), custom_call_target="tpu_custom_call" | custom-call | tf_op jit(solution)/shard_map/gather_kv/pallas_call | solution.py:419
  90.9 11.3 %attention.1 = (bf16[128,1024]{1,0:T(8,128)(2,1)}, f32[128,1024]{1,0:T(8,128)}, bf16[4096,512]{1,0:T(8,128)(2,1)}) custom-call(bf16[128,1024]{1,0:T(8,128)(2,1)} %copy.16.q_ref, bf16[128,1024]{1,0:T(8,128)(2,1)} %fusion.3.do_ref, bf16[4096,512]{1,0:T(8,128)(2,1)} %gather_kv.1.kv_ref), custom_call_target="tpu_custom_call" | custom-call | tf_op jit(solution)/shard_map/attention/pallas_call | solution.py:831
  102.2 3.8 %fusion.1 = bf16[1,128,2048]{2,1,0:T(8,128)(2,1)} fusion(bf16[128,1024]{1,0:T(8,128)(2,1)} %get-tuple-element.13, bf16[1024,2048]{1,0:T(8,128)(2,1)} %get-tuple-element.12), kind=kOutput, calls=%fused_computation.6 | convolution fusion | flops 537133056 | bytes 4980736 | tf_op jit(solution)/shard_map/dot_general | solution.py:891
  106.0 1.1 broadcast_multiply_fusion
  107.1 0.2 copy.17
  107.3 0.1 subtract_convert_fusion
  107.4 0.0 copy-start.2
  107.4 0.0 copy-start.3
  107.4 67.0 %scatter_kv.1 = f32[128,512]{1,0:T(8,128)} custom-call(bf16[4096,512]{1,0:T(8,128)(2,1)} %get-tuple-element.15.terms), custom_call_target="tpu_custom_call" | custom-call | tf_op jit(solution)/shard_map/scatter_kv/pallas_call | solution.py:478
  174.5 0.9 slice.84
  175.4 0.9 slice.50
  176.3 0.1 copy.19
  176.4 0.1 copy.18
  176.6 5.8 %fusion.2 = bf16[1,128,2048]{2,1,0:T(8,128)(2,1)} fusion(bf16[2048,1536]{1,0:T(8,128)(2,1)} %get-tuple-element.11, bf16[128,256]{0,1:T(8,128)(2,1)S(1)} %copy.19, bf16[128,256]{0,1:T(8,128)(2,1)S(1)} %bitcast.39, bf16[128,1024]{0,1:T(8,128)(2,1)S(1)} %bitcast.34), kind=kOutput, calls=%fused_computation.7 | convolution fusion | flops 806748160 | bytes 7208960 | tf_op jit(solution)/shard_map/dot_general | solution.py:900
  182.3 0.0 copy-done.2
  182.3 0.0 copy-done.3
  182.4 3.3 %convolution_convert_fusion.1.do = bf16[1024,2048]{1,0:T(8,128)(2,1)} fusion(bf16[128,1024]{1,0:T(8,128)(2,1)S(1)} %copy-done.2, bf16[1,128,2048]{2,1,0:T(8,128)(2,1)S(1)} %copy-done.3), kind=kOutput, calls=%fused_computation.2 | convolution fusion | flops 538968064 | bytes 4980736 | tf_op jit(solution)/shard_map/dot_general | solution.py:892
  185.7 4.5 %fusion.dq = bf16[2048,1536]{1,0:T(8,128)(2,1)} fusion(bf16[1,128,2048]{2,1,0:T(8,128)(2,1)S(1)} %copy-done, bf16[128,256]{0,1:T(8,128)(2,1)S(1)} %copy.19, bf16[128,256]{0,1:T(8,128)(2,1)S(1)} %bitcast.40, bf16[128,1024]{0,1:T(8,128)(2,1)S(1)} %bitcast.35), kind=kOutput, calls=%fused_computation.1 | convolution fusion | flops 809631744 | bytes 7208960 | tf_op jit(solution)/shard_map/dot_general | solution.py:903
  190.2 70.3 %scatter_weights.1 = (f32[64,1536]{1,0:T(8,128)}, f32[32,2048]{1,0:T(8,128)}) custom-call(bf16[2048,1536]{1,0:T(8,128)(2,1)} %fusion.dq, bf16[1024,2048]{1,0:T(8,128)(2,1)} %convolution_convert_fusion.1.do), custom_call_target="tpu_custom_call" | custom-call | tf_op jit(solution)/shard_map/scatter_weights/pallas_call | solution.py:664
  260.4 1.8 copy.26
  262.2 1.7 copy.27
  (11 shorter events, 0.2 us)
Async XLA Ops:
  0.6 57.2 %copy-start = (bf16[1,128,2048]{2,1,0:T(8,128)(2,1)S(1)}, bf16[1,128,2048]{2,1,0:T(8,128)(2,1)}, u32[]{:S(2)}) copy-start(bf16[1,128,2048]{2,1,0:T(8,128)(2,1)} %param.4) | copy-start | bytes 1572868
  53.2 4.7 %copy-start.1 = (bf16[2048,1536]{1,0:T(8,128)(2,1)S(1)}, bf16[2048,1536]{1,0:T(8,128)(2,1)}, u32[]{:S(2)}) copy-start(bf16[2048,1536]{1,0:T(8,128)(2,1)} %get-tuple-element.11) | copy-start | bytes 18874372
  107.4 75.0 %copy-start.2 = (bf16[128,1024]{1,0:T(8,128)(2,1)S(1)}, bf16[128,1024]{1,0:T(8,128)(2,1)}, u32[]{:S(2)}) copy-start(bf16[128,1024]{1,0:T(8,128)(2,1)} %get-tuple-element.13) | copy-start | bytes 786436
  107.4 74.9 %copy-start.3 = (bf16[1,128,2048]{2,1,0:T(8,128)(2,1)S(1)}, bf16[1,128,2048]{2,1,0:T(8,128)(2,1)}, u32[]{:S(2)}) copy-start(bf16[1,128,2048]{2,1,0:T(8,128)(2,1)} %param.7) | copy-start | bytes 1572868

commit v3 on v0

v3 whole, which is shorter than its diff:
```python
import functools
import math

import jax
import jax.numpy as jnp
from jax import lax
from jax.experimental import pallas as pl
from jax.experimental.pallas import tpu as pltpu
from jax.sharding import PartitionSpec as P

HEADS = 16
KV_HEADS = 4
HEAD_DIM = 64

ROPE_BASE = 500000.0
NEG_FILL = -1e30
MESH = pl.DeviceIdType.MESH
BF16 = jnp.bfloat16
F32 = jnp.float32
VMEM_BYTES = 60 * 1024 * 1024


class Net:
    def __init__(self):
        self.s = lax.axis_index("shard")
        self.r = lax.axis_index("rep")
        self.zh = self.s // 16
        self.x = lax.rem(self.s // 4, 4)
        self.y = lax.rem(self.s, 4)
        self.zl = self.r // 2
        self.core = lax.rem(self.r, 2)
        self.z = self.zh * 4 + self.zl

    def at(self, h, da, db):
        dx, dy = (da, db) if h == 0 else (db, da)
        return lax.rem(self.x + (dx + 4), 4), lax.rem(self.y + (dy + 4), 4)

    def dev(self, h, da, db):
        gx, gy = self.at(h, da, db)
        return (self.zh * 16 + gx * 4 + gy, self.r)

    def sibling(self):
        return (self.s, self.zl * 2 + 1 - self.core)

    def partner(self):
        return (lax.rem(self.s + 16, 32), self.r)

    def up(self, k):
        z = lax.rem(self.z + k, 8)
        return ((z // 4) * 16 + self.x * 4 + self.y, lax.rem(z, 4) * 2 + self.core)

    def xy_neighbours(self):
        return [self.dev(0, 1, 0), self.dev(0, -1, 0), self.dev(0, 0, 1), self.dev(0, 0, -1)]


def greet(devices):
    barrier = pltpu.get_barrier_semaphore()
    for device in devices:
        pl.semaphore_signal(barrier, inc=1, device_id=device, device_id_type=MESH)
    pl.semaphore_wait(barrier, len(devices))


class Wire:
    def __init__(self, send_sems, recv_sems, canvas, device):
        self.send_sems, self.recv_sems = send_sems, recv_sems
        self.canvas, self.device = canvas, device
        self.used = 0
        self.sent = []

    def new(self, count=1):
        first = self.used
        self.used += count
        return first

    def copy(self, src, dst, key, device):
        return pltpu.make_async_remote_copy(
            src_ref=src,
            dst_ref=dst,
            send_sem=self.send_sems.at[key],
            recv_sem=self.recv_sems.at[key],
            device_id=device,
            device_id_type=MESH,
        )

    def send(self, src, dst, key, device):
        self.copy(src, dst, key, device).start()
        self.sent.append((src.shape, src.dtype, key))

    def recv(self, ref, key, device):
        self.copy(ref, ref, key, device).wait_recv()

    def drain(self):
        for (rows, cols), dtype, key in self.sent:
            ref = self.canvas[dtype == F32].at[pl.ds(0, rows), pl.ds(0, cols)]
            self.copy(ref, ref, key, self.device).wait_send()
        self.sent = []


SIDES = (1, -1)
RING = (0, 1, -1, 2)
AG_KEYS = 40


def side(d):
    return 0 if d == 1 else 1


def gather_stages(net, wire, own, piece):
    base = wire.new(AG_KEYS)

    def s1(h, d):
        return base + h * 2 + side(d)

    def s2(h, d):
        return base + 4 + h * 2 + side(d)

    def t1(h, da, d):
        return base + 8 + (h * 4 + RING.index(da)) * 2 + side(d)

    def t2(h, da, d):
        return base + 24 + (h * 4 + RING.index(da)) * 2 + side(d)

    def at(h, da, db, part=None):
        return piece(*net.at(h, da, db), h, part)

    def spread(h, da, src):
        for d in SIDES:
            wire.send(src, at(h, da, 0), t1(h, da, d), net.dev(h, 0, d))

    def pass_on(h, da):
        for d in SIDES:
            wire.recv(at(h, da, -d), t1(h, da, d), net.dev(h, 0, -d))
            part = side(d)
            wire.send(at(h, da, -d, part), at(h, da, -d, part), t2(h, da, d), net.dev(h, 0, d))

    def stage_a():
        for h in (0, 1):
            for d in SIDES:
                wire.send(own(h), at(h, 0, 0), s1(h, d), net.dev(h, d, 0))
        for h in (0, 1):
            spread(h, 0, own(h))

    def stage_b():
        for d in SIDES:
            for h in (0, 1):
                wire.recv(at(h, -d, 0), s1(h, d), net.dev(h, -d, 0))
                part = side(d)
                wire.send(at(h, -d, 0, part), at(h, -d, 0, part), s2(h, d), net.dev(h, d, 0))
        for d in SIDES:
            for h in (0, 1):
                spread(h, -d, at(h, -d, 0))

    def stage_c():
        for h in (0, 1):
            pass_on(h, 0)

    def stage_d():
        for h in (0, 1):
            for d in SIDES:
                wire.recv(at(h, 2, 0, side(d)), s2(h, d), net.dev(h, -d, 0))
            spread(h, 2, at(h, 2, 0))

    def stage_e():
        for da in (-1, 1):
            for h in (0, 1):
                pass_on(h, da)

    def stage_f():
        for h in (0, 1):
            pass_on(h, 2)

    def stage_g():
        for da in (0, -1, 1, 2):
            for h in (0, 1):
                for d in SIDES:
                    wire.recv(at(h, da, 2, side(d)), t2(h, da, d), net.dev(h, 0, -d))

    return [stage_a, stage_b, stage_c, stage_d, stage_e, stage_f, stage_g]


def scatter_scratch(rows, cols):
    return [
        pltpu.VMEM((2, 4, 2, rows // 2, cols), BF16),
        pltpu.VMEM((2, 4, 2, rows, cols), BF16),
        pltpu.VMEM((2, 4, 2, rows, cols), BF16),
        pltpu.VMEM((2, 3, rows, cols), F32),
        pltpu.VMEM((2, rows, cols), BF16),
        pltpu.VMEM((2, 2, rows // 2, cols), BF16),
        pltpu.VMEM((2, 2, rows, cols), BF16),
        pltpu.VMEM((2, 2, rows, cols), BF16),
    ]


class Scatter:
    ORDER = (2, 1, -1, 0)

    def __init__(self, net, wire, own, bufs, emit):
        self.net, self.wire, self.own, self.emit = net, wire, own, emit
        self.t2b, self.t1s, self.t1b, self.row_sum, self.s2s, self.s2b, self.s1s, self.s1b = bufs
        self.rows = self.row_sum.shape[2]
        self.half = self.rows // 2
        self.base = wire.new(AG_KEYS)

    def s1(self, h, d):
        return self.base + h * 2 + side(d)

    def s2(self, h, d):
        return self.base + 4 + h * 2 + side(d)

    def t1(self, h, i, d):
        return self.base + 8 + (h * 4 + i) * 2 + side(d)

    def t2(self, h, i, d):
        return self.base + 24 + (h * 4 + i) * 2 + side(d)

    def part(self, p):
        return pl.ds(p * self.half, self.half)

    def load(self, h, da, db, part=None):
        return self.own(*self.net.at(h, da, db), h, part)[...].astype(F32)

    def a(self, h, da):
        i, net = RING.index(da), self.net
        for d in SIDES:
            p = side(d)
            src = self.own(*net.at(h, da, 2), h, p)
            self.wire.send(src, self.t2b.at[h, i, p], self.t2(h, i, d), net.dev(h, 0, d))

    def b(self, h, da, d):
        i, p, net = RING.index(da), side(d), self.net
        self.wire.recv(self.t2b.at[h, i, p], self.t2(h, i, d), net.dev(h, 0, -d))
        added = self.load(h, da, d, p) + self.t2b[h, i, p].astype(F32)
        self.t1s[h, i, p, self.part(p)] = added.astype(BF16)
        self.t1s[h, i, p, self.part(1 - p)] = self.load(h, da, d, 1 - p).astype(BF16)
        self.wire.send(self.t1s.at[h, i, p], self.t1b.at[h, i, p], self.t1(h, i, d), net.dev(h, 0, d))

    def c(self, h, da):
        i, net = RING.index(da), self.net
        for d in SIDES:
            self.wire.recv(self.t1b.at[h, i, side(d)], self.t1(h, i, d), net.dev(h, 0, -d))
        total = self.load(h, da, 0) + self.t1b[h, i, 0].astype(F32) + self.t1b[h, i, 1].astype(F32)
        if da != 2:
            self.row_sum[h, i] = total
            return
        self.s2s[h] = total.astype(BF16)
        for d in SIDES:
            p = side(d)
            self.wire.send(self.s2s.at[h, self.part(p)], self.s2b.at[h, p], self.s2(h, d), net.dev(h, d, 0))

    def d(self, h, d):
        i, p, net = RING.index(d), side(d), self.net
        self.wire.recv(self.s2b.at[h, p], self.s2(h, d), net.dev(h, -d, 0))
        added = self.row_sum[h, i, self.part(p)] + self.s2b[h, p].astype(F32)
        self.s1s[h, p, self.part(p)] = added.astype(BF16)
        self.s1s[h, p, self.part(1 - p)] = self.row_sum[h, i, self.part(1 - p)].astype(BF16)
        self.wire.send(self.s1s.at[h, p], self.s1b.at[h, p], self.s1(h, d), net.dev(h, d, 0))

    def e(self, h):
        for d in SIDES:
            self.wire.recv(self.s1b.at[h, side(d)], self.s1(h, d), self.net.dev(h, -d, 0))
        self.emit(h, self.row_sum[h, 0] + self.s1b[h, 0].astype(F32) + self.s1b[h, 1].astype(F32))

    def all_a(self):
        for da in self.ORDER:
            for h in (0, 1):
                self.a(h, da)

    def all_b(self):
        for da in self.ORDER:
            for h in (0, 1):
                for d in SIDES:
                    self.b(h, da, d)

    def all_c(self):
        for da in self.ORDER:
            for h in (0, 1):
                self.c(h, da)

    def all_d(self):
        for h in (0, 1):
            for d in SIDES:
                self.d(h, d)

    def all_e(self):
        for h in (0, 1):
            self.e(h)


def qkv_gather_kernel(qkv_in, qkv_full, send_sems, recv_sems, local_sems):
    net = Net()
    wire = Wire(send_sems, recv_sems, (qkv_full, None), net.sibling())
    core, s = net.core, net.s
    other = 1 - net.zh
    cols = pl.ds(pl.multiple_of(core * 768, 128), 768)

    def place(group):
        def piece(gx, gy, h, part):
            row = (group * 16 + gx * 4 + gy) * 64 + h * 32
            if part is None:
                return qkv_full.at[pl.ds(pl.multiple_of(row, 16), 32), cols]
            return qkv_full.at[pl.ds(pl.multiple_of(row + part * 16, 16), 16), cols]

        return piece

    greet(net.xy_neighbours() + [net.sibling(), net.partner()])
    mine = qkv_full.at[pl.ds(pl.multiple_of(s * 64, 64), 64), cols]
    zkey = wire.new(1)
    wire.send(qkv_in.at[:, cols], mine, zkey, net.partner())
    near = gather_stages(net, wire, lambda h: qkv_in.at[pl.ds(h * 32, 32), cols], place(net.zh))
    near[0]()
    keep = pltpu.make_async_copy(qkv_in.at[:, cols], mine, local_sems.at[0])
    keep.start()
    for stage in near[1:6]:
        stage()
    far_row = pl.multiple_of(lax.rem(s + 16, 32) * 64, 64)
    wire.recv(qkv_full.at[pl.ds(far_row, 64), cols], zkey, net.partner())
    far_place = place(other)
    far = gather_stages(net, wire, lambda h: far_place(net.x, net.y, h, None), far_place)
    far[0]()
    near[6]()
    keep.wait()

    def half_of(group, which):
        columns = pl.ds(pl.multiple_of(which * 768, 128), 768)
        return qkv_full.at[pl.ds(pl.multiple_of(group * 1024, 64), 1024), columns]

    share = wire.new(2)
    wire.send(half_of(net.zh, core), half_of(net.zh, core), share, net.sibling())
    for stage in far[1:]:
        stage()
    wire.send(half_of(other, core), half_of(other, core), share + 1, net.sibling())
    wire.recv(half_of(net.zh, 1 - core), share, net.sibling())
    wire.recv(half_of(other, 1 - core), share + 1, net.sibling())
    wire.drain()


def gather_qkv(qkv_weight):
    keys = 2 * AG_KEYS + 3
    return pl.pallas_call(
        qkv_gather_kernel,
        out_shape=jax.ShapeDtypeStruct((2048, 1536), BF16),
        in_specs=[pl.BlockSpec(memory_space=pl.ANY)],
        out_specs=pl.BlockSpec(memory_space=pl.ANY),
        scratch_shapes=[
            pltpu.SemaphoreType.DMA((keys,)),
            pltpu.SemaphoreType.DMA((keys,)),
            pltpu.SemaphoreType.DMA((1,)),
        ],
        compiler_params=pltpu.CompilerParams(collective_id=0, has_side_effects=True),
        name="gather_qkv",
    )(qkv_weight)


BLOCK = 512


def spread_heads(rows_t, padded, natural):
    padded[...] = jnp.zeros_like(padded)
    for g in range(4):
        for k in range(4):
            head = 4 * g + k
            padded[g, g * 64 : g * 64 + 64, k * 128 : k * 128 + 128] = rows_t[head * 64 : head * 64 + 64]
        natural[g * 512 : g * 512 + 512] = padded[g].T


def attend_kernel(
    q_ref,
    kv_in,
    cot_ref,
    out_in,
    att_ref,
    dq_ref,
    kvg_ref,
    block_ref,
    parts_o,
    kv_ref,
    out_full,
    terms,
    qt,
    qn,
    dot_,
    don,
    probs,
    peaks,
    peak,
    total,
    acc,
    dqt,
    dots,
    att_t,
    do_sib,
    sib_o,
    sum_o,
    far_out,
    far_in,
    send_sems,
    recv_sems,
    *bufs,
):
    net = Net()
    wire = Wire(send_sems, recv_sems, (out_full, None), net.sibling())
    s, x, zh, core = net.s, net.x, net.zh, net.core
    other = 1 - zh

    def kv_place(ref, group):
        def piece(gx, gy, h, part):
            row = (group * 16 + gx * 4 + gy) * 128 + h * 64
            if part is None:
                return ref.at[pl.ds(pl.multiple_of(row, 32), 64)]
            return ref.at[pl.ds(pl.multiple_of(row + part * 32, 32), 32)]

        return piece

    def out_cols(h):
        return pl.ds(pl.multiple_of(core * 1024 + h * 512, 128), 512)

    def out_place(group):
        def piece(gx, gy, h, part):
            row = (group * 16 + gx * 4 + gy) * 32
            if part is None:
                return out_full.at[pl.ds(pl.multiple_of(row, 16), 32), out_cols(h)]
            return out_full.at[pl.ds(pl.multiple_of(row + part * 16, 16), 16), out_cols(h)]

        return piece

    def out_half(group, which):
        columns = pl.ds(pl.multiple_of(which * 1024, 128), 1024)
        return out_full.at[pl.ds(pl.multiple_of(group * 512, 32), 512), columns]

    def kv_rows(shard):
        return kv_ref.at[pl.ds(pl.multiple_of(shard * 128, 128), 128)]

    far_shard = lax.rem(s + 16, 32)
    half_cols = pl.ds(pl.multiple_of(core * 1024, 128), 1024)

    def out_rows(shard):
        return out_full.at[pl.ds(pl.multiple_of(shard * 32, 32), 32), half_cols]

    greet(net.xy_neighbours() + [net.sibling(), net.partner()])

    zkey = wire.new(2)
    wire.send(kv_in, kv_rows(s), zkey, net.partner())
    near = gather_stages(net, wire, lambda h: kv_in.at[pl.ds(h * 64, 64)], kv_place(kv_ref, zh))
    near[0]()
    kv_ref[pl.ds(pl.multiple_of(s * 128, 128), 128)] = kv_in[...]
    out_full[pl.ds(pl.multiple_of(s * 32, 32), 32), half_cols] = out_in[:, half_cols]
    peak[...] = jnp.full_like(peak, NEG_FILL)
    total[...] = jnp.zeros_like(total)
    acc[...] = jnp.zeros_like(acc)
    dqt[...] = jnp.zeros_like(dqt)
    near[1]()
    near[2]()
    spread_heads(q_ref[...].T, qt, qn)
    for stage in near[3:6]:
        stage()
    wire.recv(kv_rows(far_shard), zkey, net.partner())
    wire.send(out_in.at[:, half_cols], out_rows(s), zkey + 1, net.partner())
    far_place = kv_place(kv_ref, other)
    far = gather_stages(net, wire, lambda h: far_place(net.x, net.y, h, None), far_place)
    far[0]()
    near[6]()

    near_o = gather_stages(net, wire, lambda h: out_in.at[:, out_cols(h)], out_place(zh))
    far_op = out_place(other)
    far_o = gather_stages(net, wire, lambda h: far_op(net.x, net.y, h, None), far_op)
    share = wire.new(2)

    def rows_of(j):
        return pl.ds(pl.multiple_of(j * BLOCK, BLOCK), BLOCK)

    def forward(j, masked):
        keys = kv_ref[rows_of(j), 0:256]
        values_t = kv_ref[rows_of(j), 256:512].T
        if masked:
            key_at = lax.broadcasted_iota(jnp.int32, (BLOCK, 512), 0) + j * BLOCK
            query_at = lax.rem(lax.broadcasted_iota(jnp.int32, (BLOCK, 512), 1), 128) + s * 128
            visible = key_at <= query_at
        ahead = jnp.dot(keys, qt[0], preferred_element_type=F32)
        for g in range(4):
            scores = ahead
            if g < 3:
                ahead = jnp.dot(keys, qt[g + 1], preferred_element_type=F32)
            if masked:
                scores = jnp.where(visible, scores, NEG_FILL)
            before = peak[g]
            now = jnp.maximum(before, jnp.max(scores, axis=0, keepdims=True))
            fade = jnp.exp(before - now)
            e = jnp.exp(scores - now)
            total[g] = total[g] * fade + jnp.sum(e, axis=0, keepdims=True)
            e = e.astype(BF16)
            probs[g, j] = e
            peaks[g, j] = now
            peak[g] = now
            acc[g] = acc[g] * fade + jnp.dot(values_t[g * 64 : g * 64 + 64], e, preferred_element_type=F32)

    def in_turn(plans, i):
        for k, plan in enumerate(plans):

            @pl.when(i == k)
            def _():
                for stage in plan:
                    stage()

    def near_forward(i, carry):
        in_turn([[far[1]], [far[2]], [far[3], near_o[0]], [far[4]]], i)

        @pl.when(i < x)
        def _():
            forward(zh * 4 + i, False)

        @pl.when(i == x)
        def _():
            forward(zh * 4 + i, True)

        return carry

    lax.fori_loop(0, 4, near_forward, 0)
    far[5]()
    near_o[1]()
    far[6]()

    def recv_out():
        wire.recv(out_rows(far_shard), zkey + 1, net.partner())

    def share_near():
        wire.send(out_half(zh, core), out_half(zh, core), share, net.sibling())

    def far_forward(i, carry):
        in_turn(
            [
                [near_o[2], near_o[3]],
                [near_o[4], near_o[5], recv_out, far_o[0]],
                [near_o[6], share_near, far_o[1], far_o[2]],
                [far_o[3], far_o[4]],
            ],
            i,
        )

        @pl.when(zh == 1)
        def _():
            forward(i, False)

        return carry

    lax.fori_loop(0, 4, far_forward, 0)
    far_o[5]()
    far_o[6]()
    wire.send(out_half(other, core), out_half(other, core), share + 1, net.sibling())

    for g in range(4):
        attended = (acc[g] / total[g]).astype(BF16)
        for k in range(4):
            head = 4 * g + k
            att_t[head * 64 : head * 64 + 64] = attended[:, k * 128 : k * 128 + 128]
    core_key = wire.new(2)
    for g in (0, 1):
        rows = slice(g * 512, g * 512 + 512)
        sib_cols = pl.ds(pl.multiple_of((1 - core) * 1024, 128), 1024)
        do_sib[rows] = jnp.dot(att_t[rows], cot_ref[:, sib_cols], preferred_element_type=F32).astype(BF16)
        wire.send(do_sib.at[pl.ds(g * 512, 512)], sib_o.at[pl.ds(g * 512, 512)], core_key + g, net.sibling())
    att_ref[...] = att_t[...].T
    wire.recv(out_half(zh, 1 - core), share, net.sibling())
    wire.recv(out_half(other, 1 - core), share + 1, net.sibling())
    grad_t = lax.dot_general(
        out_full[...], cot_ref[...], (((1,), (1,)), ((), ())), preferred_element_type=F32
    ).astype(BF16)
    spread_heads(grad_t, dot_, don)
    for g in range(4):
        for k in range(4):
            head = 4 * g + k
            rows = slice(head * 64, head * 64 + 64)
            both = att_t[rows].astype(F32) * dot_[g, g * 64 : g * 64 + 64, k * 128 : k * 128 + 128].astype(F32)
            dots[g, :, k * 128 : k * 128 + 128] = jnp.sum(both, axis=0, keepdims=True)
        peak[g] = peak[g] + jnp.log(total[g])

    def out_own(group):
        def piece(gx, gy, h, part):
            row = (group * 16 + gx * 4 + gy) * 32
            if part is None:
                return sum_o.at[pl.ds(pl.multiple_of(row, 16), 32), pl.ds(h * 512, 512)]
            return sum_o.at[pl.ds(pl.multiple_of(row + part * 16, 16), 16), pl.ds(h * 512, 512)]

        return piece

    def out_emit(group):
        def emit(h, result):
            for part in (0, 1):
                parts_o[group, 2 * h + part] = result[:, part * 256 : part * 256 + 256]

        return emit

    scat_o = [Scatter(net, wire, out_own(g), bufs[16 + 8 * g : 24 + 8 * g], out_emit(g)) for g in (0, 1)]

    def add_cores(g):
        def run():
            rows = slice(g * 512, g * 512 + 512)
            wire.recv(sib_o.at[pl.ds(g * 512, 512)], core_key + g, net.sibling())
            own = jnp.dot(att_t[rows], cot_ref[:, half_cols], preferred_element_type=F32)
            sum_o[rows] = (own + sib_o[rows].astype(F32)).astype(BF16)
            scat_o[g].all_a()

        return run

    def backward(j):
        keys_t = kv_ref[rows_of(j), 0:256].T
        values = kv_ref[rows_of(j), 256:512]
        ahead = jnp.dot(values, dot_[0], preferred_element_type=F32)
        dk = dv = None
        for g in range(4):
            grads = ahead
            if g < 3:
                ahead = jnp.dot(values, dot_[g + 1], preferred_element_type=F32)
            p = probs[g, j].astype(F32) * jnp.exp(peaks[g, j] - peak[g])
            ds = (p * (grads - dots[g])).astype(BF16)
            p = p.astype(BF16)
            dqt[g] += jnp.dot(keys_t[g * 64 : g * 64 + 64], ds, preferred_element_type=F32)
            rows = slice(g * 512, g * 512 + 512)
            dk_g = jnp.dot(ds, qn[rows], preferred_element_type=F32)
            dv_g = jnp.dot(p, don[rows], preferred_element_type=F32)
            dk = dk_g if g == 0 else dk + dk_g
            dv = dv_g if g == 0 else dv + dv_g
        terms[rows_of(j), 0:256] = dk.astype(BF16)
        terms[rows_of(j), 256:512] = dv.astype(BF16)

    zback = wire.new(2)

    def emit_far(h, result):
        far_out[h] = result.astype(BF16)
        wire.send(far_out.at[h], far_in.at[h], zback + h, net.partner())

    def emit_near(h, result):
        kvg_ref[pl.ds(h * 64, 64)] = result

    scat_far = Scatter(net, wire, kv_place(terms, other), bufs[0:8], emit_far)
    scat_near = Scatter(net, wire, kv_place(terms, zh), bufs[8:16], emit_near)

    def after(scat):
        one = functools.partial

        def plan0():
            scat.a(0, 2)
            for da in scat.ORDER:
                scat.a(1, da)

        def plan1():
            scat.a(0, 1)
            for da in scat.ORDER:
                scat.b(1, da, 1)
            for d in SIDES:
                scat.b(0, 2, d)

        def plan2():
            scat.a(0, -1)
            for da in scat.ORDER:
                scat.b(1, da, -1)
            for d in SIDES:
                scat.b(0, 1, d)
            scat.c(0, 2)

        def plan3():
            scat.a(0, 0)
            for d in SIDES:
                scat.b(0, -1, d)
            scat.c(1, 2)
            scat.c(0, 1)

        return [[plan0], [plan1], [plan2], [plan3]]

    def late1(scat):
        def run():
            for d in SIDES:
                scat.b(0, 0, d)
            for da in (1, -1, 0):
                scat.c(1, da)
            scat.c(0, -1)

        return run

    def late2(scat):
        def run():
            scat.c(0, 0)
            scat.all_d()

        return run

    def block_loop(group, plans):
        def step(i, carry):
            turn = lax.rem(18 - i + 3 * ((i * (i - 1)) // 2), 4)
            j = group * 4 + lax.rem(x + turn, 4)

            @pl.when(j <= s // 4)
            def _():
                backward(j)

            @pl.when(j > s // 4)
            def _():
                terms[rows_of(j)] = jnp.zeros((BLOCK, 512), BF16)

            in_turn(plans, i)
            return carry

        lax.fori_loop(0, 4, step, 0)

    plans = after(scat_far)
    plans[1].append(add_cores(0))
    plans[2].append(add_cores(1))
    plans[3].append(scat_o[0].all_b)
    block_loop(other, plans)
    plans = after(scat_near)
    plans[0] = [late1(scat_far)] + plans[0] + [scat_o[1].all_b]
    plans[1] = [late2(scat_far)] + plans[1] + [scat_o[0].all_c]
    plans[2] = [scat_far.all_e] + plans[2] + [scat_o[1].all_c, scat_o[0].all_d]
    plans[3] = plans[3] + [scat_o[1].all_d, scat_o[0].all_e]
    block_loop(zh, plans)
    late1(scat_near)()
    for c in range(4):
        cols = slice(c * 512, c * 512 + 512)
        block_ref[:, cols] = jnp.dot(att_ref[...], out_full[:, cols], preferred_element_type=F32).astype(BF16)
    late2(scat_near)()
    for g in range(4):
        for k in range(0, 4, 2):
            head = 4 * g + k
            pair = jnp.concatenate([dqt[g, :, k * 128 : k * 128 + 128], dqt[g, :, k * 128 + 128 : k * 128 + 256]], axis=0)
            dq_ref[:, head * 64 : head * 64 + 128] = pair.T
    scat_o[1].all_e()
    scat_near.all_e()
    for h in (0, 1):
        wire.recv(far_in.at[h], zback + h, net.partner())
        kvg_ref[pl.ds(h * 64, 64)] += far_in[h].astype(F32)
    wire.drain()


def attend(queries, kv, cotangent, out_weight):
    keys = 8 * AG_KEYS + 8
    return pl.pallas_call(
        attend_kernel,
        out_shape=(
            jax.ShapeDtypeStruct((128, 1024), BF16),
            jax.ShapeDtypeStruct((128, 1024), F32),
            jax.ShapeDtypeStruct((128, 512), F32),
            jax.ShapeDtypeStruct((128, 2048), BF16),
            jax.ShapeDtypeStruct((2, 4, 32, 256), F32),
        ),
        in_specs=[pl.BlockSpec(memory_space=pltpu.VMEM)] * 4,
        out_specs=[pl.BlockSpec(memory_space=pltpu.VMEM)] * 5,
        scratch_shapes=[
            pltpu.VMEM((4096, 512), BF16),
            pltpu.VMEM((1024, 2048), BF16),
            pltpu.VMEM((4096, 512), BF16),
            pltpu.VMEM((4, 256, 512), BF16),
            pltpu.VMEM((2048, 256), BF16),
            pltpu.VMEM((4, 256, 512), BF16),
            pltpu.VMEM((2048, 256), BF16),
            pltpu.VMEM((4, 8, BLOCK, 512), BF16),
            pltpu.VMEM((4, 8, 1, 512), F32),
            pltpu.VMEM((4, 1, 512), F32),
            pltpu.VMEM((4, 1, 512), F32),
            pltpu.VMEM((4, 64, 512), F32),
            pltpu.VMEM((4, 64, 512), F32),
            pltpu.VMEM((4, 1, 512), F32),
            pltpu.VMEM((1024, 128), BF16),
            pltpu.VMEM((1024, 1024), BF16),
            pltpu.VMEM((1024, 1024), BF16),
            pltpu.VMEM((1024, 1024), BF16),
            pltpu.VMEM((2, 64, 512), BF16),
            pltpu.VMEM((2, 64, 512), BF16),
            pltpu.SemaphoreType.DMA((keys,)),
            pltpu.SemaphoreType.DMA((keys,)),
            *scatter_scratch(64, 512),
            *scatter_scratch(64, 512),
            *scatter_scratch(32, 512),
            *scatter_scratch(32, 512),
        ],
        compiler_params=pltpu.CompilerParams(
            collective_id=1, has_side_effects=True, vmem_limit_bytes=VMEM_BYTES
        ),
        name="attend",
    )(queries, kv, cotangent, out_weight)


def weight_grad_kernel(
    scale,
    x_ref,
    gp_ref,
    w_ref,
    parts_o,
    tg_ref,
    out_q,
    out_o,
    xt,
    do_sib,
    sib_q,
    sum_q,
    zs_q,
    zs_o,
    zr_q,
    zr_o,
    keep_q,
    fin_q,
    fin_o,
    send_sems,
    recv_sems,
    *bufs,
):
    net = Net()
    wire = Wire(send_sems, recv_sems, (sum_q, out_q), net.sibling())
    core = net.core
    cols_q = [pl.ds(pl.multiple_of(c * 768, 128), 768) for c in (core, 1 - core)]
    cols_o = [pl.ds(pl.multiple_of(c * 1024, 128), 1024) for c in (core, 1 - core)]
    greet(net.xy_neighbours() + [net.sibling()] + [net.up(k) for k in range(1, 8)])

    z1 = wire.new(14)

    def z_send(k, staged, slots, key):
        target = lax.rem(net.z + k, 8)
        wire.send(staged.at[target // 4, lax.rem(target, 4)], slots.at[k - 1], key + k - 1, net.up(k))

    for g in (0, 1):
        for l in range(4):
            zs_o[g, l] = parts_o[g, l].astype(BF16)
    for k in range(1, 8):
        z_send(k, zs_o, zr_o, z1)

    xt[...] = x_ref[...].T
    ckey = wire.new(2)

    def product(rows, cols):
        return jnp.dot(xt[rows], gp_ref[:, cols], preferred_element_type=F32)

    def make_sibling(g):
        def step(i, carry):
            rows = pl.ds(pl.multiple_of(g * 1024 + i * 256, 256), 256)
            do_sib[rows] = product(rows, cols_q[1]).astype(BF16)
            return carry

        lax.fori_loop(0, 4, step, 0)
        rows = pl.ds(g * 1024, 1024)
        wire.send(do_sib.at[rows], sib_q.at[rows], ckey + g, net.sibling())

    def add_cores(g):
        wire.recv(sib_q.at[pl.ds(g * 1024, 1024)], ckey + g, net.sibling())

        def step(i, carry):
            rows = pl.ds(pl.multiple_of(g * 1024 + i * 256, 256), 256)
            sum_q[rows] = (product(rows, cols_q[0]) + sib_q[rows].astype(F32)).astype(BF16)
            return carry

        lax.fori_loop(0, 4, step, 0)

    def own_q(g):
        def piece(gx, gy, h, part):
            row = (g * 16 + gx * 4 + gy) * 64 + h * 32
            if part is None:
                return sum_q.at[pl.ds(pl.multiple_of(row, 16), 32)]
            return sum_q.at[pl.ds(pl.multiple_of(row + part * 16, 16), 16)]

        return piece

    def emit_q(g):
        def emit(h, result):
            for part in (0, 1):
                rows = result[part * 16 : part * 16 + 16]
                keep_q[g, 2 * h + part] = rows
                zs_q[g, 2 * h + part] = rows.astype(BF16)

        return emit

    runs = [Scatter(net, wire, own_q(g), bufs[8 * g : 8 * g + 8], emit_q(g)) for g in (0, 1)]

    def tokens_grad(c):
        rows = slice(c * 512, c * 512 + 512)
        tg_ref[:, rows] = lax.dot_general(
            gp_ref[...], w_ref[rows], (((1,), (1,)), ((), ())), preferred_element_type=F32
        ).astype(BF16)

    make_sibling(0)
    make_sibling(1)
    add_cores(0)
    runs[0].all_a()
    add_cores(1)
    runs[1].all_a()
    tokens_grad(0)
    runs[0].all_b()
    runs[1].all_b()
    tokens_grad(1)
    runs[0].all_c()
    runs[1].all_c()
    tokens_grad(2)
    runs[0].all_d()
    runs[1].all_d()
    tokens_grad(3)
    runs[0].all_e()
    runs[1].all_e()

    z1q = z1 + 7
    for k in range(1, 8):
        z_send(k, zs_q, zr_q, z1q)

    def place(l):
        return (
            out_q.at[pl.ds(pl.multiple_of(l * 16, 16), 16), cols_q[0]],
            out_o.at[:, pl.ds(pl.multiple_of(core * 1024 + l * 256, 128), 256)],
        )

    def level(k):
        l = lax.rem(net.zl + k, 4)
        return l, (net.s, l * 2 + core)

    z2 = wire.new(6)
    mine = place(net.zl)

    def z_sum(first, slots, key):
        result = first
        for k in range(1, 8):
            wire.recv(slots.at[k - 1], key + k - 1, net.up(8 - k))
            result = result + slots[k - 1].astype(F32)
        return result * scale

    def z_spread(which, ref, key):
        for k in (1, 2, 3):
            wire.send(ref, mine[which], key + k - 1, level(k)[1])

    fin_o[...] = z_sum(parts_o[net.zh, net.zl], zr_o, z1)
    z_spread(1, fin_o, z2)
    out_o[:, pl.ds(pl.multiple_of(core * 1024 + net.zl * 256, 128), 256)] = fin_o[...]
    fin_q[...] = z_sum(keep_q[net.zh, net.zl], zr_q, z1q)
    z_spread(0, fin_q, z2 + 3)
    out_q[pl.ds(pl.multiple_of(net.zl * 16, 16), 16), cols_q[0]] = fin_q[...]
    last = wire.new(2)
    for k in (1, 2, 3):
        l, device = level(4 - k)
        wire.recv(place(l)[1], z2 + k - 1, device)
    wire.send(out_o.at[:, cols_o[0]], out_o.at[:, cols_o[0]], last, net.sibling())
    for k in (1, 2, 3):
        l, device = level(4 - k)
        wire.recv(place(l)[0], z2 + 3 + k - 1, device)
    wire.send(out_q.at[:, cols_q[0]], out_q.at[:, cols_q[0]], last + 1, net.sibling())
    wire.recv(out_o.at[:, cols_o[1]], last, net.sibling())
    wire.recv(out_q.at[:, cols_q[1]], last + 1, net.sibling())
    wire.drain()


def weight_grads(inputs, grad_proj, qkv_full, parts_o, scale):
    keys = 2 * AG_KEYS + 14 + 2 + 6 + 2
    return pl.pallas_call(
        functools.partial(weight_grad_kernel, scale),
        out_shape=(
            jax.ShapeDtypeStruct((128, 2048), BF16),
            jax.ShapeDtypeStruct((64, 1536), F32),
            jax.ShapeDtypeStruct((32, 2048), F32),
        ),
        in_specs=[pl.BlockSpec(memory_space=pltpu.VMEM)] * 4,
        out_specs=[pl.BlockSpec(memory_space=pltpu.VMEM)] * 3,
        scratch_shapes=[
            pltpu.VMEM((2048, 128), BF16),
            pltpu.VMEM((2048, 768), BF16),
            pltpu.VMEM((2048, 768), BF16),
            pltpu.VMEM((2048, 768), BF16),
            pltpu.VMEM((2, 4, 16, 768), BF16),
            pltpu.VMEM((2, 4, 32, 256), BF16),
            pltpu.VMEM((7, 16, 768), BF16),
            pltpu.VMEM((7, 32, 256), BF16),
            pltpu.VMEM((2, 4, 16, 768), F32),
            pltpu.VMEM((16, 768), F32),
            pltpu.VMEM((32, 256), F32),
            pltpu.SemaphoreType.DMA((keys,)),
            pltpu.SemaphoreType.DMA((keys,)),
            *scatter_scratch(32, 768),
            *scatter_scratch(32, 768),
        ],
        compiler_params=pltpu.CompilerParams(
            collective_id=2, has_side_effects=True, vmem_limit_bytes=VMEM_BYTES
        ),
        name="weight_grads",
    )(inputs, grad_proj, qkv_full, parts_o)


def tables(positions, head_size):
    halves = head_size // 2
    frequency = ROPE_BASE ** (-(jnp.arange(halves, dtype=jnp.float32) * 2.0) / head_size)
    angles = positions.astype(jnp.float32)[:, None] * frequency[None, :]
    return (jnp.cos(angles), jnp.sin(angles))


def rotate(matrix, cos_rows, sin_rows, head_count):
    row_count = matrix.shape[0]
    head_size = matrix.shape[1] // head_count
    halves = head_size // 2
    pieces = matrix.reshape(row_count, head_count, 2, halves)
    lower_half = pieces[:, :, 0]
    upper_half = pieces[:, :, 1]
    cos_part = cos_rows[:, None, :]
    sin_part = sin_rows[:, None, :]
    turned = jnp.stack(
        [
            lower_half * cos_part - upper_half * sin_part,
            upper_half * cos_part + lower_half * sin_part,
        ],
        axis=2,
    )
    return turned.reshape(row_count, head_count * head_size)


def body(tokens, qkv_weight, out_weight, cotangent):
    inner_width = HEADS * HEAD_DIM
    kv_width = KV_HEADS * HEAD_DIM
    logit_scale = HEAD_DIM ** (-0.5)
    inputs = tokens[0]
    grad_output = cotangent[0]
    tok_count = inputs.shape[0]
    qkv_full = gather_qkv(qkv_weight)
    positions = lax.axis_index("shard") * tok_count + jnp.arange(tok_count, dtype=jnp.int32)
    cosine, sine = tables(positions, HEAD_DIM)
    projected = jnp.dot(inputs, qkv_full, preferred_element_type=F32)
    queries = rotate(projected[:, :inner_width], cosine, sine, HEADS).astype(BF16)
    key_rows = rotate(projected[:, inner_width : inner_width + kv_width], cosine, sine, KV_HEADS).astype(BF16)
    value_rows = projected[:, inner_width + kv_width :].astype(BF16)
    attended, query_sum, kv_grad, block_output, parts_o = attend(
        queries * BF16(logit_scale),
        jnp.concatenate([key_rows, value_rows], axis=1),
        grad_output,
        out_weight,
    )
    query_gradient = rotate(query_sum * logit_scale, cosine, -sine, HEADS).astype(BF16)
    grad_keys = rotate(kv_grad[:, :kv_width], cosine, -sine, KV_HEADS).astype(BF16)
    grad_values = kv_grad[:, kv_width:].astype(BF16)
    grad_proj = jnp.concatenate([query_gradient, grad_keys, grad_values], axis=1)
    norm_factor = 1.0 / math.sqrt(lax.axis_size("rep") * lax.axis_size("shard") * tok_count)
    tokens_grad, qkv_grad, out_grad = weight_grads(inputs, grad_proj, qkv_full, parts_o, norm_factor)
    return (block_output[None], tokens_grad[None], qkv_grad, out_grad)


def solution(mesh):
    return jax.shard_map(
        body,
        mesh=mesh,
        in_specs=(
            P("rep", "shard", None),
            P("shard", None),
            P("shard", None),
            P("rep", "shard", None),
        ),
        out_specs=(
            P("rep", "shard", None),
            P("rep", "shard", None),
            P("shard", None),
            P("shard", None),
        ),
        check_vma=False,
    )
```

time: 1280 us -> 222 us (0.17)
  waiting for transfers between devices: 1140 us -> 0 us
  Pallas kernels: 0 us -> 204 us
  blocking collectives: 57.5 us -> 0 us
  matrix products: 31 us -> 3.77 us
  local copies, waits for them, and re-layouts: 31.4 us -> 9.77 us
  between operations: 14.4 us -> 0.87 us
    unnamed x8 -> x0, waiting for transfers between devices: 575 us -> none
    all_gather x3 -> x0, waiting for transfers between devices: 345 us -> none  [the longest x1 138 us: body(): lax.all_gather(qkv_weight, 'shard', axis=0, tiled=True)]
    reduce_scatter x1 -> x0, waiting for transfers between devices: 216 us -> none  [body(): lax.psum_scatter(lax.dot_general(attended_values, grad_output, (((0,), (0...]
    pallas_call x0 -> x3, Pallas kernels: none -> 204 us  [the longest x1 106 us: attend(): pl.pallas_call(attend_kernel, out_shape=(jax.ShapeDtypeStruct((128, 1024)...]
    psum x1 -> x0, blocking collectives: 57.5 us -> none  [body(): qkv_total, out_total = lax.psum((qkv_share, out_share), 'rep')]
    dot_general x13 -> x1, matrix products: 31 us -> 3.77 us  [body(): projected = jnp.dot(inputs, qkv_full, preferred_element_type=F32)]
    unnamed x13 -> x8, local copies, waits for them, and re-layouts: 24.1 us -> 6.12 us
  transfers between devices with their start and end apart: 6 -> 0, of which waited for: 6 -> 0; matrix products, arithmetic and copies ran while one was open for 3% -> 0% of each run, Pallas kernels for 0% -> 0%
where the time goes in v3:
time: 222 us
  Pallas kernels  204 us (92%)
  local copies, waits for them, and re-layouts  9.77 us (4%)
  matrix products  3.77 us (2%)
  other arithmetic  2.99 us (1%)
    pallas_call x1, Pallas kernels, attend(): pl.pallas_call(attend_kernel, out_shape=(jax.ShapeDtypeStruct((128, 1024)...  106 us
    pallas_call x1, Pallas kernels, weight_grads(): pl.pallas_call(functools.partial(weight_grad_kernel, scale), out_shape=(j...  54.6 us
    pallas_call x1, Pallas kernels, gather_qkv(): pl.pallas_call(qkv_gather_kernel, out_shape=jax.ShapeDtypeStruct((2048, 1...  43.5 us
    unnamed x8, local copies, waits for them, and re-layouts  6.12 us

profile of v3, /device:TPU:1, one launch (start us, length us, event | category | flops | bytes accessed | tf_op | source)
XLA Modules:
  0.0 221.8 jit_solution(1026531342450130655)
XLA Ops:
  0.6 0.0 copy-start
  0.7 0.1 fusion
  0.8 43.5 %gather_qkv.1.w_ref = bf16[2048,1536]{1,0:T(8,128)(2,1)} custom-call(bf16[64,1536]{1,0:T(8,128)(2,1)} %qkv_in.1), custom_call_target="tpu_custom_call" | custom-call | tf_op jit(solution)/shard_map/gather_qkv/pallas_call | solution.py:339
  44.4 0.0 copy-done
  44.4 3.8 %fusion.1 = f32[128,1536]{1,0:T(8,128)S(1)} fusion(bf16[2048,1536]{1,0:T(8,128)(2,1)} %gather_qkv.1.w_ref, bf16[1,128,2048]{2,1,0:T(8,128)(2,1)S(1)} %copy-done), kind=kOutput, calls=%fused_computation.22 | convolution fusion | flops 805306368 | bytes 7602176 | tf_op jit(solution)/shard_map/dot_general | solution.py:1014
  48.2 0.2 copy.8
  48.4 0.1 subtract_convert_fusion.1
  48.6 0.9 copy.11.q_ref
  49.4 0.1 copy.9
  49.5 0.1 copy.10
  49.7 0.7 pad_maximum_fusion.2.kv_in
  50.3 106.2 %attend.1 = (bf16[128,1024]{1,0:T(8,128)(2,1)}, f32[128,1024]{1,0:T(8,128)}, f32[128,512]{1,0:T(8,128)}, bf16[128,2048]{1,0:T(8,128)(2,1)}, f32[2,4,32,256]{3,2,1,0:T(8,128)}) custom-call(bf16[128,1024]{1,0:T(8,128)(2,1)} %copy.11.q_ref, bf16[128,512]{1,0:T(8,128)(2,1)} %pad_maximum_fusion.2.kv_in, bf16[128,2048]{1,0:T(8,128)(2,1)} %bitcast.22, ...), custom_call_target="tpu_custom_call" | custom-call | tf_op jit(solution)/shard_map/attend/pallas_call | solution.py:735
  156.6 0.9 slice.84
  157.5 0.9 slice.50
  158.4 0.1 copy.13
  158.5 0.0 copy-start.1
  158.6 0.1 copy.15
  158.7 1.1 broadcast_multiply_fusion
  159.8 0.2 copy.12
  160.0 0.1 subtract_convert_fusion
  160.1 0.1 copy.14
  160.3 0.8 pad_maximum_fusion.gp_ref
  161.0 54.6 %weight_grads.1 = (bf16[128,2048]{1,0:T(8,128)(2,1)}, f32[64,1536]{1,0:T(8,128)}, f32[32,2048]{1,0:T(8,128)}) custom-call(bf16[128,2048]{1,0:T(8,128)(2,1)} %bitcast.15, bf16[128,1536]{1,0:T(8,128)(2,1)} %pad_maximum_fusion.gp_ref, bf16[2048,1536]{1,0:T(8,128)(2,1)} %gather_qkv.1.w_ref, f32[2,4,32,256]{3,2,1,0:T(8,128)} %get-tuple-element.14.parts_o), custom_call_target="tpu_custom_call" | custom-call | tf_op jit(solution)/shard_map/weight_grads/pallas_call | solution.py:945
  215.7 0.0 copy-done.1
  215.7 0.8 copy.20
  216.5 1.9 copy.21
  218.3 1.8 copy.22
  220.1 1.7 copy.23
  (11 shorter events, 0.2 us)
Async XLA Ops:
  0.6 43.7 %copy-start = (bf16[1,128,2048]{2,1,0:T(8,128)(2,1)S(1)}, bf16[1,128,2048]{2,1,0:T(8,128)(2,1)}, u32[]{:S(2)}) copy-start(bf16[1,128,2048]{2,1,0:T(8,128)(2,1)} %param.4) | copy-start | bytes 1572868
  158.5 57.1 %copy-start.1 = (bf16[128,2048]{1,0:T(8,128)(2,1)S(1)}, bf16[128,2048]{1,0:T(8,128)(2,1)}, u32[]{:S(2)}) copy-start(bf16[128,2048]{1,0:T(8,128)(2,1)} %get-tuple-element.11) | copy-start | bytes 1572868

commit v4 on v3

--- a/solution.py
+++ b/solution.py
@@ -286,69 +286,112 @@
             self.e(h)
 
 
-def qkv_gather_kernel(qkv_in, qkv_full, send_sems, recv_sems, local_sems):
+def weight_gather_kernel(qkv_in, out_in, qkv_full, out_full, send_sems, recv_sems, local_sems):
     net = Net()
-    wire = Wire(send_sems, recv_sems, (qkv_full, None), net.sibling())
+    wire = Wire(send_sems, recv_sems, (out_full, None), net.sibling())
     core, s = net.core, net.s
     other = 1 - net.zh
-    cols = pl.ds(pl.multiple_of(core * 768, 128), 768)
-
-    def place(group):
+    qcols = pl.ds(pl.multiple_of(core * 768, 128), 768)
+
+    def ocols(h):
+        return pl.ds(pl.multiple_of(core * 1024 + h * 512, 128), 512)
+
+    def qkv_piece(group):
         def piece(gx, gy, h, part):
             row = (group * 16 + gx * 4 + gy) * 64 + h * 32
             if part is None:
-                return qkv_full.at[pl.ds(pl.multiple_of(row, 16), 32), cols]
-            return qkv_full.at[pl.ds(pl.multiple_of(row + part * 16, 16), 16), cols]
+                return qkv_full.at[pl.ds(pl.multiple_of(row, 16), 32), qcols]
+            return qkv_full.at[pl.ds(pl.multiple_of(row + part * 16, 16), 16), qcols]
 
         return piece
 
+    def out_piece(group):
+        def piece(gx, gy, h, part):
+            row = (group * 16 + gx * 4 + gy) * 32
+            if part is None:
+                return out_full.at[pl.ds(pl.multiple_of(row, 16), 32), ocols(h)]
+            return out_full.at[pl.ds(pl.multiple_of(row + part * 16, 16), 16), ocols(h)]
+
+        return piece
+
     greet(net.xy_neighbours() + [net.sibling(), net.partner()])
-    mine = qkv_full.at[pl.ds(pl.multiple_of(s * 64, 64), 64), cols]
-    zkey = wire.new(1)
-    wire.send(qkv_in.at[:, cols], mine, zkey, net.partner())
-    near = gather_stages(net, wire, lambda h: qkv_in.at[pl.ds(h * 32, 32), cols], place(net.zh))
-    near[0]()
-    keep = pltpu.make_async_copy(qkv_in.at[:, cols], mine, local_sems.at[0])
-    keep.start()
-    for stage in near[1:6]:
-        stage()
-    far_row = pl.multiple_of(lax.rem(s + 16, 32) * 64, 64)
-    wire.recv(qkv_full.at[pl.ds(far_row, 64), cols], zkey, net.partner())
-    far_place = place(other)
-    far = gather_stages(net, wire, lambda h: far_place(net.x, net.y, h, None), far_place)
-    far[0]()
-    near[6]()
-    keep.wait()
-
-    def half_of(group, which):
-        columns = pl.ds(pl.multiple_of(which * 768, 128), 768)
-        return qkv_full.at[pl.ds(pl.multiple_of(group * 1024, 64), 1024), columns]
-
-    share = wire.new(2)
-    wire.send(half_of(net.zh, core), half_of(net.zh, core), share, net.sibling())
-    for stage in far[1:]:
-        stage()
-    wire.send(half_of(other, core), half_of(other, core), share + 1, net.sibling())
-    wire.recv(half_of(net.zh, 1 - core), share, net.sibling())
-    wire.recv(half_of(other, 1 - core), share + 1, net.sibling())
+
+    ohalf = pl.ds(pl.multiple_of(core * 1024, 128), 1024)
+    qrow = pl.ds(pl.multiple_of(s * 64, 64), 64)
+    orow = pl.ds(pl.multiple_of(s * 32, 32), 32)
+    zkey = wire.new(2)
+    wire.send(qkv_in.at[:, qcols], qkv_full.at[qrow, qcols], zkey, net.partner())
+    wire.send(out_in.at[:, ohalf], out_full.at[orow, ohalf], zkey + 1, net.partner())
+    own_q = gather_stages(net, wire, lambda h: qkv_in.at[pl.ds(h * 32, 32), qcols], qkv_piece(net.zh))
+    own_o = gather_stages(net, wire, lambda h: out_in.at[:, ocols(h)], out_piece(net.zh))
+    for a, b in zip(own_q[:1], own_o[:1]):
+        a()
+        b()
+    keep_q = pltpu.make_async_copy(qkv_in.at[:, qcols], qkv_full.at[qrow, qcols], local_sems.at[0])
+    keep_o = pltpu.make_async_copy(out_in.at[:, ohalf], out_full.at[orow, ohalf], local_sems.at[1])
+    keep_q.start()
+    keep_o.start()
+    for a, b in zip(own_q[1:6], own_o[1:6]):
+        a()
+        b()
+    far = lax.rem(s + 16, 32)
+    far_q = qkv_full.at[pl.ds(pl.multiple_of(far * 64, 64), 64), qcols]
+    far_o = out_full.at[pl.ds(pl.multiple_of(far * 32, 32), 32), ohalf]
+    wire.recv(far_q, zkey, net.partner())
+    wire.recv(far_o, zkey + 1, net.partner())
+    far_qp, far_op = qkv_piece(other), out_piece(other)
+    two_q = gather_stages(net, wire, lambda h: far_qp(net.x, net.y, h, None), far_qp)
+    two_o = gather_stages(net, wire, lambda h: far_op(net.x, net.y, h, None), far_op)
+    two_q[0]()
+    two_o[0]()
+    own_q[6]()
+    own_o[6]()
+    keep_q.wait()
+    keep_o.wait()
+
+    dkey = wire.new(4)
+
+    def sides_of(group, which):
+        cols = pl.ds(pl.multiple_of(which * 768, 128), 768)
+        cols_o = pl.ds(pl.multiple_of(which * 1024, 128), 1024)
+        return (
+            qkv_full.at[pl.ds(pl.multiple_of(group * 1024, 64), 1024), cols],
+            out_full.at[pl.ds(pl.multiple_of(group * 512, 32), 512), cols_o],
+        )
+
+    def share(group, key):
+        for i, ref in enumerate(sides_of(group, core)):
+            wire.send(ref, ref, key + i, net.sibling())
+
+    share(net.zh, dkey)
+    for a, b in zip(two_q[1:], two_o[1:]):
+        a()
+        b()
+    share(other, dkey + 2)
+    for group, key in ((net.zh, dkey), (other, dkey + 2)):
+        for i, ref in enumerate(sides_of(group, 1 - core)):
+            wire.recv(ref, key + i, net.sibling())
     wire.drain()
 
 
-def gather_qkv(qkv_weight):
-    keys = 2 * AG_KEYS + 3
+def gather_weights(qkv_weight, out_weight):
+    keys = 4 * AG_KEYS + 6
     return pl.pallas_call(
-        qkv_gather_kernel,
-        out_shape=jax.ShapeDtypeStruct((2048, 1536), BF16),
-        in_specs=[pl.BlockSpec(memory_space=pl.ANY)],
-        out_specs=pl.BlockSpec(memory_space=pl.ANY),
+        weight_gather_kernel,
+        out_shape=(
+            jax.ShapeDtypeStruct((2048, 1536), BF16),
+            jax.ShapeDtypeStruct((1024, 2048), BF16),
+        ),
+        in_specs=[pl.BlockSpec(memory_space=pl.ANY)] * 2,
+        out_specs=[pl.BlockSpec(memory_space=pl.ANY)] * 2,
         scratch_shapes=[
             pltpu.SemaphoreType.DMA((keys,)),
             pltpu.SemaphoreType.DMA((keys,)),
-            pltpu.SemaphoreType.DMA((1,)),
+            pltpu.SemaphoreType.DMA((2,)),
         ],
         compiler_params=pltpu.CompilerParams(collective_id=0, has_side_effects=True),
-        name="gather_qkv",
-    )(qkv_weight)
+        name="gather_weights",
+    )(qkv_weight, out_weight)
 
 
 BLOCK = 512
@@ -367,14 +410,15 @@
     q_ref,
     kv_in,
     cot_ref,
-    out_in,
-    att_ref,
-    dq_ref,
-    kvg_ref,
+    out_hbm,
+    cos_ref,
+    sin_ref,
+    gp_ref,
     block_ref,
     parts_o,
     kv_ref,
     out_full,
+    kvg_ref,
     terms,
     qt,
     qn,
@@ -395,10 +439,11 @@
     far_in,
     send_sems,
     recv_sems,
+    local_sem,
     *bufs,
 ):
     net = Net()
-    wire = Wire(send_sems, recv_sems, (out_full, None), net.sibling())
+    wire = Wire(send_sems, recv_sems, (sum_o, None), net.sibling())
     s, x, zh, core = net.s, net.x, net.zh, net.core
     other = 1 - zh
 
@@ -411,59 +456,41 @@
 
         return piece
 
-    def out_cols(h):
-        return pl.ds(pl.multiple_of(core * 1024 + h * 512, 128), 512)
-
-    def out_place(group):
-        def piece(gx, gy, h, part):
-            row = (group * 16 + gx * 4 + gy) * 32
-            if part is None:
-                return out_full.at[pl.ds(pl.multiple_of(row, 16), 32), out_cols(h)]
-            return out_full.at[pl.ds(pl.multiple_of(row + part * 16, 16), 16), out_cols(h)]
-
-        return piece
-
-    def out_half(group, which):
-        columns = pl.ds(pl.multiple_of(which * 1024, 128), 1024)
-        return out_full.at[pl.ds(pl.multiple_of(group * 512, 32), 512), columns]
-
     def kv_rows(shard):
         return kv_ref.at[pl.ds(pl.multiple_of(shard * 128, 128), 128)]
 
     far_shard = lax.rem(s + 16, 32)
     half_cols = pl.ds(pl.multiple_of(core * 1024, 128), 1024)
 
-    def out_rows(shard):
-        return out_full.at[pl.ds(pl.multiple_of(shard * 32, 32), 32), half_cols]
-
     greet(net.xy_neighbours() + [net.sibling(), net.partner()])
 
-    zkey = wire.new(2)
+    fetch = pltpu.make_async_copy(out_hbm, out_full, local_sem)
+    fetch.start()
+    zkey = wire.new(1)
     wire.send(kv_in, kv_rows(s), zkey, net.partner())
     near = gather_stages(net, wire, lambda h: kv_in.at[pl.ds(h * 64, 64)], kv_place(kv_ref, zh))
     near[0]()
     kv_ref[pl.ds(pl.multiple_of(s * 128, 128), 128)] = kv_in[...]
-    out_full[pl.ds(pl.multiple_of(s * 32, 32), 32), half_cols] = out_in[:, half_cols]
     peak[...] = jnp.full_like(peak, NEG_FILL)
     total[...] = jnp.zeros_like(total)
     acc[...] = jnp.zeros_like(acc)
     dqt[...] = jnp.zeros_like(dqt)
+    spread_heads(q_ref[...].T, qt, qn)
     near[1]()
     near[2]()
-    spread_heads(q_ref[...].T, qt, qn)
-    for stage in near[3:6]:
-        stage()
+    fetch.wait()
+    grad_t = lax.dot_general(
+        out_full[...], cot_ref[...], (((1,), (1,)), ((), ())), preferred_element_type=F32
+    ).astype(BF16)
+    near[3]()
+    near[4]()
+    spread_heads(grad_t, dot_, don)
+    near[5]()
     wire.recv(kv_rows(far_shard), zkey, net.partner())
-    wire.send(out_in.at[:, half_cols], out_rows(s), zkey + 1, net.partner())
     far_place = kv_place(kv_ref, other)
     far = gather_stages(net, wire, lambda h: far_place(net.x, net.y, h, None), far_place)
     far[0]()
     near[6]()
-
-    near_o = gather_stages(net, wire, lambda h: out_in.at[:, out_cols(h)], out_place(zh))
-    far_op = out_place(other)
-    far_o = gather_stages(net, wire, lambda h: far_op(net.x, net.y, h, None), far_op)
-    share = wire.new(2)
 
     def rows_of(j):
         return pl.ds(pl.multiple_of(j * BLOCK, BLOCK), BLOCK)
@@ -502,7 +529,7 @@
                     stage()
 
     def near_forward(i, carry):
-        in_turn([[far[1]], [far[2]], [far[3], near_o[0]], [far[4]]], i)
+        in_turn([[far[1]], [far[2]], [far[3]], [far[4]]], i)
 
         @pl.when(i < x)
         def _():
@@ -516,36 +543,15 @@
 
     lax.fori_loop(0, 4, near_forward, 0)
     far[5]()
-    near_o[1]()
     far[6]()
 
-    def recv_out():
-        wire.recv(out_rows(far_shard), zkey + 1, net.partner())
-
-    def share_near():
-        wire.send(out_half(zh, core), out_half(zh, core), share, net.sibling())
-
-    def far_forward(i, carry):
-        in_turn(
-            [
-                [near_o[2], near_o[3]],
-                [near_o[4], near_o[5], recv_out, far_o[0]],
-                [near_o[6], share_near, far_o[1], far_o[2]],
-                [far_o[3], far_o[4]],
-            ],
-            i,
-        )
-
-        @pl.when(zh == 1)
-        def _():
+    @pl.when(zh == 1)
+    def _():
+        def far_forward(i, carry):
             forward(i, False)
-
-        return carry
-
-    lax.fori_loop(0, 4, far_forward, 0)
-    far_o[5]()
-    far_o[6]()
-    wire.send(out_half(other, core), out_half(other, core), share + 1, net.sibling())
+            return carry
+
+        lax.fori_loop(0, 4, far_forward, 0)
 
     for g in range(4):
         attended = (acc[g] / total[g]).astype(BF16)
@@ -558,13 +564,6 @@
         sib_cols = pl.ds(pl.multiple_of((1 - core) * 1024, 128), 1024)
         do_sib[rows] = jnp.dot(att_t[rows], cot_ref[:, sib_cols], preferred_element_type=F32).astype(BF16)
         wire.send(do_sib.at[pl.ds(g * 512, 512)], sib_o.at[pl.ds(g * 512, 512)], core_key + g, net.sibling())
-    att_ref[...] = att_t[...].T
-    wire.recv(out_half(zh, 1 - core), share, net.sibling())
-    wire.recv(out_half(other, 1 - core), share + 1, net.sibling())
-    grad_t = lax.dot_general(
-        out_full[...], cot_ref[...], (((1,), (1,)), ((), ())), preferred_element_type=F32
-    ).astype(BF16)
-    spread_heads(grad_t, dot_, don)
     for g in range(4):
         for k in range(4):
             head = 4 * g + k
@@ -713,39 +712,52 @@
     plans[3] = plans[3] + [scat_o[1].all_d, scat_o[0].all_e]
     block_loop(zh, plans)
     late1(scat_near)()
+    attended = att_t[...].T
     for c in range(4):
         cols = slice(c * 512, c * 512 + 512)
-        block_ref[:, cols] = jnp.dot(att_ref[...], out_full[:, cols], preferred_element_type=F32).astype(BF16)
+        block_ref[:, cols] = jnp.dot(attended, out_full[:, cols], preferred_element_type=F32).astype(BF16)
     late2(scat_near)()
+    cos, sin = cos_ref[...], sin_ref[...]
+
+    def turn_back(rows_t):
+        a, b = rows_t[0:32], rows_t[32:64]
+        return jnp.concatenate([a * cos + b * sin, b * cos - a * sin], axis=0)
+
     for g in range(4):
         for k in range(0, 4, 2):
             head = 4 * g + k
-            pair = jnp.concatenate([dqt[g, :, k * 128 : k * 128 + 128], dqt[g, :, k * 128 + 128 : k * 128 + 256]], axis=0)
-            dq_ref[:, head * 64 : head * 64 + 128] = pair.T
+            pair = [turn_back(dqt[g, :, c * 128 : c * 128 + 128] * 0.125) for c in (k, k + 1)]
+            gp_ref[:, head * 64 : head * 64 + 128] = jnp.concatenate(pair, axis=0).T.astype(BF16)
     scat_o[1].all_e()
     scat_near.all_e()
     for h in (0, 1):
         wire.recv(far_in.at[h], zback + h, net.partner())
         kvg_ref[pl.ds(h * 64, 64)] += far_in[h].astype(F32)
+    for c in range(2):
+        keys_t = kvg_ref[:, c * 128 : c * 128 + 128].T
+        pair = [turn_back(keys_t[0:64]), turn_back(keys_t[64:128])]
+        gp_ref[:, 1024 + c * 128 : 1152 + c * 128] = jnp.concatenate(pair, axis=0).T.astype(BF16)
+    gp_ref[:, 1280:1536] = kvg_ref[:, 256:512].astype(BF16)
     wire.drain()
 
 
-def attend(queries, kv, cotangent, out_weight):
-    keys = 8 * AG_KEYS + 8
+def attend(queries, kv, cotangent, out_full, cos_t, sin_t):
+    keys = 6 * AG_KEYS + 5
     return pl.pallas_call(
         attend_kernel,
         out_shape=(
-            jax.ShapeDtypeStruct((128, 1024), BF16),
-            jax.ShapeDtypeStruct((128, 1024), F32),
-            jax.ShapeDtypeStruct((128, 512), F32),
+            jax.ShapeDtypeStruct((128, 1536), BF16),
             jax.ShapeDtypeStruct((128, 2048), BF16),
             jax.ShapeDtypeStruct((2, 4, 32, 256), F32),
         ),
-        in_specs=[pl.BlockSpec(memory_space=pltpu.VMEM)] * 4,
-        out_specs=[pl.BlockSpec(memory_space=pltpu.VMEM)] * 5,
+        in_specs=[pl.BlockSpec(memory_space=pltpu.VMEM)] * 3
+        + [pl.BlockSpec(memory_space=pl.ANY)]
+        + [pl.BlockSpec(memory_space=pltpu.VMEM)] * 2,
+        out_specs=[pl.BlockSpec(memory_space=pltpu.VMEM)] * 3,
         scratch_shapes=[
             pltpu.VMEM((4096, 512), BF16),
             pltpu.VMEM((1024, 2048), BF16),
+            pltpu.VMEM((128, 512), F32),
             pltpu.VMEM((4096, 512), BF16),
             pltpu.VMEM((4, 256, 512), BF16),
             pltpu.VMEM((2048, 256), BF16),
@@ -766,6 +778,7 @@
             pltpu.VMEM((2, 64, 512), BF16),
             pltpu.SemaphoreType.DMA((keys,)),
             pltpu.SemaphoreType.DMA((keys,)),
+            pltpu.SemaphoreType.DMA,
             *scatter_scratch(64, 512),
             *scatter_scratch(64, 512),
             *scatter_scratch(32, 512),
@@ -775,7 +788,7 @@
             collective_id=1, has_side_effects=True, vmem_limit_bytes=VMEM_BYTES
         ),
         name="attend",
-    )(queries, kv, cotangent, out_weight)
+    )(queries, kv, cotangent, out_full, cos_t, sin_t)
 
 
 def weight_grad_kernel(
@@ -798,12 +811,15 @@
     keep_q,
     fin_q,
     fin_o,
+    got_q,
+    got_o,
+    canvas,
     send_sems,
     recv_sems,
     *bufs,
 ):
     net = Net()
-    wire = Wire(send_sems, recv_sems, (sum_q, out_q), net.sibling())
+    wire = Wire(send_sems, recv_sems, (canvas, None), net.sibling())
     core = net.core
     cols_q = [pl.ds(pl.multiple_of(c * 768, 128), 768) for c in (core, 1 - core)]
     cols_o = [pl.ds(pl.multiple_of(c * 1024, 128), 1024) for c in (core, 1 - core)]
@@ -898,8 +914,8 @@
 
     def place(l):
         return (
-            out_q.at[pl.ds(pl.multiple_of(l * 16, 16), 16), cols_q[0]],
-            out_o.at[:, pl.ds(pl.multiple_of(core * 1024 + l * 256, 128), 256)],
+            got_q.at[pl.ds(pl.multiple_of(l * 16, 16), 16), cols_q[0]],
+            got_o.at[:, pl.ds(pl.multiple_of(core * 1024 + l * 256, 128), 256)],
         )
 
     def level(k):
@@ -914,7 +930,7 @@
         for k in range(1, 8):
             wire.recv(slots.at[k - 1], key + k - 1, net.up(8 - k))
             result = result + slots[k - 1].astype(F32)
-        return result * scale
+        return (result * scale).astype(BF16)
 
     def z_spread(which, ref, key):
         for k in (1, 2, 3):
@@ -922,21 +938,23 @@
 
     fin_o[...] = z_sum(parts_o[net.zh, net.zl], zr_o, z1)
     z_spread(1, fin_o, z2)
-    out_o[:, pl.ds(pl.multiple_of(core * 1024 + net.zl * 256, 128), 256)] = fin_o[...]
+    got_o[:, pl.ds(pl.multiple_of(core * 1024 + net.zl * 256, 128), 256)] = fin_o[...]
     fin_q[...] = z_sum(keep_q[net.zh, net.zl], zr_q, z1q)
     z_spread(0, fin_q, z2 + 3)
-    out_q[pl.ds(pl.multiple_of(net.zl * 16, 16), 16), cols_q[0]] = fin_q[...]
+    got_q[pl.ds(pl.multiple_of(net.zl * 16, 16), 16), cols_q[0]] = fin_q[...]
     last = wire.new(2)
     for k in (1, 2, 3):
         l, device = level(4 - k)
         wire.recv(place(l)[1], z2 + k - 1, device)
-    wire.send(out_o.at[:, cols_o[0]], out_o.at[:, cols_o[0]], last, net.sibling())
+    wire.send(got_o.at[:, cols_o[0]], got_o.at[:, cols_o[0]], last, net.sibling())
     for k in (1, 2, 3):
         l, device = level(4 - k)
         wire.recv(place(l)[0], z2 + 3 + k - 1, device)
-    wire.send(out_q.at[:, cols_q[0]], out_q.at[:, cols_q[0]], last + 1, net.sibling())
-    wire.recv(out_o.at[:, cols_o[1]], last, net.sibling())
-    wire.recv(out_q.at[:, cols_q[1]], last + 1, net.sibling())
+    wire.send(got_q.at[:, cols_q[0]], got_q.at[:, cols_q[0]], last + 1, net.sibling())
+    wire.recv(got_o.at[:, cols_o[1]], last, net.sibling())
+    wire.recv(got_q.at[:, cols_q[1]], last + 1, net.sibling())
+    out_o[...] = got_o[...].astype(F32)
+    out_q[...] = got_q[...].astype(F32)
     wire.drain()
 
 
@@ -961,8 +979,11 @@
             pltpu.VMEM((7, 16, 768), BF16),
             pltpu.VMEM((7, 32, 256), BF16),
             pltpu.VMEM((2, 4, 16, 768), F32),
-            pltpu.VMEM((16, 768), F32),
-            pltpu.VMEM((32, 256), F32),
+            pltpu.VMEM((16, 768), BF16),
+            pltpu.VMEM((32, 256), BF16),
+            pltpu.VMEM((64, 1536), BF16),
+            pltpu.VMEM((32, 2048), BF16),
+            pltpu.VMEM((1024, 1024), BF16),
             pltpu.SemaphoreType.DMA((keys,)),
             pltpu.SemaphoreType.DMA((keys,)),
             *scatter_scratch(32, 768),
@@ -973,6 +994,21 @@
         ),
         name="weight_grads",
     )(inputs, grad_proj, qkv_full, parts_o)
+
+
+def finish_kernel(*refs):
+    for i in range(4):
+        refs[i + 4][...] = refs[i][...]
+
+
+def finish(*results):
+    return pl.pallas_call(
+        finish_kernel,
+        out_shape=tuple(jax.ShapeDtypeStruct(r.shape, r.dtype) for r in results),
+        in_specs=[pl.BlockSpec(memory_space=pltpu.VMEM)] * 4,
+        out_specs=[pl.BlockSpec(memory_space=pltpu.VMEM)] * 4,
+        name="finish",
+    )(*results)
 
 
 def tables(positions, head_size):
@@ -1008,25 +1044,24 @@
     inputs = tokens[0]
     grad_output = cotangent[0]
     tok_count = inputs.shape[0]
-    qkv_full = gather_qkv(qkv_weight)
+    qkv_full, out_full = gather_weights(qkv_weight, out_weight)
     positions = lax.axis_index("shard") * tok_count + jnp.arange(tok_count, dtype=jnp.int32)
     cosine, sine = tables(positions, HEAD_DIM)
     projected = jnp.dot(inputs, qkv_full, preferred_element_type=F32)
     queries = rotate(projected[:, :inner_width], cosine, sine, HEADS).astype(BF16)
     key_rows = rotate(projected[:, inner_width : inner_width + kv_width], cosine, sine, KV_HEADS).astype(BF16)
     value_rows = projected[:, inner_width + kv_width :].astype(BF16)
-    attended, query_sum, kv_grad, block_output, parts_o = attend(
+    grad_proj, block_output, parts_o = attend(
         queries * BF16(logit_scale),
         jnp.concatenate([key_rows, value_rows], axis=1),
         grad_output,
-        out_weight,
+        out_full,
+        cosine.T,
+        sine.T,
     )
-    query_gradient = rotate(query_sum * logit_scale, cosine, -sine, HEADS).astype(BF16)
-    grad_keys = rotate(kv_grad[:, :kv_width], cosine, -sine, KV_HEADS).astype(BF16)
-    grad_values = kv_grad[:, kv_width:].astype(BF16)
-    grad_proj = jnp.concatenate([query_gradient, grad_keys, grad_values], axis=1)
     norm_factor = 1.0 / math.sqrt(lax.axis_size("rep") * lax.axis_size("shard") * tok_count)
     tokens_grad, qkv_grad, out_grad = weight_grads(inputs, grad_proj, qkv_full, parts_o, norm_factor)
+    block_output, tokens_grad, qkv_grad, out_grad = finish(block_output, tokens_grad, qkv_grad, out_grad)
     return (block_output[None], tokens_grad[None], qkv_grad, out_grad)
 
 

time: 222 us -> 202 us (0.910)
  Pallas kernels: 204 us -> 194 us
  local copies, waits for them, and re-layouts: 9.77 us -> 1.29 us
    pallas_call x2 -> x3, Pallas kernels: 150 us -> 130 us  [the longest x1 75.3 us: attend(): pl.pallas_call(attend_kernel, out_shape=(jax.ShapeDtypeStruct((128, 1536)...]
    pallas_call x1, Pallas kernels: 54.6 us -> 64.2 us  [weight_grads(): pl.pallas_call(functools.partial(weight_grad_kernel, scale), out_shape=(j...]
    unnamed x8 -> x0, local copies, waits for them, and re-layouts: 6.12 us -> none
where the time goes in v4:
time: 202 us
  Pallas kernels  194 us (96%)
  matrix products  3.96 us (2%)
    pallas_call x1, Pallas kernels, attend(): pl.pallas_call(attend_kernel, out_shape=(jax.ShapeDtypeStruct((128, 1536)...  75.3 us
    pallas_call x1, Pallas kernels, weight_grads(): pl.pallas_call(functools.partial(weight_grad_kernel, scale), out_shape=(j...  64.2 us
    pallas_call x1, Pallas kernels, gather_weights(): pl.pallas_call(weight_gather_kernel, out_shape=(jax.ShapeDtypeStruct((204...  52.3 us

profile of v4, /device:TPU:1, one launch (start us, length us, event | category | flops | bytes accessed | tf_op | source)
XLA Modules:
  0.0 202.2 jit_solution(1242964570165255385)
XLA Ops:
  0.7 0.8 multiply_sine_fusion
  1.4 0.1 multiply_cosine_fusion.1
  1.6 52.3 %gather_weights.1 = (bf16[2048,1536]{1,0:T(8,128)(2,1)}, bf16[1024,2048]{1,0:T(8,128)(2,1)}) custom-call(bf16[64,1536]{1,0:T(8,128)(2,1)} %qkv_in.1, bf16[32,2048]{1,0:T(8,128)(2,1)} %out_in.1), custom_call_target="tpu_custom_call" | custom-call | tf_op jit(solution)/shard_map/gather_weights/pallas_call | solution.py:379
  53.9 4.0 %convolution_bitcast_fusion = f32[128,1536]{1,0:T(8,128)S(1)} fusion(bf16[2048,1536]{1,0:T(8,128)(2,1)} %get-tuple-element.16.w_ref, bf16[1,128,2048]{2,1,0:T(8,128)(2,1)} %param.4), kind=kOutput, calls=%fused_computation | convolution fusion | flops 805306368 | bytes 7602176 | tf_op jit(solution)/shard_map/dot_general | solution.py:1050
  58.0 0.2 copy.10
  58.2 0.1 subtract_convert_fusion
  58.3 0.9 copy.13.q_ref
  59.1 0.1 copy.11
  59.3 0.1 copy.12
  59.4 0.7 pad_maximum_fusion.kv_in
  60.1 75.3 %attend.1 = (bf16[128,1536]{1,0:T(8,128)(2,1)}, bf16[128,2048]{1,0:T(8,128)(2,1)}, f32[2,4,32,256]{3,2,1,0:T(8,128)}) custom-call(bf16[128,1024]{1,0:T(8,128)(2,1)} %copy.13.q_ref, bf16[128,512]{1,0:T(8,128)(2,1)} %pad_maximum_fusion.kv_in, bf16[128,2048]{1,0:T(8,128)(2,1)} %bitcast.16, bf16[1024,2048]{1,0:T(8,128)(2,1)} %get-tuple-element.17.out_hbm, ...), custom_call_target="tpu_custom_call" | custom-call | tf_op jit(solution)/shard_map/attend/pallas_call | solution.py:746
  135.4 64.2 %weight_grads.1 = (bf16[128,2048]{1,0:T(8,128)(2,1)}, f32[64,1536]{1,0:T(8,128)}, f32[32,2048]{1,0:T(8,128)}) custom-call(bf16[128,2048]{1,0:T(8,128)(2,1)} %bitcast.13, bf16[128,1536]{1,0:T(8,128)(2,1)} %get-tuple-element.19.gp_ref, bf16[2048,1536]{1,0:T(8,128)(2,1)} %get-tuple-element.16.w_ref, f32[2,4,32,256]{3,2,1,0:T(8,128)} %get-tuple-element.20.parts_o), custom_call_target="tpu_custom_call" | custom-call | tf_op jit(solution)/shard_map/weight_grads/pallas_call | solution.py:963
  199.6 2.6 %finish.1 = (bf16[128,2048]{1,0:T(8,128)(2,1)}, bf16[128,2048]{1,0:T(8,128)(2,1)}, f32[64,1536]{1,0:T(8,128)}, f32[32,2048]{1,0:T(8,128)}) custom-call(bf16[128,2048]{1,0:T(8,128)(2,1)} %get-tuple-element.18.refs_0_, bf16[128,2048]{1,0:T(8,128)(2,1)} %get-tuple-element.21.refs_1_, f32[64,1536]{1,0:T(8,128)} %get-tuple-element.22.refs_2_, ...), custom_call_target="tpu_custom_call" | custom-call | tf_op jit(solution)/shard_map/finish/pallas_call | solution.py:1005
  (8 shorter events, 0.1 us)

commit v5 on v4

--- a/solution.py
+++ b/solution.py
@@ -17,7 +17,7 @@
 MESH = pl.DeviceIdType.MESH
 BF16 = jnp.bfloat16
 F32 = jnp.float32
-VMEM_BYTES = 60 * 1024 * 1024
+VMEM_BYTES = 62 * 1024 * 1024
 
 
 class Net:
@@ -89,11 +89,16 @@
     def recv(self, ref, key, device):
         self.copy(ref, ref, key, device).wait_recv()
 
-    def drain(self):
-        for (rows, cols), dtype, key in self.sent:
+    def taken(self):
+        sent, self.sent = self.sent, []
+        return sent
+
+    def drain(self, sent=None):
+        for shape, dtype, key in self.taken() if sent is None else sent:
+            cols = shape[1] if len(shape) == 2 else 1024 if len(shape) == 4 else 256
+            rows = math.prod(shape) // cols
             ref = self.canvas[dtype == F32].at[pl.ds(0, rows), pl.ds(0, cols)]
             self.copy(ref, ref, key, self.device).wait_send()
-        self.sent = []
 
 
 SIDES = (1, -1)
@@ -103,6 +108,12 @@
 
 def side(d):
     return 0 if d == 1 else 1
+
+
+class Stages(list):
+    def __init__(self, base, stages):
+        super().__init__(stages)
+        self.base = base
 
 
 def gather_stages(net, wire, own, piece):
@@ -175,7 +186,7 @@
                 for d in SIDES:
                     wire.recv(at(h, da, 2, side(d)), t2(h, da, d), net.dev(h, 0, -d))
 
-    return [stage_a, stage_b, stage_c, stage_d, stage_e, stage_f, stage_g]
+    return Stages(base, [stage_a, stage_b, stage_c, stage_d, stage_e, stage_f, stage_g])
 
 
 def scatter_scratch(rows, cols):
@@ -286,114 +297,6 @@
             self.e(h)
 
 
-def weight_gather_kernel(qkv_in, out_in, qkv_full, out_full, send_sems, recv_sems, local_sems):
-    net = Net()
-    wire = Wire(send_sems, recv_sems, (out_full, None), net.sibling())
-    core, s = net.core, net.s
-    other = 1 - net.zh
-    qcols = pl.ds(pl.multiple_of(core * 768, 128), 768)
-
-    def ocols(h):
-        return pl.ds(pl.multiple_of(core * 1024 + h * 512, 128), 512)
-
-    def qkv_piece(group):
-        def piece(gx, gy, h, part):
-            row = (group * 16 + gx * 4 + gy) * 64 + h * 32
-            if part is None:
-                return qkv_full.at[pl.ds(pl.multiple_of(row, 16), 32), qcols]
-            return qkv_full.at[pl.ds(pl.multiple_of(row + part * 16, 16), 16), qcols]
-
-        return piece
-
-    def out_piece(group):
-        def piece(gx, gy, h, part):
-            row = (group * 16 + gx * 4 + gy) * 32
-            if part is None:
-                return out_full.at[pl.ds(pl.multiple_of(row, 16), 32), ocols(h)]
-            return out_full.at[pl.ds(pl.multiple_of(row + part * 16, 16), 16), ocols(h)]
-
-        return piece
-
-    greet(net.xy_neighbours() + [net.sibling(), net.partner()])
-
-    ohalf = pl.ds(pl.multiple_of(core * 1024, 128), 1024)
-    qrow = pl.ds(pl.multiple_of(s * 64, 64), 64)
-    orow = pl.ds(pl.multiple_of(s * 32, 32), 32)
-    zkey = wire.new(2)
-    wire.send(qkv_in.at[:, qcols], qkv_full.at[qrow, qcols], zkey, net.partner())
-    wire.send(out_in.at[:, ohalf], out_full.at[orow, ohalf], zkey + 1, net.partner())
-    own_q = gather_stages(net, wire, lambda h: qkv_in.at[pl.ds(h * 32, 32), qcols], qkv_piece(net.zh))
-    own_o = gather_stages(net, wire, lambda h: out_in.at[:, ocols(h)], out_piece(net.zh))
-    for a, b in zip(own_q[:1], own_o[:1]):
-        a()
-        b()
-    keep_q = pltpu.make_async_copy(qkv_in.at[:, qcols], qkv_full.at[qrow, qcols], local_sems.at[0])
-    keep_o = pltpu.make_async_copy(out_in.at[:, ohalf], out_full.at[orow, ohalf], local_sems.at[1])
-    keep_q.start()
-    keep_o.start()
-    for a, b in zip(own_q[1:6], own_o[1:6]):
-        a()
-        b()
-    far = lax.rem(s + 16, 32)
-    far_q = qkv_full.at[pl.ds(pl.multiple_of(far * 64, 64), 64), qcols]
-    far_o = out_full.at[pl.ds(pl.multiple_of(far * 32, 32), 32), ohalf]
-    wire.recv(far_q, zkey, net.partner())
-    wire.recv(far_o, zkey + 1, net.partner())
-    far_qp, far_op = qkv_piece(other), out_piece(other)
-    two_q = gather_stages(net, wire, lambda h: far_qp(net.x, net.y, h, None), far_qp)
-    two_o = gather_stages(net, wire, lambda h: far_op(net.x, net.y, h, None), far_op)
-    two_q[0]()
-    two_o[0]()
-    own_q[6]()
-    own_o[6]()
-    keep_q.wait()
-    keep_o.wait()
-
-    dkey = wire.new(4)
-
-    def sides_of(group, which):
-        cols = pl.ds(pl.multiple_of(which * 768, 128), 768)
-        cols_o = pl.ds(pl.multiple_of(which * 1024, 128), 1024)
-        return (
-            qkv_full.at[pl.ds(pl.multiple_of(group * 1024, 64), 1024), cols],
-            out_full.at[pl.ds(pl.multiple_of(group * 512, 32), 512), cols_o],
-        )
-
-    def share(group, key):
-        for i, ref in enumerate(sides_of(group, core)):
-            wire.send(ref, ref, key + i, net.sibling())
-
-    share(net.zh, dkey)
-    for a, b in zip(two_q[1:], two_o[1:]):
-        a()
-        b()
-    share(other, dkey + 2)
-    for group, key in ((net.zh, dkey), (other, dkey + 2)):
-        for i, ref in enumerate(sides_of(group, 1 - core)):
-            wire.recv(ref, key + i, net.sibling())
-    wire.drain()
-
-
-def gather_weights(qkv_weight, out_weight):
-    keys = 4 * AG_KEYS + 6
-    return pl.pallas_call(
-        weight_gather_kernel,
-        out_shape=(
-            jax.ShapeDtypeStruct((2048, 1536), BF16),
-            jax.ShapeDtypeStruct((1024, 2048), BF16),
-        ),
-        in_specs=[pl.BlockSpec(memory_space=pl.ANY)] * 2,
-        out_specs=[pl.BlockSpec(memory_space=pl.ANY)] * 2,
-        scratch_shapes=[
-            pltpu.SemaphoreType.DMA((keys,)),
-            pltpu.SemaphoreType.DMA((keys,)),
-            pltpu.SemaphoreType.DMA((2,)),
-        ],
-        compiler_params=pltpu.CompilerParams(collective_id=0, has_side_effects=True),
-        name="gather_weights",
-    )(qkv_weight, out_weight)
-
-
 BLOCK = 512
 
 
@@ -407,15 +310,19 @@
 
 
 def attend_kernel(
-    q_ref,
-    kv_in,
+    x_ref,
+    qkv_in,
+    out_in,
     cot_ref,
-    out_hbm,
     cos_ref,
     sin_ref,
     gp_ref,
     block_ref,
     parts_o,
+    qkv_hbm,
+    qkv_own,
+    proj,
+    kv_in,
     kv_ref,
     out_full,
     kvg_ref,
@@ -439,7 +346,7 @@
     far_in,
     send_sems,
     recv_sems,
-    local_sem,
+    local_sems,
     *bufs,
 ):
     net = Net()
@@ -461,36 +368,146 @@
 
     far_shard = lax.rem(s + 16, 32)
     half_cols = pl.ds(pl.multiple_of(core * 1024, 128), 1024)
-
+    panels = pl.ds(core * 3, 3)
+
+    def qkv_at(which, row, count):
+        return probs.at[which, row // 512, pl.ds(pl.multiple_of(lax.rem(row, 512), 16), count)]
+
+    def qkv_place(group):
+        def piece(gx, gy, h, part):
+            row = (group * 16 + gx * 4 + gy) * 64 + h * 32
+            return qkv_at(panels, row, 32) if part is None else qkv_at(panels, row + part * 16, 16)
+
+        return piece
+
+    def qkv_half(group, which):
+        return probs.at[pl.ds(which * 3, 3), pl.ds(group * 2, 2)]
+
+    def out_cols(h):
+        return pl.ds(pl.multiple_of(core * 1024 + h * 512, 128), 512)
+
+    def out_place(group):
+        def piece(gx, gy, h, part):
+            row = (group * 16 + gx * 4 + gy) * 32
+            if part is None:
+                return out_full.at[pl.ds(pl.multiple_of(row, 16), 32), out_cols(h)]
+            return out_full.at[pl.ds(pl.multiple_of(row + part * 16, 16), 16), out_cols(h)]
+
+        return piece
+
+    def out_half(group, which):
+        columns = pl.ds(pl.multiple_of(which * 1024, 128), 1024)
+        return out_full.at[pl.ds(pl.multiple_of(group * 512, 32), 512), columns]
+
+    def out_rows(shard):
+        return out_full.at[pl.ds(pl.multiple_of(shard * 32, 32), 32), half_cols]
+
+    for p in range(6):
+        qkv_own[p] = qkv_in[:, p * 256 : p * 256 + 256]
     greet(net.xy_neighbours() + [net.sibling(), net.partner()])
 
-    fetch = pltpu.make_async_copy(out_hbm, out_full, local_sem)
-    fetch.start()
+    zq = wire.new(1)
+    wire.send(qkv_own.at[panels], qkv_at(panels, s * 64, 64), zq, net.partner())
+    near_q = gather_stages(net, wire, lambda h: qkv_own.at[panels, pl.ds(h * 32, 32)], qkv_place(zh))
+    near_q[0]()
+    probs[panels, (s * 64) // 512, pl.ds(pl.multiple_of(lax.rem(s * 64, 512), 64), 64)] = qkv_own[panels]
+    out_full[pl.ds(pl.multiple_of(s * 32, 32), 32), half_cols] = out_in[:, half_cols]
+    peak[...] = jnp.full_like(peak, NEG_FILL)
+    total[...] = jnp.zeros_like(total)
+    acc[...] = jnp.zeros_like(acc)
+    dqt[...] = jnp.zeros_like(dqt)
+    for stage in near_q[1:6]:
+        stage()
+    wire.recv(qkv_at(panels, far_shard * 64, 64), zq, net.partner())
+    zo = wire.new(1)
+    wire.send(out_in.at[:, half_cols], out_rows(s), zo, net.partner())
+    far_qp = qkv_place(other)
+    far_q = gather_stages(net, wire, lambda h: far_qp(net.x, net.y, h, None), far_qp)
+    far_q[0]()
+    near_q[6]()
+    share_q = wire.new(2)
+    wire.send(qkv_half(zh, core), qkv_half(zh, core), share_q, net.sibling())
+    for stage in far_q[1:3]:
+        stage()
+
+    def project(group, first):
+        def step(p, carry):
+            columns = pl.ds(pl.multiple_of(p * 256, 256), 256)
+            result = jnp.zeros((128, 256), F32) if first else proj[:, columns]
+            for b in (0, 1):
+                rows = pl.ds(pl.multiple_of(group * 1024 + b * 512, 512), 512)
+                result = result + jnp.dot(x_ref[:, rows], probs[p, group * 2 + b], preferred_element_type=F32)
+            proj[:, columns] = result
+            return carry
+
+        lax.fori_loop(0, 6, step, 0)
+
+    for stage in far_q[3:5]:
+        stage()
+    wire.recv(qkv_half(zh, 1 - core), share_q, net.sibling())
+    project(zh, True)
+    for stage in far_q[5:]:
+        stage()
+    wire.send(qkv_half(other, core), qkv_half(other, core), share_q + 1, net.sibling())
+    early = wire.taken()
+    near_o = gather_stages(net, wire, lambda h: out_in.at[:, out_cols(h)], out_place(zh))
+    near_o[0]()
+    wire.recv(qkv_half(other, 1 - core), share_q + 1, net.sibling())
+    keep = []
+    for p in range(6):
+        for b in range(4):
+            place = qkv_hbm.at[pl.ds(b * 512, 512), pl.ds(p * 256, 256)]
+            keep.append(pltpu.make_async_copy(probs.at[p, b], place, local_sems.at[p * 4 + b]))
+    for made in keep:
+        made.start()
+    project(other, False)
+    cos, sin = cos_ref[...], sin_ref[...]
+
+    def turn(rows_t):
+        a, b = rows_t[0:32], rows_t[32:64]
+        return [a * cos - b * sin, b * cos + a * sin]
+
+    for c in (0, 1):
+        keys_t = proj[:, 1024 + c * 128 : 1152 + c * 128].T
+        pair = turn(keys_t[0:64]) + turn(keys_t[64:128])
+        kv_in[:, c * 128 : c * 128 + 128] = jnp.concatenate(pair, axis=0).astype(BF16).T
+    kv_in[:, 256:512] = proj[:, 1280:1536].astype(BF16)
+
     zkey = wire.new(1)
     wire.send(kv_in, kv_rows(s), zkey, net.partner())
     near = gather_stages(net, wire, lambda h: kv_in.at[pl.ds(h * 64, 64)], kv_place(kv_ref, zh))
     near[0]()
+    near_o[1]()
     kv_ref[pl.ds(pl.multiple_of(s * 128, 128), 128)] = kv_in[...]
-    peak[...] = jnp.full_like(peak, NEG_FILL)
-    total[...] = jnp.zeros_like(total)
-    acc[...] = jnp.zeros_like(acc)
-    dqt[...] = jnp.zeros_like(dqt)
-    spread_heads(q_ref[...].T, qt, qn)
+    pieces = []
+    for c in range(8):
+        queries_t = proj[:, c * 128 : c * 128 + 128].T
+        pieces += turn(queries_t[0:64]) + turn(queries_t[64:128])
+    spread_heads((jnp.concatenate(pieces, axis=0).astype(BF16).astype(F32) * 0.125).astype(BF16), qt, qn)
     near[1]()
+    near_o[2]()
     near[2]()
-    fetch.wait()
-    grad_t = lax.dot_general(
-        out_full[...], cot_ref[...], (((1,), (1,)), ((), ())), preferred_element_type=F32
-    ).astype(BF16)
+    near_o[3]()
     near[3]()
     near[4]()
-    spread_heads(grad_t, dot_, don)
+    near_o[4]()
     near[5]()
+    near_o[5]()
     wire.recv(kv_rows(far_shard), zkey, net.partner())
     far_place = kv_place(kv_ref, other)
     far = gather_stages(net, wire, lambda h: far_place(net.x, net.y, h, None), far_place)
     far[0]()
+    wire.recv(out_rows(far_shard), zo, net.partner())
+    far_op = out_place(other)
+    far_o = gather_stages(net, wire, lambda h: far_op(net.x, net.y, h, None), far_op)
+    far_o[0]()
     near[6]()
+    near_o[6]()
+    share_o = wire.new(2)
+    wire.send(out_half(zh, core), out_half(zh, core), share_o, net.sibling())
+    for made in keep:
+        made.wait()
+    wire.drain(early)
 
     def rows_of(j):
         return pl.ds(pl.multiple_of(j * BLOCK, BLOCK), BLOCK)
@@ -515,7 +532,8 @@
             e = jnp.exp(scores - now)
             total[g] = total[g] * fade + jnp.sum(e, axis=0, keepdims=True)
             e = e.astype(BF16)
-            probs[g, j] = e
+            for c in (0, 1):
+                probs[4 * g + j // 2, lax.rem(j, 2) * 2 + c] = e[:, c * 256 : c * 256 + 256]
             peaks[g, j] = now
             peak[g] = now
             acc[g] = acc[g] * fade + jnp.dot(values_t[g * 64 : g * 64 + 64], e, preferred_element_type=F32)
@@ -529,7 +547,7 @@
                     stage()
 
     def near_forward(i, carry):
-        in_turn([[far[1]], [far[2]], [far[3]], [far[4]]], i)
+        in_turn([[far[1], far_o[1]], [far[2], far_o[2]], [far[3], far_o[3]], [far[4], far_o[4]]], i)
 
         @pl.when(i < x)
         def _():
@@ -543,15 +561,33 @@
 
     lax.fori_loop(0, 4, near_forward, 0)
     far[5]()
-    far[6]()
-
-    @pl.when(zh == 1)
-    def _():
-        def far_forward(i, carry):
-            forward(i, False)
-            return carry
-
-        lax.fori_loop(0, 4, far_forward, 0)
+    far_o[5]()
+
+    def landed(h, da, d):
+        key = far.base + 24 + (h * 4 + RING.index(da)) * 2 + side(d)
+        wire.recv(far_place(*net.at(h, da, 2), h, side(d)), key, net.dev(h, 0, -d))
+
+    def far_forward(i, carry):
+        for k, da in enumerate((0, 1, -1, 2)):
+
+            @pl.when(i == k)
+            def _(da=da):
+                for d in SIDES:
+                    landed(0, da, d)
+                if da == 2:
+                    for db in RING:
+                        for d in SIDES:
+                            landed(1, db, d)
+
+        @pl.when(zh == 1)
+        def _():
+            forward(lax.rem(x + lax.rem(8 + i - 3 * ((i * (i - 1)) // 2) + 4 * i, 4), 4), False)
+
+        return carry
+
+    lax.fori_loop(0, 4, far_forward, 0)
+    far_o[6]()
+    wire.send(out_half(other, core), out_half(other, core), share_o + 1, net.sibling())
 
     for g in range(4):
         attended = (acc[g] / total[g]).astype(BF16)
@@ -564,6 +600,12 @@
         sib_cols = pl.ds(pl.multiple_of((1 - core) * 1024, 128), 1024)
         do_sib[rows] = jnp.dot(att_t[rows], cot_ref[:, sib_cols], preferred_element_type=F32).astype(BF16)
         wire.send(do_sib.at[pl.ds(g * 512, 512)], sib_o.at[pl.ds(g * 512, 512)], core_key + g, net.sibling())
+    wire.recv(out_half(zh, 1 - core), share_o, net.sibling())
+    wire.recv(out_half(other, 1 - core), share_o + 1, net.sibling())
+    grad_t = lax.dot_general(
+        out_full[...], cot_ref[...], (((1,), (1,)), ((), ())), preferred_element_type=F32
+    ).astype(BF16)
+    spread_heads(grad_t, dot_, don)
     for g in range(4):
         for k in range(4):
             head = 4 * g + k
@@ -609,7 +651,8 @@
             grads = ahead
             if g < 3:
                 ahead = jnp.dot(values, dot_[g + 1], preferred_element_type=F32)
-            p = probs[g, j].astype(F32) * jnp.exp(peaks[g, j] - peak[g])
+            e = jnp.concatenate([probs[4 * g + j // 2, lax.rem(j, 2) * 2 + c] for c in (0, 1)], axis=1)
+            p = e.astype(F32) * jnp.exp(peaks[g, j] - peak[g])
             ds = (p * (grads - dots[g])).astype(BF16)
             p = p.astype(BF16)
             dqt[g] += jnp.dot(keys_t[g * 64 : g * 64 + 64], ds, preferred_element_type=F32)
@@ -717,8 +760,6 @@
         cols = slice(c * 512, c * 512 + 512)
         block_ref[:, cols] = jnp.dot(attended, out_full[:, cols], preferred_element_type=F32).astype(BF16)
     late2(scat_near)()
-    cos, sin = cos_ref[...], sin_ref[...]
-
     def turn_back(rows_t):
         a, b = rows_t[0:32], rows_t[32:64]
         return jnp.concatenate([a * cos + b * sin, b * cos - a * sin], axis=0)
@@ -741,20 +782,22 @@
     wire.drain()
 
 
-def attend(queries, kv, cotangent, out_full, cos_t, sin_t):
-    keys = 6 * AG_KEYS + 5
+def attend(inputs, qkv_weight, out_weight, cotangent, cos_t, sin_t):
+    keys = 10 * AG_KEYS + 11
     return pl.pallas_call(
         attend_kernel,
         out_shape=(
             jax.ShapeDtypeStruct((128, 1536), BF16),
             jax.ShapeDtypeStruct((128, 2048), BF16),
             jax.ShapeDtypeStruct((2, 4, 32, 256), F32),
+            jax.ShapeDtypeStruct((2048, 1536), BF16),
         ),
-        in_specs=[pl.BlockSpec(memory_space=pltpu.VMEM)] * 3
-        + [pl.BlockSpec(memory_space=pl.ANY)]
-        + [pl.BlockSpec(memory_space=pltpu.VMEM)] * 2,
-        out_specs=[pl.BlockSpec(memory_space=pltpu.VMEM)] * 3,
+        in_specs=[pl.BlockSpec(memory_space=pltpu.VMEM)] * 6,
+        out_specs=[pl.BlockSpec(memory_space=pltpu.VMEM)] * 3 + [pl.BlockSpec(memory_space=pl.ANY)],
         scratch_shapes=[
+            pltpu.VMEM((6, 64, 256), BF16),
+            pltpu.VMEM((128, 1536), F32),
+            pltpu.VMEM((128, 512), BF16),
             pltpu.VMEM((4096, 512), BF16),
             pltpu.VMEM((1024, 2048), BF16),
             pltpu.VMEM((128, 512), F32),
@@ -763,7 +806,7 @@
             pltpu.VMEM((2048, 256), BF16),
             pltpu.VMEM((4, 256, 512), BF16),
             pltpu.VMEM((2048, 256), BF16),
-            pltpu.VMEM((4, 8, BLOCK, 512), BF16),
+            pltpu.VMEM((16, 4, BLOCK, 256), BF16),
             pltpu.VMEM((4, 8, 1, 512), F32),
             pltpu.VMEM((4, 1, 512), F32),
             pltpu.VMEM((4, 1, 512), F32),
@@ -778,17 +821,17 @@
             pltpu.VMEM((2, 64, 512), BF16),
             pltpu.SemaphoreType.DMA((keys,)),
             pltpu.SemaphoreType.DMA((keys,)),
-            pltpu.SemaphoreType.DMA,
+            pltpu.SemaphoreType.DMA((24,)),
             *scatter_scratch(64, 512),
             *scatter_scratch(64, 512),
             *scatter_scratch(32, 512),
             *scatter_scratch(32, 512),
         ],
         compiler_params=pltpu.CompilerParams(
-            collective_id=1, has_side_effects=True, vmem_limit_bytes=VMEM_BYTES
+            collective_id=0, has_side_effects=True, vmem_limit_bytes=VMEM_BYTES
         ),
         name="attend",
-    )(queries, kv, cotangent, out_full, cos_t, sin_t)
+    )(inputs, qkv_weight, out_weight, cotangent, cos_t, sin_t)
 
 
 def weight_grad_kernel(
@@ -1038,26 +1081,12 @@
 
 
 def body(tokens, qkv_weight, out_weight, cotangent):
-    inner_width = HEADS * HEAD_DIM
-    kv_width = KV_HEADS * HEAD_DIM
-    logit_scale = HEAD_DIM ** (-0.5)
     inputs = tokens[0]
-    grad_output = cotangent[0]
     tok_count = inputs.shape[0]
-    qkv_full, out_full = gather_weights(qkv_weight, out_weight)
     positions = lax.axis_index("shard") * tok_count + jnp.arange(tok_count, dtype=jnp.int32)
     cosine, sine = tables(positions, HEAD_DIM)
-    projected = jnp.dot(inputs, qkv_full, preferred_element_type=F32)
-    queries = rotate(projected[:, :inner_width], cosine, sine, HEADS).astype(BF16)
-    key_rows = rotate(projected[:, inner_width : inner_width + kv_width], cosine, sine, KV_HEADS).astype(BF16)
-    value_rows = projected[:, inner_width + kv_width :].astype(BF16)
-    grad_proj, block_output, parts_o = attend(
-        queries * BF16(logit_scale),
-        jnp.concatenate([key_rows, value_rows], axis=1),
-        grad_output,
-        out_full,
-        cosine.T,
-        sine.T,
+    grad_proj, block_output, parts_o, qkv_full = attend(
+        inputs, qkv_weight, out_weight, cotangent[0], cosine.T, sine.T
     )
     norm_factor = 1.0 / math.sqrt(lax.axis_size("rep") * lax.axis_size("shard") * tok_count)
     tokens_grad, qkv_grad, out_grad = weight_grads(inputs, grad_proj, qkv_full, parts_o, norm_factor)

time: 202 us -> 189 us (0.936)
  Pallas kernels: 194 us -> 187 us
  matrix products: 3.96 us -> 0 us
    pallas_call x1 -> x0, Pallas kernels: 52.3 us -> none  [gather_weights(): pl.pallas_call(weight_gather_kernel, out_shape=(jax.ShapeDtypeStruct((204...]
    pallas_call x1, Pallas kernels: 75.3 us -> 126 us  [attend(): pl.pallas_call(attend_kernel, out_shape=(jax.ShapeDtypeStruct((128, 1536)...]
    pallas_call x1, Pallas kernels: 64.2 us -> 58.3 us  [weight_grads(): pl.pallas_call(functools.partial(weight_grad_kernel, scale), out_shape=(j...]
    dot_general x1 -> x0, matrix products: 3.96 us -> none  [body(): projected = jnp.dot(inputs, qkv_full, preferred_element_type=F32)]
where the time goes in v5:
time: 189 us
  Pallas kernels  187 us (99%)
    pallas_call x1, Pallas kernels, attend(): pl.pallas_call(attend_kernel, out_shape=(jax.ShapeDtypeStruct((128, 1536)...  126 us
    pallas_call x1, Pallas kernels, weight_grads(): pl.pallas_call(functools.partial(weight_grad_kernel, scale), out_shape=(j...  58.3 us

profile of v5, /device:TPU:1, one launch (start us, length us, event | category | flops | bytes accessed | tf_op | source)
XLA Modules:
  0.0 188.5 jit_solution(4288592984978187735)
XLA Ops:
  0.7 0.8 multiply_sine_fusion
  1.4 126.2 %attend.1 = (bf16[128,1536]{1,0:T(8,128)(2,1)}, bf16[128,2048]{1,0:T(8,128)(2,1)}, f32[2,4,32,256]{3,2,1,0:T(8,128)}, bf16[2048,1536]{1,0:T(8,128)(2,1)}) custom-call(bf16[128,2048]{1,0:T(8,128)(2,1)} %bitcast.4, bf16[64,1536]{1,0:T(8,128)(2,1)} %qkv_in.1, bf16[32,2048]{1,0:T(8,128)(2,1)} %out_in.1, bf16[128,2048]{1,0:T(8,128)(2,1)} %bitcast.6, ...), custom_call_target="tpu_custom_call" | custom-call | tf_op jit(solution)/shard_map/attend/pallas_call | solution.py:787
  127.6 58.3 %weight_grads.1 = (bf16[128,2048]{1,0:T(8,128)(2,1)}, f32[64,1536]{1,0:T(8,128)}, f32[32,2048]{1,0:T(8,128)}) custom-call(bf16[128,2048]{1,0:T(8,128)(2,1)} %bitcast.5, bf16[128,1536]{1,0:T(8,128)(2,1)} %get-tuple-element.16.gp_ref, bf16[2048,1536]{1,0:T(8,128)(2,1)} %get-tuple-element.17.w_ref, f32[2,4,32,256]{3,2,1,0:T(8,128)} %get-tuple-element.18.parts_o), custom_call_target="tpu_custom_call" | custom-call | tf_op jit(solution)/shard_map/weight_grads/pallas_call | solution.py:1006
  185.9 2.6 %finish.1 = (bf16[128,2048]{1,0:T(8,128)(2,1)}, bf16[128,2048]{1,0:T(8,128)(2,1)}, f32[64,1536]{1,0:T(8,128)}, f32[32,2048]{1,0:T(8,128)}) custom-call(bf16[128,2048]{1,0:T(8,128)(2,1)} %get-tuple-element.15.refs_0_, bf16[128,2048]{1,0:T(8,128)(2,1)} %get-tuple-element.19.refs_1_, f32[64,1536]{1,0:T(8,128)} %get-tuple-element.20.refs_2_, ...), custom_call_target="tpu_custom_call" | custom-call | tf_op jit(solution)/shard_map/finish/pallas_call | solution.py:1048
  (2 shorter events, 0.0 us)

commit v6 on v5

--- a/solution.py
+++ b/solution.py
@@ -701,27 +701,31 @@
 
         def plan3():
             scat.a(0, 0)
+            scat.c(1, 2)
             for d in SIDES:
                 scat.b(0, -1, d)
-            scat.c(1, 2)
             scat.c(0, 1)
 
         return [[plan0], [plan1], [plan2], [plan3]]
 
     def late1(scat):
         def run():
+            scat.c(1, 1)
+            scat.c(1, -1)
             for d in SIDES:
                 scat.b(0, 0, d)
-            for da in (1, -1, 0):
-                scat.c(1, da)
+            for d in SIDES:
+                scat.d(1, d)
             scat.c(0, -1)
+            for d in SIDES:
+                scat.d(0, d)
 
         return run
 
     def late2(scat):
         def run():
+            scat.c(1, 0)
             scat.c(0, 0)
-            scat.all_d()
 
         return run
 
@@ -759,7 +763,6 @@
     for c in range(4):
         cols = slice(c * 512, c * 512 + 512)
         block_ref[:, cols] = jnp.dot(attended, out_full[:, cols], preferred_element_type=F32).astype(BF16)
-    late2(scat_near)()
     def turn_back(rows_t):
         a, b = rows_t[0:32], rows_t[32:64]
         return jnp.concatenate([a * cos + b * sin, b * cos - a * sin], axis=0)
@@ -770,6 +773,7 @@
             pair = [turn_back(dqt[g, :, c * 128 : c * 128 + 128] * 0.125) for c in (k, k + 1)]
             gp_ref[:, head * 64 : head * 64 + 128] = jnp.concatenate(pair, axis=0).T.astype(BF16)
     scat_o[1].all_e()
+    late2(scat_near)()
     scat_near.all_e()
     for h in (0, 1):
         wire.recv(far_in.at[h], zback + h, net.partner())

time: 189 us -> 187 us (0.989)
  Pallas kernels: 187 us -> 185 us
    pallas_call x1, Pallas kernels: 126 us -> 124 us  [attend(): pl.pallas_call(attend_kernel, out_shape=(jax.ShapeDtypeStruct((128, 1536)...]
where the time goes in v6:
time: 187 us
  Pallas kernels  185 us (99%)
    pallas_call x1, Pallas kernels, attend(): pl.pallas_call(attend_kernel, out_shape=(jax.ShapeDtypeStruct((128, 1536)...  124 us
    pallas_call x1, Pallas kernels, weight_grads(): pl.pallas_call(functools.partial(weight_grad_kernel, scale), out_shape=(j...  58.8 us

profile of v6, /device:TPU:1, one launch (start us, length us, event | category | flops | bytes accessed | tf_op | source)
XLA Modules:
  0.0 186.6 jit_solution(7977539559691658451)
XLA Ops:
  0.7 0.8 multiply_sine_fusion
  1.4 123.8 %attend.1 = (bf16[128,1536]{1,0:T(8,128)(2,1)}, bf16[128,2048]{1,0:T(8,128)(2,1)}, f32[2,4,32,256]{3,2,1,0:T(8,128)}, bf16[2048,1536]{1,0:T(8,128)(2,1)}) custom-call(bf16[128,2048]{1,0:T(8,128)(2,1)} %bitcast.4, bf16[64,1536]{1,0:T(8,128)(2,1)} %qkv_in.1, bf16[32,2048]{1,0:T(8,128)(2,1)} %out_in.1, bf16[128,2048]{1,0:T(8,128)(2,1)} %bitcast.6, ...), custom_call_target="tpu_custom_call" | custom-call | tf_op jit(solution)/shard_map/attend/pallas_call | solution.py:791
  125.2 58.8 %weight_grads.1 = (bf16[128,2048]{1,0:T(8,128)(2,1)}, f32[64,1536]{1,0:T(8,128)}, f32[32,2048]{1,0:T(8,128)}) custom-call(bf16[128,2048]{1,0:T(8,128)(2,1)} %bitcast.5, bf16[128,1536]{1,0:T(8,128)(2,1)} %get-tuple-element.16.gp_ref, bf16[2048,1536]{1,0:T(8,128)(2,1)} %get-tuple-element.17.w_ref, f32[2,4,32,256]{3,2,1,0:T(8,128)} %get-tuple-element.18.parts_o), custom_call_target="tpu_custom_call" | custom-call | tf_op jit(solution)/shard_map/weight_grads/pallas_call | solution.py:1010
  184.0 2.6 %finish.1 = (bf16[128,2048]{1,0:T(8,128)(2,1)}, bf16[128,2048]{1,0:T(8,128)(2,1)}, f32[64,1536]{1,0:T(8,128)}, f32[32,2048]{1,0:T(8,128)}) custom-call(bf16[128,2048]{1,0:T(8,128)(2,1)} %get-tuple-element.15.refs_0_, bf16[128,2048]{1,0:T(8,128)(2,1)} %get-tuple-element.19.refs_1_, f32[64,1536]{1,0:T(8,128)} %get-tuple-element.20.refs_2_, ...), custom_call_target="tpu_custom_call" | custom-call | tf_op jit(solution)/shard_map/finish/pallas_call | solution.py:1052
  (2 shorter events, 0.0 us)

commit v7 on v6

--- a/solution.py
+++ b/solution.py
@@ -946,12 +946,20 @@
     runs[0].all_b()
     runs[1].all_b()
     tokens_grad(1)
-    runs[0].all_c()
-    runs[1].all_c()
+    for run in runs:
+        run.c(0, 2)
+        run.c(1, 2)
+    for run in runs:
+        for da in (1, -1):
+            run.c(0, da)
+            run.c(1, da)
     tokens_grad(2)
     runs[0].all_d()
     runs[1].all_d()
     tokens_grad(3)
+    for run in runs:
+        run.c(0, 0)
+        run.c(1, 0)
     runs[0].all_e()
     runs[1].all_e()
 

time: 187 us -> 186 us (level)
  no operation moved by 1% of the time
where the time goes in v7:
time: 186 us
  Pallas kernels  185 us (99%)
    pallas_call x1, Pallas kernels, attend(): pl.pallas_call(attend_kernel, out_shape=(jax.ShapeDtypeStruct((128, 1536)...  124 us
    pallas_call x1, Pallas kernels, weight_grads(): pl.pallas_call(functools.partial(weight_grad_kernel, scale), out_shape=(j...  58.4 us

profile of v7, /device:TPU:1, one launch (start us, length us, event | category | flops | bytes accessed | tf_op | source)
XLA Modules:
  0.0 186.2 jit_solution(12479962233789632299)
XLA Ops:
  0.7 0.8 multiply_sine_fusion
  1.4 123.8 %attend.1 = (bf16[128,1536]{1,0:T(8,128)(2,1)}, bf16[128,2048]{1,0:T(8,128)(2,1)}, f32[2,4,32,256]{3,2,1,0:T(8,128)}, bf16[2048,1536]{1,0:T(8,128)(2,1)}) custom-call(bf16[128,2048]{1,0:T(8,128)(2,1)} %bitcast.4, bf16[64,1536]{1,0:T(8,128)(2,1)} %qkv_in.1, bf16[32,2048]{1,0:T(8,128)(2,1)} %out_in.1, bf16[128,2048]{1,0:T(8,128)(2,1)} %bitcast.6, ...), custom_call_target="tpu_custom_call" | custom-call | tf_op jit(solution)/shard_map/attend/pallas_call | solution.py:791
  125.2 58.4 %weight_grads.1 = (bf16[128,2048]{1,0:T(8,128)(2,1)}, f32[64,1536]{1,0:T(8,128)}, f32[32,2048]{1,0:T(8,128)}) custom-call(bf16[128,2048]{1,0:T(8,128)(2,1)} %bitcast.5, bf16[128,1536]{1,0:T(8,128)(2,1)} %get-tuple-element.16.gp_ref, bf16[2048,1536]{1,0:T(8,128)(2,1)} %get-tuple-element.17.w_ref, f32[2,4,32,256]{3,2,1,0:T(8,128)} %get-tuple-element.18.parts_o), custom_call_target="tpu_custom_call" | custom-call | tf_op jit(solution)/shard_map/weight_grads/pallas_call | solution.py:1018
  183.6 2.6 %finish.1 = (bf16[128,2048]{1,0:T(8,128)(2,1)}, bf16[128,2048]{1,0:T(8,128)(2,1)}, f32[64,1536]{1,0:T(8,128)}, f32[32,2048]{1,0:T(8,128)}) custom-call(bf16[128,2048]{1,0:T(8,128)(2,1)} %get-tuple-element.15.refs_0_, bf16[128,2048]{1,0:T(8,128)(2,1)} %get-tuple-element.19.refs_1_, f32[64,1536]{1,0:T(8,128)} %get-tuple-element.20.refs_2_, ...), custom_call_target="tpu_custom_call" | custom-call | tf_op jit(solution)/shard_map/finish/pallas_call | solution.py:1060
  (2 shorter events, 0.0 us)
